TPU v7x, 512 devices: a whole 4x8x8 slice. The times are simulated.
512 devices in a mesh: row: 16 (over z_lo, x), col: 32 (over z_hi, y, core).
Axes of the slice: x: 4, y: 8, z: 8 (z_hi: 2, z_lo: 4; z = z_hi * 4 + z_lo), core: 2. Of those that a mesh axis runs over, the one named last changes fastest.
Arguments:
- ppmi_tiles: bfloat16 [1, 16, 512, 256, 256], P(None, 'row', 'col')
- tile_map: int32 [1, 16, 32, 16], P(None, 'row', 'col'), may hold values from 0 to 15, each once within a row
- sketch: bfloat16 [131072, 128], P(('col', 'row')), may hold values from -6 to 6
Outputs:
- q_basis: float32 [131072, 128], P(('col', 'row'))
Inputs may be any that keep to these rules, and one draw needn't show every extreme that they name: For every k, r, c the entries tile_map[k, r, c, :] are each of 0 to 15 once.
All inputs are finite; a program needn't handle non-finite values.
Results may differ from a plain program's by a relative error of at most 0.0065.
Values may be sent and summed in bfloat16 or wider, within the bound.
No kernel may reach another device: no remote copies, remote signals or barrier semaphores. Data moves between devices by JAX's collectives and lax.ppermute only.
A program may use at most 64 MiB of HBM per device.

v0:
```python
import jax
import jax.numpy as jnp
from jax import lax
from jax.sharding import PartitionSpec as P


def broadcast(value, axis, source):
    kept = jnp.where(lax.axis_index(axis) == source, value, 0).astype(value.dtype)
    return lax.psum(kept, axis)


def one_pass(tile_set, slot_cols, correction, basis_in):
    row_size = lax.axis_size("row")
    col_id = lax.axis_index("col")
    row_id = lax.axis_index("row")
    band_count = tile_set.shape[0]
    tile_rows = tile_set.shape[2]
    width = basis_in.shape[1]
    band_ids = row_id + row_size * jnp.arange(band_count, dtype=jnp.int32)
    columns = row_size * col_id + slot_cols
    keep_mask = (columns >= band_ids[:, None]).astype(jnp.bfloat16)
    gathered = lax.all_gather(basis_in, "row", axis=0, tiled=True)
    blocks = gathered.reshape(row_size, tile_rows, width)
    by_slot = jnp.take(blocks, slot_cols, axis=0)
    masked = by_slot * keep_mask[:, :, None, None]
    row_part = jnp.einsum("ktab,ktbn->kan", tile_set, masked, preferred_element_type=jnp.float32)
    received = [broadcast(basis_in, "col", 0)]
    band_blocks = jnp.stack(received)
    row_part = row_part + jnp.einsum(
        "kab,kbn->kan", correction, band_blocks, preferred_element_type=jnp.float32
    )
    band_sum = lax.psum(row_part, "col")
    own_band = band_sum[jnp.minimum(col_id, band_count - 1)] * (col_id < band_count).astype(
        jnp.float32
    )
    strict = (columns > band_ids[:, None]).astype(jnp.float32)
    products = jnp.einsum(
        "ktab,kan->ktbn", tile_set, band_blocks, preferred_element_type=jnp.float32
    )
    products = products * strict[:, :, None, None]
    select = (slot_cols[:, :, None] == jnp.arange(row_size, dtype=jnp.int32)[None, None, :]).astype(
        jnp.float32
    )
    placed = jnp.einsum("kts,ktbn->sbn", select, products)
    col_sum = lax.psum_scatter(
        placed.reshape(row_size * tile_rows, width), "row", scatter_dimension=0, tiled=True
    )
    stacked = col_sum + own_band
    local_gram = jnp.dot(stacked.T, stacked, precision=lax.Precision.HIGHEST)
    gram_matrix = lax.psum(local_gram, ("row", "col"))
    factor = jnp.linalg.cholesky(gram_matrix)
    return jax.scipy.linalg.solve_triangular(factor, stacked.T, lower=True).T


def local(ppmi_tiles, tile_map, sketch):
    row_id = lax.axis_index("row")
    col_id = lax.axis_index("col")
    row_size = lax.axis_size("row")
    tile_set = ppmi_tiles[:, 0]
    slot_cols = tile_map[:, 0, 0]
    band_count = tile_set.shape[0]
    band_ids = row_id + row_size * jnp.arange(band_count, dtype=jnp.int32)
    is_diag = row_size * col_id + slot_cols == band_ids[:, None]
    diag_slot = jnp.sum(
        jnp.arange(row_size, dtype=jnp.int32)[None, :] * is_diag.astype(jnp.int32), axis=1
    )
    present = jnp.any(is_diag, axis=1).astype(jnp.bfloat16)
    diag_tiles = tile_set[jnp.arange(band_count), diag_slot]
    correction = jnp.swapaxes(jnp.triu(diag_tiles, 1), 1, 2) - jnp.tril(diag_tiles, -1)
    correction = correction * present[:, None, None]
    basis = one_pass(tile_set, slot_cols, correction, sketch).astype(jnp.bfloat16)
    return one_pass(tile_set, slot_cols, correction, basis)


def solution(mesh):
    in_specs = (
        P(None, "row", "col", None, None),
        P(None, "row", "col", None),
        P(("col", "row"), None),
    )
    out_specs = P(("col", "row"), None)
    return jax.shard_map(local, mesh=mesh, in_specs=in_specs, out_specs=out_specs, check_vma=False)
```

profile of v0, /device:TPU:1, one launch (start us, length us, event | category | flops | bytes accessed | tf_op | source)
XLA Modules:
  0.0 1842.3 jit_solution(1399048602244538028)
XLA Ops:
  8.1 0.9 copy.15
  10.5 1.3 fusion.48
  11.8 1.3 compare_reduce_fusion.2
  13.0 3.3 copy.31
  19.9 71.0 %all-gather.3.cloned.1.call-done = bf16[4096,128]{1,0:T(8,128)(2,1)} async-done(((bf16[256,128]{1,0:T(8,128)(2,1)}), bf16[4096,128]{1,0:T(8,128)(2,1)}) %all-gather.3.cloned.1.call-update) | async-done | bytes 1048592 | tf_op jit(solution)/shard_map/all_gather | solution.py:22
  90.9 2.0 gather_fusion
  92.9 3.4 convolution_bitcast_fusion.2
  96.3 226.8 %all-reduce.7.cloned.1.call-done = bf16[256,128]{0,1:T(8,128)(2,1)} async-done(((bf16[256,128]{0,1:T(8,128)(2,1)}), bf16[256,128]{0,1:T(8,128)(2,1)}) %all-reduce.7.cloned.1.call-update) | async-done | bytes 65552 | tf_op jit(solution)/shard_map/psum | solution.py:9
  323.1 1.9 fusion.6
  325.1 3.4 fusion
  328.5 3.6 copy.16
  332.1 2.9 copy.17
  335.1 304.4 %all-reduce.9.cloned.1.call-done = f32[1,256,128]{1,2,0:T(8,128)} async-done(((f32[1,256,128]{1,2,0:T(8,128)}), f32[1,256,128]{1,2,0:T(8,128)}) %all-reduce.9.cloned.1.call-update) | async-done | bytes 131088 | tf_op jit(solution)/shard_map/psum | solution.py:32
  639.4 2.0 fusion.40
  641.5 258.3 %all-reduce.11.cloned.1.call-done = f32[128,128]{0,1:T(8,128)} async-done(((f32[128,128]{0,1:T(8,128)}), f32[128,128]{0,1:T(8,128)}) %all-reduce.11.cloned.1.call-update) | async-done | bytes 65552 | tf_op jit(solution)/shard_map/psum | solution.py:50
  901.7 11.7 cholesky.44
  914.7 9.8 custom-call.6
  924.5 1.9 broadcast_select_fusion
  927.4 297.5 %all-reduce.13.cloned.1.call-done = bf16[256,128]{0,1:T(8,128)(2,1)} async-done(((bf16[256,128]{0,1:T(8,128)(2,1)}), bf16[256,128]{0,1:T(8,128)(2,1)}) %all-reduce.13.cloned.1.call-update) | async-done | bytes 65552 | tf_op jit(solution)/shard_map/psum | solution.py:9
  1224.9 1.5 multiply_bitcast_fusion
  1226.5 1.3 copy.35
  1227.8 1.6 copy.40
  1230.1 2.7 convolution_bitcast_fusion.1
  1232.9 0.9 fusion.5
  1234.3 3.0 copy.41
  1237.4 309.8 %all-reduce.15.cloned.1.call-done = f32[1,256,128]{1,2,0:T(8,128)} async-done(((f32[1,256,128]{1,2,0:T(8,128)}), f32[1,256,128]{1,2,0:T(8,128)}) %all-reduce.15.cloned.1.call-update) | async-done | bytes 131088 | tf_op jit(solution)/shard_map/psum | solution.py:32
  1547.2 2.0 fusion.41
  1549.3 259.2 %all-reduce.17.cloned.1.call-done = f32[128,128]{0,1:T(8,128)} async-done(((f32[128,128]{0,1:T(8,128)}), f32[128,128]{0,1:T(8,128)}) %all-reduce.17.cloned.1.call-update) | async-done | bytes 65552 | tf_op jit(solution)/shard_map/psum | solution.py:50
  1808.5 0.9 copy.29
  1810.3 11.7 cholesky.55
  1823.3 9.8 custom-call.7
  1833.2 1.3 convolution_bitcast_fusion
  (45 shorter events, 11.7 us)
Async XLA Ops:
  7.4 83.6 %all-gather.3.cloned.1.call-start = ((), (), s32[]{:S(2)}) async-start(), calls=%async_computation.4 | async-start | bytes 1114112 | tf_op jit(solution)/shard_map/all_gather | solution.py:22
  8.1 315.0 %all-reduce.7.cloned.1.call-start = ((), (), s32[]{:S(2)}) async-start(), calls=%async_computation.2 | async-start | bytes 131072 | tf_op jit(solution)/shard_map/psum | solution.py:9
  9.7 629.7 %all-reduce.9.cloned.1.call-start = ((), (), s32[]{:S(2)}) async-start(), calls=%async_computation.5 | async-start | bytes 262144 | tf_op jit(solution)/shard_map/psum | solution.py:32
  92.9 232.1 %copy-start.1 = (s32[1,1,1,16]{3,2,1,0:T(1,128)S(1)}, s32[1,1,1,16]{3,2,1,0:T(1,128)}, u32[]{:S(2)}) copy-start(s32[1,1,1,16]{3,2,1,0:T(1,128)} %param.9) | copy-start | bytes 196
  325.0 314.4 %reduce-scatter.3.cloned.1.call-start = ((), (), s32[]{:S(2)}) async-start(), calls=%async_computation.3 | async-start | bytes 2228224 | tf_op jit(solution)/shard_map/reduce_scatter | solution.py:45
  335.0 564.9 %all-reduce.11.cloned.1.call-start = ((), (), s32[]{:S(2)}) async-start(), calls=%async_computation.6 | async-start | bytes 131072 | tf_op jit(solution)/shard_map/psum | solution.py:50
  641.5 583.4 %all-reduce.13.cloned.1.call-start = ((), (), s32[]{:S(2)}) async-start(), calls=%async_computation.7 | async-start | bytes 131072 | tf_op jit(solution)/shard_map/psum | solution.py:9
  926.5 301.3 %all-gather.5.cloned.1.call-start = ((), (), s32[]{:S(2)}) async-start(), calls=%async_computation.9 | async-start | bytes 1114112 | tf_op jit(solution)/shard_map/all_gather | solution.py:22
  927.2 620.0 %all-reduce.15.cloned.1.call-start = ((), (), s32[]{:S(2)}) async-start(), calls=%async_computation.10 | async-start | bytes 262144 | tf_op jit(solution)/shard_map/psum | solution.py:32
  1230.1 2.8 copy-start
  1233.9 313.4 %reduce-scatter.5.cloned.1.call-start = ((), (), s32[]{:S(2)}) async-start(), calls=%async_computation.8 | async-start | bytes 2228224 | tf_op jit(solution)/shard_map/reduce_scatter | solution.py:45
  1237.3 571.2 %all-reduce.17.cloned.1.call-start = ((), (), s32[]{:S(2)}) async-start(), calls=%async_computation.11 | async-start | bytes 131072 | tf_op jit(solution)/shard_map/psum | solution.py:50
Sparse Core Ops, SparseCore 0:
  10.5 80.4 all-gather.2
  335.1 77.9 reduce-scatter.2
  929.3 55.8 all-gather.4
  1237.5 77.9 reduce-scatter.4
Sparse Core Ops, SparseCore 1:
  11.5 311.6 all-reduce.6
  326.2 313.2 all-reduce.8
  644.3 255.5 all-reduce.10
  926.6 298.3 all-reduce.12
  1233.9 313.2 all-reduce.14
  1553.0 255.4 all-reduce.16
where the time goes:
time: 1840 us
  waiting for transfers between devices  1730 us (94%)
  other arithmetic  51.3 us (3%)
  local copies, waits for them, and re-layouts  23 us (1%)
  matrix products  21.5 us (1%)
    psum x2, waiting for transfers between devices, one_pass(): band_sum = lax.psum(row_part, 'col')  614 us
    psum x2, waiting for transfers between devices, broadcast(): return lax.psum(kept, axis)  524 us
    psum x2, waiting for transfers between devices, one_pass(): gram_matrix = lax.psum(local_gram, ('row', 'col'))  518 us
    all_gather x2, waiting for transfers between devices, one_pass(): gathered = lax.all_gather(basis_in, 'row', axis=0, tiled=True)  71 us
  transfers between devices with their start and end apart: 10, of which 7 were waited for; matrix products, arithmetic and copies ran while one was open for 2% of the time, Pallas kernels for 0%

commit v1 on v0

v1 whole, which is shorter than its diff:
```python
import jax
import jax.numpy as jnp
from jax import lax
from jax.sharding import Mesh, PartitionSpec as P

ROW = ("zl", "x")
COL = ("zh", "y", "core")
HIGHEST = lax.Precision.HIGHEST


def swap(value, axes):
    return lax.all_to_all(value, axes, 0, 0, tiled=True)


def gather_row(block):
    return swap(jnp.broadcast_to(block[None], (16,) + block.shape), ROW)


def from_first_column(block):
    with jax.named_scope("sketch_to_columns"):
        other = lax.ppermute(block, "zh", [(0, 1)])
        block = jnp.where(lax.axis_index("zh") == 0, block, other)
        block = swap(jnp.broadcast_to(block[None], (8,) + block.shape), "y")[0]
        other = lax.ppermute(block, "core", [(0, 1)])
        return jnp.where(lax.axis_index("core") == 0, block, other)


def multiply(tiles, columns, band_id, near, band_block):
    keep = (columns >= band_id).astype(jnp.bfloat16)
    strict = (columns > band_id).astype(jnp.float32)
    row_part = jnp.einsum(
        "tab,tbn->an", tiles, near * keep[:, None, None], preferred_element_type=jnp.float32
    )
    products = jnp.einsum("tab,an->tbn", tiles, band_block, preferred_element_type=jnp.float32)
    return row_part, products * strict[:, None, None]


def one_pass(tiles, slots, inverse, correction, own, band_block):
    row_id, col_id = lax.axis_index(ROW), lax.axis_index(COL)
    columns = 16 * col_id + slots
    blocks = gather_row(own)
    near = jnp.take(blocks, slots, axis=0)
    row_part, products = multiply(tiles, columns, row_id, near, band_block)
    row_part = row_part + jnp.dot(correction, own, preferred_element_type=jnp.float32)
    placed = jnp.take(products, inverse, axis=0).astype(jnp.bfloat16)
    received = swap(placed, ROW)
    col_sum = jnp.sum(received.astype(jnp.float32), axis=0)
    first_col = col_id == 0
    row_part = row_part + jnp.where(first_col, col_sum, 0.0)
    rest = jnp.where(first_col, 0.0, col_sum)
    band_rows = jnp.sum(swap(row_part.reshape(32, 8, 128), COL), axis=0)
    stacked = jnp.concatenate([rest, band_rows], axis=0)
    gram = jnp.dot(stacked.T, stacked, precision=HIGHEST)
    piece = jnp.sum(swap(gram.reshape(16, 8, 128), ROW), axis=0)
    both = jnp.concatenate([piece, band_rows], axis=0)
    both = swap(jnp.broadcast_to(both[None], (32, 16, 128)), COL)
    piece = jnp.sum(both[:, :8], axis=0)
    band = both[:, 8:].reshape(256, 128)
    gram = gather_row(piece).reshape(128, 128)
    factor = jnp.linalg.cholesky(gram)
    own = jnp.where(first_col, band, rest)
    return factor, own, band


def local(ppmi_tiles, tile_map, sketch):
    row_id, col_id = lax.axis_index(ROW), lax.axis_index(COL)
    tiles = ppmi_tiles[0, 0]
    slots = tile_map[0, 0, 0]
    inverse = jnp.argmax(slots[None, :] == jnp.arange(16)[:, None], axis=1)
    is_diag = 16 * col_id + slots == row_id
    diag = tiles[jnp.argmax(is_diag)]
    correction = jnp.swapaxes(jnp.triu(diag, 1), 0, 1) - jnp.tril(diag, -1)
    correction = correction * jnp.any(is_diag).astype(jnp.bfloat16)
    band_block = from_first_column(sketch)
    factor, own, band = one_pass(tiles, slots, inverse, correction, sketch, band_block)
    wide = jnp.concatenate([own, band], axis=0)
    basis = jax.scipy.linalg.solve_triangular(factor, wide.T, lower=True).T.astype(jnp.bfloat16)
    factor, own, _ = one_pass(tiles, slots, inverse, correction, basis[:256], basis[256:])
    return jax.scipy.linalg.solve_triangular(factor, own.T, lower=True).T


def solution(mesh):
    fine = Mesh(mesh.devices.reshape(4, 4, 2, 8, 2), ROW + COL)
    in_specs = (
        P(None, ROW, COL, None, None),
        P(None, ROW, COL, None),
        P(COL + ROW, None),
    )
    return jax.shard_map(
        local, mesh=fine, in_specs=in_specs, out_specs=P(COL + ROW, None), check_vma=False
    )
```

time: 1840 us -> 349 us (0.19)
  waiting for transfers between devices: 1730 us -> 118 us
  starting transfers between devices: 0.57 us -> 74 us
  blocking collectives: 0 us -> 69.2 us
    psum x6 -> x0, waiting for transfers between devices: 1660 us -> none  [the longest x2 614 us: one_pass(): band_sum = lax.psum(row_part, 'col')]
    all_to_all x0 -> x9, waiting for transfers between devices: none -> 114 us  [swap(): return lax.all_to_all(value, axes, 0, 0, tiled=True)]
    all_gather x2 -> x0, waiting for transfers between devices: 71 us -> none  [one_pass(): gathered = lax.all_gather(basis_in, 'row', axis=0, tiled=True)]
    all_to_all x0 -> x4, blocking collectives: none -> 69.2 us  [swap(): return lax.all_to_all(value, axes, 0, 0, tiled=True)]
    all_to_all x0 -> x9, starting transfers between devices: none -> 61.1 us  [swap(): return lax.all_to_all(value, axes, 0, 0, tiled=True)]
    another operation x10 -> x12, other arithmetic: 45.7 us -> 47 us  [the longest x6 24.8 us: one_pass(): factor = jnp.linalg.cholesky(gram)]
  transfers between devices with their start and end apart: 10 -> 11, of which waited for: 7 -> 11; matrix products, arithmetic and copies ran while one was open for 2% -> 7% of each run, Pallas kernels for 0% -> 0%
where the time goes in v1:
time: 349 us; the launch traced here: 347 us
  waiting for transfers between devices  118 us (34%)
  starting transfers between devices  74 us (21%)
  blocking collectives  69.2 us (20%)
  other arithmetic  51.9 us (15%)
  local copies, waits for them, and re-layouts  17.8 us (5%)
  matrix products  13.7 us (4%)
    all_to_all x9, waiting for transfers between devices, swap(): return lax.all_to_all(value, axes, 0, 0, tiled=True)  114 us
    all_to_all x4, blocking collectives, swap(): return lax.all_to_all(value, axes, 0, 0, tiled=True)  69.2 us
    all_to_all x9, starting transfers between devices, swap(): return lax.all_to_all(value, axes, 0, 0, tiled=True)  61.1 us
    another operation x6, other arithmetic, one_pass(): factor = jnp.linalg.cholesky(gram)  24.8 us
    ppermute x1, starting transfers between devices, from_first_column(): other = lax.ppermute(block, 'zh', [(0, 1)])  11.6 us
    another operation x2, other arithmetic, local(): jax.scipy.linalg.solve_triangular(factor, wide.T, lower=True)  10.5 us
    another operation x2, other arithmetic, local(): return jax.scipy.linalg.solve_triangular(factor, own.T, lower=True).T  10.5 us
  transfers between devices with their start and end apart: 11, of which 11 were waited for; matrix products, arithmetic and copies ran while one was open for 7% of the time, Pallas kernels for 0%

profile of v1, /device:TPU:1, one launch (start us, length us, event | category | flops | bytes accessed | tf_op | source)
XLA Modules:
  0.0 347.4 jit_solution(13171010489657921386)
XLA Ops:
  0.0 11.6 %collective-permute-start = (bf16[256,128]{1,0:T(8,128)(2,1)}, bf16[256,128]{1,0:T(8,128)(2,1)S(1)}, u32[]{:S(2)}, u32[]{:S(2)}) collective-permute-start(bf16[256,128]{1,0:T(8,128)(2,1)} %param.10), channel_id=1, source_target_pairs={{0,16},{1,17},{2,18},{3,19},{4,20},{5,21},{6,22},{7,23},{8,24},{9,... | collective-permute-start | bytes 196616 | tf_op jit(solution)/shard_map/sketch_to_columns/ppermute | solution.py:21
  15.0 7.0 %all-to-all-start = ((bf16[8,256,128]{1,2,0:T(8,128)(2,1)}), bf16[8,256,128]{1,2,0:T(8,128)(2,1)S(1)}, u32[]{:S(2)}, u32[]{:S(2)}) async-start(bf16[8,256,128]{1,2,0:T(8,128)(2,1)} %broadcast_in_dim.48), calls=%async_computation | async-start | bytes 1048576 | tf_op jit(solution)/shard_map/sketch_to_columns/all_to_all | solution.py:12
  22.0 15.9 %all-to-all-done = bf16[8,256,128]{1,2,0:T(8,128)(2,1)S(1)} async-done(((bf16[8,256,128]{1,2,0:T(8,128)(2,1)}), bf16[8,256,128]{1,2,0:T(8,128)(2,1)S(1)}, u32[]{:S(2)}, u32[]{:S(2)}) %all-to-all-start) | async-done | bytes 524320 | tf_op jit(solution)/shard_map/sketch_to_columns/all_to_all | solution.py:12
  39.9 8.3 %all-to-all-start.2 = ((bf16[16,256,128]{2,1,0:T(8,128)(2,1)}), bf16[16,256,128]{2,1,0:T(8,128)(2,1)}, u32[]{:S(2)}, u32[]{:S(2)}) async-start(bf16[16,256,128]{2,1,0:T(8,128)(2,1)} %broadcast_in_dim.49), calls=%async_computation.2 | async-start | bytes 2097152 | tf_op jit(solution)/shard_map/all_to_all | solution.py:12
  50.8 2.6 collective-permute-done.1
  58.2 12.2 %all-to-all-done.2 = bf16[16,256,128]{2,1,0:T(8,128)(2,1)} async-done(((bf16[16,256,128]{2,1,0:T(8,128)(2,1)}), bf16[16,256,128]{2,1,0:T(8,128)(2,1)}, u32[]{:S(2)}, u32[]{:S(2)}) %all-to-all-start.2) | async-done | bytes 1048608 | tf_op jit(solution)/shard_map/all_to_all | solution.py:12
  70.4 7.8 %all-to-all-start.1 = ((bf16[16,256,128]{1,2,0:T(8,128)(2,1)}), bf16[16,256,128]{1,2,0:T(8,128)(2,1)S(1)}, u32[]{:S(2)}, u32[]{:S(2)}) async-start(bf16[16,256,128]{1,2,0:T(8,128)(2,1)} %select_convert_fusion.1), calls=%async_computation.1 | async-start | bytes 2097152 | tf_op jit(solution)/shard_map/all_to_all | solution.py:12
  82.2 2.9 gather_fusion.1
  85.1 3.0 fusion.12
  88.1 12.2 %all-to-all-done.1 = bf16[16,256,128]{1,2,0:T(8,128)(2,1)S(1)} async-done(((bf16[16,256,128]{1,2,0:T(8,128)(2,1)}), bf16[16,256,128]{1,2,0:T(8,128)(2,1)S(1)}, u32[]{:S(2)}, u32[]{:S(2)}) %all-to-all-start.1) | async-done | bytes 1048608 | tf_op jit(solution)/shard_map/all_to_all | solution.py:12
  102.5 11.5 %all-to-all-start.3 = ((f32[32,8,128]{2,1,0:T(8,128)}), f32[32,8,128]{2,1,0:T(8,128)S(1)}, u32[]{:S(2)}, u32[]{:S(2)}) async-start(f32[32,8,128]{2,1,0:T(8,128)} %bitcast.9), calls=%async_computation.3 | async-start | bytes 262144 | tf_op jit(solution)/shard_map/all_to_all | solution.py:12
  114.0 13.0 %all-to-all-done.3 = f32[32,8,128]{2,1,0:T(8,128)S(1)} async-done(((f32[32,8,128]{2,1,0:T(8,128)}), f32[32,8,128]{2,1,0:T(8,128)S(1)}, u32[]{:S(2)}, u32[]{:S(2)}) %all-to-all-start.3) | async-done | bytes 131104 | tf_op jit(solution)/shard_map/all_to_all | solution.py:12
  127.5 13.0 %all_to_all.65 = f32[16,8,128]{2,1,0:T(8,128)S(1)} all-to-all(f32[16,8,128]{2,1,0:T(8,128)S(1)} %convolution_bitcast_fusion.1), channel_id=1, replica_groups=mesh['zl'=4,'x'=4,'zh'=2,'y'=8,'core'=2] {'zl','x'}, dimensions={0} | all-to-all | bytes 131072 | tf_op jit(solution)/shard_map/all_to_all | solution.py:12
  140.5 21.6 %all_to_all.66 = f32[32,16,128]{2,1,0:T(8,128)S(1)} all-to-all(f32[32,16,128]{2,1,0:T(8,128)S(1)} %broadcast_in_dim.51), channel_id=1, replica_groups=mesh['zl'=4,'x'=4,'zh'=2,'y'=8,'core'=2] {'zh','y','core'}, dimensions={0} | all-to-all | bytes 524288 | tf_op jit(solution)/shard_map/all_to_all | solution.py:12
  162.9 3.7 %all-to-all-start.6 = ((f32[16,8,128]{2,1,0:T(8,128)}), f32[16,8,128]{2,1,0:T(8,128)S(1)}, u32[]{:S(2)}, u32[]{:S(2)}) async-start(f32[16,8,128]{2,1,0:T(8,128)} %broadcast_in_dim.52), calls=%async_computation.6 | async-start | bytes 131072 | tf_op jit(solution)/shard_map/all_to_all | solution.py:12
  166.6 7.0 %all-to-all-done.6 = f32[16,8,128]{2,1,0:T(8,128)S(1)} async-done(((f32[16,8,128]{2,1,0:T(8,128)}), f32[16,8,128]{2,1,0:T(8,128)S(1)}, u32[]{:S(2)}, u32[]{:S(2)}) %all-to-all-start.6) | async-done | bytes 65568 | tf_op jit(solution)/shard_map/all_to_all | solution.py:12
  173.7 11.7 %cholesky.44 = f32[128,128]{1,0:T(8,128)S(1)} custom-call(f32[128,128]{1,0:T(8,128)S(1)} %fusion.49), custom_call_target="Cholesky" | custom-call | tf_op jit(solution)/shard_map/jit(cholesky)/cholesky | solution.py:60
  186.8 9.8 %custom-call.10 = f32[1,128,128]{1,2,0:T(8,128)S(1)} custom-call(f32[1,128,128]{2,1,0:T(8,128)S(1)} %fusion.44), custom_call_target="InvertDiagBlocksLowerTriangular" | custom-call | tf_op jit(solution)/shard_map/jit(_solve_triangular)/triangular_solve | solution.py:77
  198.4 4.3 %all-to-all-start.8 = ((bf16[16,256,128]{2,1,0:T(8,128)(2,1)}), bf16[16,256,128]{2,1,0:T(8,128)(2,1)}, u32[]{:S(2)}, u32[]{:S(2)}) async-start(bf16[16,256,128]{2,1,0:T(8,128)(2,1)} %broadcast_in_dim.53), calls=%async_computation.8 | async-start | bytes 2097152 | tf_op jit(solution)/shard_map/all_to_all | solution.py:12
  207.4 17.3 %all-to-all-done.8 = bf16[16,256,128]{2,1,0:T(8,128)(2,1)} async-done(((bf16[16,256,128]{2,1,0:T(8,128)(2,1)}), bf16[16,256,128]{2,1,0:T(8,128)(2,1)}, u32[]{:S(2)}, u32[]{:S(2)}) %all-to-all-start.8) | async-done | bytes 1048608 | tf_op jit(solution)/shard_map/all_to_all | solution.py:12
  224.8 7.8 %all-to-all-start.7 = ((bf16[16,256,128]{1,2,0:T(8,128)(2,1)}), bf16[16,256,128]{1,2,0:T(8,128)(2,1)S(1)}, u32[]{:S(2)}, u32[]{:S(2)}) async-start(bf16[16,256,128]{1,2,0:T(8,128)(2,1)} %select_convert_fusion), calls=%async_computation.7 | async-start | bytes 2097152 | tf_op jit(solution)/shard_map/all_to_all | solution.py:12
  232.5 2.9 gather_fusion.3
  235.4 3.0 fusion.15
  238.4 16.2 %all-to-all-done.7 = bf16[16,256,128]{1,2,0:T(8,128)(2,1)S(1)} async-done(((bf16[16,256,128]{1,2,0:T(8,128)(2,1)}), bf16[16,256,128]{1,2,0:T(8,128)(2,1)S(1)}, u32[]{:S(2)}, u32[]{:S(2)}) %all-to-all-start.7) | async-done | bytes 1048608 | tf_op jit(solution)/shard_map/all_to_all | solution.py:12
  256.8 7.0 %all-to-all-start.9 = ((f32[32,8,128]{2,1,0:T(8,128)}), f32[32,8,128]{2,1,0:T(8,128)S(1)}, u32[]{:S(2)}, u32[]{:S(2)}) async-start(f32[32,8,128]{2,1,0:T(8,128)} %bitcast.20), calls=%async_computation.9 | async-start | bytes 262144 | tf_op jit(solution)/shard_map/all_to_all | solution.py:12
  263.9 13.0 %all-to-all-done.9 = f32[32,8,128]{2,1,0:T(8,128)S(1)} async-done(((f32[32,8,128]{2,1,0:T(8,128)}), f32[32,8,128]{2,1,0:T(8,128)S(1)}, u32[]{:S(2)}, u32[]{:S(2)}) %all-to-all-start.9) | async-done | bytes 131104 | tf_op jit(solution)/shard_map/all_to_all | solution.py:12
  277.4 13.0 %all_to_all.67 = f32[16,8,128]{2,1,0:T(8,128)S(1)} all-to-all(f32[16,8,128]{2,1,0:T(8,128)S(1)} %convolution_bitcast_fusion), channel_id=1, replica_groups=mesh['zl'=4,'x'=4,'zh'=2,'y'=8,'core'=2] {'zl','x'}, dimensions={0} | all-to-all | bytes 131072 | tf_op jit(solution)/shard_map/all_to_all | solution.py:12
  290.4 21.6 %all_to_all.68 = f32[32,16,128]{2,1,0:T(8,128)S(1)} all-to-all(f32[32,16,128]{2,1,0:T(8,128)S(1)} %broadcast_in_dim.54), channel_id=1, replica_groups=mesh['zl'=4,'x'=4,'zh'=2,'y'=8,'core'=2] {'zh','y','core'}, dimensions={0} | all-to-all | bytes 524288 | tf_op jit(solution)/shard_map/all_to_all | solution.py:12
  312.8 3.7 %all-to-all-start.12 = ((f32[16,8,128]{2,1,0:T(8,128)}), f32[16,8,128]{2,1,0:T(8,128)S(1)}, u32[]{:S(2)}, u32[]{:S(2)}) async-start(f32[16,8,128]{2,1,0:T(8,128)} %broadcast_in_dim.88), calls=%async_computation.12 | async-start | bytes 131072 | tf_op jit(solution)/shard_map/all_to_all | solution.py:12
  316.6 6.9 %all-to-all-done.12 = f32[16,8,128]{2,1,0:T(8,128)S(1)} async-done(((f32[16,8,128]{2,1,0:T(8,128)}), f32[16,8,128]{2,1,0:T(8,128)S(1)}, u32[]{:S(2)}, u32[]{:S(2)}) %all-to-all-start.12) | async-done | bytes 65568 | tf_op jit(solution)/shard_map/all_to_all | solution.py:12
  323.6 11.7 %cholesky.55 = f32[128,128]{1,0:T(8,128)S(1)} custom-call(f32[128,128]{1,0:T(8,128)S(1)} %fusion.47), custom_call_target="Cholesky" | custom-call | tf_op jit(solution)/shard_map/jit(cholesky)/cholesky | solution.py:60
  336.7 9.8 %custom-call.11 = f32[1,128,128]{1,2,0:T(8,128)S(1)} custom-call(f32[1,128,128]{2,1,0:T(8,128)S(1)} %fusion.45), custom_call_target="InvertDiagBlocksLowerTriangular" | custom-call | tf_op jit(solution)/shard_map/jit(_solve_triangular)/triangular_solve | solution.py:79
  (84 shorter events, 31.5 us)
Async XLA Ops:
  0.0 53.4 %copy-start = (bf16[1,1,16,256,256]{4,3,2,1,0:T(8,128)(2,1)S(1)}, bf16[1,1,16,256,256]{4,3,2,1,0:T(8,128)(2,1)}, u32[]{:S(2)}) copy-start(bf16[1,1,16,256,256]{4,3,2,1,0:T(8,128)(2,1)} %param.8) | copy-start | bytes 6291460
  0.0 13.2 %collective-permute-start = (bf16[256,128]{1,0:T(8,128)(2,1)}, bf16[256,128]{1,0:T(8,128)(2,1)S(1)}, u32[]{:S(2)}, u32[]{:S(2)}) collective-permute-start(bf16[256,128]{1,0:T(8,128)(2,1)} %param.10), channel_id=1, source_target_pairs={{0,16},{1,17},{2,18},{3,19},{4,20},{5,21},{6,22},{7,23},{8,24},{9,... | collective-permute-start | bytes 196616 | tf_op jit(solution)/shard_map/sketch_to_columns/ppermute | solution.py:21
  15.0 33.2 %copy-start.2 = (s32[1,1,1,16]{3,2,1,0:T(1,128)S(1)}, s32[1,1,1,16]{3,2,1,0:T(1,128)}, u32[]{:S(2)}) copy-start(s32[1,1,1,16]{3,2,1,0:T(1,128)} %param.9) | copy-start | bytes 196
  15.0 22.9 %all-to-all-start = ((bf16[8,256,128]{1,2,0:T(8,128)(2,1)}), bf16[8,256,128]{1,2,0:T(8,128)(2,1)S(1)}, u32[]{:S(2)}, u32[]{:S(2)}) async-start(bf16[8,256,128]{1,2,0:T(8,128)(2,1)} %broadcast_in_dim.48), calls=%async_computation | async-start | bytes 1048576 | tf_op jit(solution)/shard_map/sketch_to_columns/all_to_all | solution.py:12
  39.9 30.5 %all-to-all-start.2 = ((bf16[16,256,128]{2,1,0:T(8,128)(2,1)}), bf16[16,256,128]{2,1,0:T(8,128)(2,1)}, u32[]{:S(2)}, u32[]{:S(2)}) async-start(bf16[16,256,128]{2,1,0:T(8,128)(2,1)} %broadcast_in_dim.49), calls=%async_computation.2 | async-start | bytes 2097152 | tf_op jit(solution)/shard_map/all_to_all | solution.py:12
  49.5 35.5 %copy-start.3 = (pred[16]{0:T(512)(128)(4,1)}, pred[16]{0:T(512)(128)(4,1)S(1)}, u32[]{:S(2)}) copy-start(pred[16]{0:T(512)(128)(4,1)S(1)} %get-tuple-element.18) | copy-start | bytes 52
  49.5 35.5 %copy-start.5 = (bf16[16]{0:T(256)(128)(2,1)}, bf16[16]{0:T(256)(128)(2,1)S(1)}, u32[]{:S(2)}) copy-start(bf16[16]{0:T(256)(128)(2,1)S(1)} %get-tuple-element.17) | copy-start | bytes 100
  49.5 3.9 %collective-permute-start.1 = (bf16[256,128]{0,1:T(8,128)(2,1)S(1)}, bf16[256,128]{0,1:T(8,128)(2,1)S(1)}, u32[]{:S(2)}, u32[]{:S(2)}) collective-permute-start(bf16[256,128]{0,1:T(8,128)(2,1)S(1)} %slice_bitcast_fusion.3), channel_id=1, source_target_pairs={{0,1},{2,3},{4,5},{6,7},{8,9},{10,11},{12,13},{14,15},{16,17},{18,... | collective-permute-start | bytes 196616 | tf_op jit(solution)/shard_map/sketch_to_columns/ppermute | solution.py:24
  70.4 29.9 %all-to-all-start.1 = ((bf16[16,256,128]{1,2,0:T(8,128)(2,1)}), bf16[16,256,128]{1,2,0:T(8,128)(2,1)S(1)}, u32[]{:S(2)}, u32[]{:S(2)}) async-start(bf16[16,256,128]{1,2,0:T(8,128)(2,1)} %select_convert_fusion.1), calls=%async_computation.1 | async-start | bytes 2097152 | tf_op jit(solution)/shard_map/all_to_all | solution.py:12
  82.1 18.3 %copy-start.7 = (s32[256]{0:T(256)}, s32[256]{0:T(256)S(1)}, u32[]{:S(2)}) copy-start(s32[256]{0:T(256)S(1)} %iota_add_fusion) | copy-start | bytes 3076
  85.1 15.4 %copy-start.1 = (bf16[256,128]{1,0:T(8,128)(2,1)S(1)}, bf16[256,128]{1,0:T(8,128)(2,1)}, u32[]{:S(2)}) copy-start(bf16[256,128]{1,0:T(8,128)(2,1)} %param.10) | copy-start | bytes 196612
  102.5 24.5 %all-to-all-start.3 = ((f32[32,8,128]{2,1,0:T(8,128)}), f32[32,8,128]{2,1,0:T(8,128)S(1)}, u32[]{:S(2)}, u32[]{:S(2)}) async-start(f32[32,8,128]{2,1,0:T(8,128)} %bitcast.9), calls=%async_computation.3 | async-start | bytes 262144 | tf_op jit(solution)/shard_map/all_to_all | solution.py:12
  162.9 10.7 %all-to-all-start.6 = ((f32[16,8,128]{2,1,0:T(8,128)}), f32[16,8,128]{2,1,0:T(8,128)S(1)}, u32[]{:S(2)}, u32[]{:S(2)}) async-start(f32[16,8,128]{2,1,0:T(8,128)} %broadcast_in_dim.52), calls=%async_computation.6 | async-start | bytes 131072 | tf_op jit(solution)/shard_map/all_to_all | solution.py:12
  198.4 26.4 %all-to-all-start.8 = ((bf16[16,256,128]{2,1,0:T(8,128)(2,1)}), bf16[16,256,128]{2,1,0:T(8,128)(2,1)}, u32[]{:S(2)}, u32[]{:S(2)}) async-start(bf16[16,256,128]{2,1,0:T(8,128)(2,1)} %broadcast_in_dim.53), calls=%async_computation.8 | async-start | bytes 2097152 | tf_op jit(solution)/shard_map/all_to_all | solution.py:12
  207.4 28.0 %copy-start.4 = (pred[16]{0:T(512)(128)(4,1)S(1)}, pred[16]{0:T(512)(128)(4,1)}, u32[]{:S(2)}) copy-start(pred[16]{0:T(512)(128)(4,1)} %copy-done.3) | copy-start | bytes 52
  207.4 28.0 %copy-start.6 = (bf16[16]{0:T(256)(128)(2,1)S(1)}, bf16[16]{0:T(256)(128)(2,1)}, u32[]{:S(2)}) copy-start(bf16[16]{0:T(256)(128)(2,1)} %copy-done.5) | copy-start | bytes 100
  224.8 29.9 %all-to-all-start.7 = ((bf16[16,256,128]{1,2,0:T(8,128)(2,1)}), bf16[16,256,128]{1,2,0:T(8,128)(2,1)S(1)}, u32[]{:S(2)}, u32[]{:S(2)}) async-start(bf16[16,256,128]{1,2,0:T(8,128)(2,1)} %select_convert_fusion), calls=%async_computation.7 | async-start | bytes 2097152 | tf_op jit(solution)/shard_map/all_to_all | solution.py:12
  235.4 19.4 %copy-start.8 = (s32[256]{0:T(256)S(1)}, s32[256]{0:T(256)}, u32[]{:S(2)}) copy-start(s32[256]{0:T(256)} %copy-done.7) | copy-start | bytes 3076
  256.8 20.1 %all-to-all-start.9 = ((f32[32,8,128]{2,1,0:T(8,128)}), f32[32,8,128]{2,1,0:T(8,128)S(1)}, u32[]{:S(2)}, u32[]{:S(2)}) async-start(f32[32,8,128]{2,1,0:T(8,128)} %bitcast.20), calls=%async_computation.9 | async-start | bytes 262144 | tf_op jit(solution)/shard_map/all_to_all | solution.py:12
  312.8 10.7 %all-to-all-start.12 = ((f32[16,8,128]{2,1,0:T(8,128)}), f32[16,8,128]{2,1,0:T(8,128)S(1)}, u32[]{:S(2)}, u32[]{:S(2)}) async-start(f32[16,8,128]{2,1,0:T(8,128)} %broadcast_in_dim.88), calls=%async_computation.12 | async-start | bytes 131072 | tf_op jit(solution)/shard_map/all_to_all | solution.py:12

commit v2 on v1

v2 whole, which is shorter than its diff:
```python
import functools

import jax
import jax.numpy as jnp
from jax import lax
from jax.experimental import pallas as pl
from jax.experimental.pallas import tpu as pltpu
from jax.sharding import Mesh, PartitionSpec as P

ROW = ("zl", "x")
COL = ("zh", "y", "core")
HIGHEST = lax.Precision.HIGHEST
PANEL = 32


def swap(value, axes):
    return lax.all_to_all(value, axes, 0, 0, tiled=True)


def copies_of(block, count):
    return jnp.broadcast_to(block[None], (count,) + block.shape)


FAR = [[(0, 4)], [(0, 8)], [(0, 12)]]
NEAR = [[(0, 1), (4, 5)], [(0, 7), (4, 3)], [(0, 2), (4, 6)]]


def backward(pairs):
    return [(target, source) for source, target in pairs]


def from_first_column(block):
    zh, y, core = (lax.axis_index(axis) for axis in COL)
    far = sum(lax.ppermute(block, ("zh", "y"), pairs) for pairs in FAR)
    block = jnp.where((zh == 0) & (y == 0), block, far)
    near = sum(lax.ppermute(block, "y", pairs) for pairs in NEAR)
    block = jnp.where(y % 4 == 0, block, near)
    other = lax.ppermute(block, "core", [(0, 1)])
    return jnp.where(core == 0, block, other)


def to_first_column(value):
    half = value.shape[0] // 2
    core = lax.axis_index("core")
    given = lax.dynamic_slice_in_dim(value, (1 - core) * half, half)
    value = lax.dynamic_slice_in_dim(value, core * half, half)
    value = value + lax.ppermute(given, "core", [(0, 1), (1, 0)])
    value = value + sum(lax.ppermute(value, "y", backward(pairs)) for pairs in NEAR)
    value = value + sum(lax.ppermute(value, ("zh", "y"), backward(pairs)) for pairs in FAR)
    return jnp.concatenate([value, lax.ppermute(value, "core", [(1, 0)])], axis=0)


VMEM = pl.BlockSpec(memory_space=pltpu.VMEM)
SMEM = pl.BlockSpec(memory_space=pltpu.SMEM)


def column_kernel(by_x, slots_ref, place_ref, tiles_ref, band_ref, out_ref):
    band = band_ref[...]

    def one(t, carry):
        slot = slots_ref[t]
        product = lax.dot_general(
            tiles_ref[t], band, (((0,), (0,)), ((), ())), preferred_element_type=jnp.float32
        )
        where = lax.rem(slot, 4) * 4 + lax.div(slot, 4) if by_x else slot
        out_ref[where] = jnp.where(slot > place_ref[0], product, 0.0).astype(jnp.bfloat16)
        return carry

    lax.fori_loop(0, tiles_ref.shape[0], one, 0, unroll=4)


def column_products(tiles, slots, place, band_block, by_x):
    count, tile = tiles.shape[:2]
    shape = (count, tile, band_block.shape[1])
    return pl.pallas_call(
        functools.partial(column_kernel, by_x),
        out_shape=jax.ShapeDtypeStruct(shape, jnp.bfloat16),
        in_specs=[SMEM, SMEM, VMEM, VMEM],
        out_specs=VMEM,
        cost_estimate=pl.CostEstimate(
            flops=2 * count * tile * tile * shape[2], bytes_accessed=1 << 23, transcendentals=0
        ),
        name="column_products",
    )(slots, place, tiles, band_block)


def normalise_kernel(gram_ref, wide_ref, out_ref, inverse_ref, work):
    size = gram_ref.shape[0]
    work[:, :size] = gram_ref[...]
    down = lax.broadcasted_iota(jnp.int32, (size, size), 0)
    across = lax.broadcasted_iota(jnp.int32, (size, size), 1)
    work[:, size:] = (down == across).astype(jnp.float32)
    rows = lax.broadcasted_iota(jnp.int32, (PANEL, size), 0)
    for start in range(0, size, PANEL):
        left = work[start : start + PANEL, :size]
        right = work[start : start + PANEL, size:]
        lanes = [
            jnp.broadcast_to(left[:, start + j : start + j + 1], (PANEL, size))
            for j in range(PANEL)
        ]
        for k in range(PANEL):
            pivot = jnp.broadcast_to(lanes[k][k : k + 1], (PANEL, size))
            scale = lax.rsqrt(pivot)
            scale = scale * (1.5 - 0.5 * pivot * scale * scale)
            below = jnp.where(rows > k, lanes[k] * scale, 0.0)
            for j in range(k + 1, PANEL):
                lanes[j] = lanes[j] - below * jnp.broadcast_to(below[j : j + 1], (PANEL, size))
            line = left[k : k + 1] * scale[k : k + 1]
            left = jnp.where(rows == k, line, left - below * line)
            line = right[k : k + 1] * scale[k : k + 1]
            right = jnp.where(rows == k, line, right - below * line)
        both = jnp.concatenate([left, right], axis=1)
        work[start : start + PANEL, :] = both
        after = start + PANEL
        if after < size:
            update = lax.dot_general(
                left,
                both,
                (((0,), (0,)), ((), ())),
                precision=HIGHEST,
                preferred_element_type=jnp.float32,
            )
            work[after:, :] = work[after:, :] - update[after:, :]
    out = lax.dot_general(
        wide_ref[...],
        work[:, size:],
        (((1,), (1,)), ((), ())),
        precision=HIGHEST,
        preferred_element_type=jnp.float32,
    )
    out_ref[...] = out.astype(out_ref.dtype)
    inverse_ref[...] = work[:, size:]


def normalise(gram, wide, dtype):
    size = gram.shape[0]
    return pl.pallas_call(
        normalise_kernel,
        out_shape=(
            jax.ShapeDtypeStruct(wide.shape, dtype),
            jax.ShapeDtypeStruct(gram.shape, jnp.float32),
        ),
        in_specs=[pl.BlockSpec(memory_space=pltpu.VMEM)] * 2,
        out_specs=[pl.BlockSpec(memory_space=pltpu.VMEM)] * 2,
        scratch_shapes=[pltpu.VMEM((size, 2 * size), jnp.float32)],
        name="normalise",
    )(gram, wide)


def row_products(tiles, slots, place, blocks):
    keep = (slots >= place).astype(jnp.bfloat16)
    near = jnp.take(blocks, slots, axis=0) * keep[:, None, None]
    return jnp.einsum("tab,tbn->an", tiles, near, preferred_element_type=jnp.float32)


def total(received):
    return jnp.sum(received.astype(jnp.float32), axis=0)


def local(ppmi_tiles, tile_map, sketch):
    row_id, col_id = lax.axis_index(ROW), lax.axis_index(COL)
    first_col = col_id == 0
    tiles = ppmi_tiles[0, 0]
    slots = tile_map[0, 0, 0]
    place = (row_id - 16 * col_id)[None]
    is_diag = slots == place
    diag = tiles[jnp.argmax(is_diag)]
    correction = jnp.swapaxes(jnp.triu(diag, 1), 0, 1) - jnp.tril(diag, -1)
    correction = correction * jnp.any(is_diag).astype(jnp.bfloat16)

    copies, sketch = lax.optimization_barrier((copies_of(sketch, 16), sketch))
    blocks = swap(copies, ROW)
    band_block = from_first_column(sketch)
    received = swap(column_products(tiles, slots, place, band_block, False), ROW)
    row_part = row_products(tiles, slots, place, blocks)
    row_part = row_part + jnp.dot(correction, sketch, preferred_element_type=jnp.float32)
    band = to_first_column(row_part)
    own = total(received) + jnp.where(first_col, band, 0.0)

    blocks = lax.all_gather(own, ROW, axis=0)
    gram = jnp.dot(own.T, own, precision=HIGHEST)
    both = jnp.concatenate([gram.reshape(32, 4, 128), own.reshape(32, 8, 128)], axis=1)
    both = swap(both, COL)
    piece = total(swap(copies_of(total(both[:, :4]), 16), ROW))
    both = swap(copies_of(jnp.concatenate([piece, both[0, 4:]], axis=0), 32), COL)
    gram = both[:, :4].reshape(128, 128)
    band = both[:, 4:].reshape(256, 128)
    band_block, factor = normalise(gram, band, jnp.bfloat16)

    placed = column_products(tiles, slots, place, band_block, True)
    received = total(swap(placed.reshape(4, 4, 256, 128), "x")).astype(jnp.bfloat16)
    received, blocks = lax.optimization_barrier((received, blocks))
    received = swap(received, "zl")
    blocks = lax.dot_general(
        blocks, factor, (((2,), (1,)), ((), ())), precision=HIGHEST
    ).astype(jnp.bfloat16)
    row_part = row_products(tiles, slots, place, blocks)
    row_part = row_part + jnp.dot(correction, band_block, preferred_element_type=jnp.float32)
    col_sum = total(received)
    row_part = row_part + jnp.where(first_col, col_sum, 0.0)
    rest = jnp.where(first_col, 0.0, col_sum)
    band_rows = total(swap(row_part.reshape(32, 8, 128), COL))
    stacked = jnp.concatenate([rest, band_rows], axis=0)
    gram = jnp.dot(stacked.T, stacked, precision=HIGHEST)
    piece = total(swap(gram.reshape(16, 8, 128), ROW))
    both = swap(copies_of(jnp.concatenate([piece, band_rows], axis=0), 32), COL)
    gram = swap(copies_of(total(both[:, :8]), 16), ROW).reshape(128, 128)
    own = jnp.where(first_col, both[:, 8:].reshape(256, 128), rest)
    return normalise(gram, own, jnp.float32)[0]


def solution(mesh):
    fine = Mesh(mesh.devices.reshape(4, 4, 2, 8, 2), ROW + COL)
    in_specs = (
        P(None, ROW, COL, None, None),
        P(None, ROW, COL, None),
        P(COL + ROW, None),
    )
    return jax.shard_map(
        local, mesh=fine, in_specs=in_specs, out_specs=P(COL + ROW, None), check_vma=False
    )
```

time: 349 us -> 282 us (0.81)
  waiting for transfers between devices: 118 us -> 44.6 us
  other arithmetic: 51.9 us -> 6.04 us
  blocking collectives: 69.2 us -> 92.8 us
  Pallas kernels: 0 us -> 19.9 us
  between operations: 2.86 us -> 16.4 us
  local copies, waits for them, and re-layouts: 17.8 us -> 10.4 us
  starting transfers between devices: 74 us -> 80.7 us
  matrix products: 13.7 us -> 9.64 us
    all_to_all x9 -> x6, waiting for transfers between devices: 114 us -> 26.5 us  [swap(): return lax.all_to_all(value, axes, 0, 0, tiled=True)]
    another operation x11 -> x0, other arithmetic: 46.3 us -> none  [the longest x6 24.8 us: one_pass(): factor = jnp.linalg.cholesky(gram)]
    ppermute x1 -> x14, starting transfers between devices: 11.6 us -> 35.5 us  [the longest x3 15.8 us: from_first_column(): far = sum((lax.ppermute(block, ('zh', 'y'), pairs) for pairs in FAR))]
    all_to_all x4 -> x5, blocking collectives: 69.2 us -> 92.8 us  [swap(): return lax.all_to_all(value, axes, 0, 0, tiled=True)]
    pallas_call x0 -> x4, Pallas kernels: none -> 19.9 us  [the longest x2 11.9 us: normalise(): pl.pallas_call(normalise_kernel, out_shape=(jax.ShapeDtypeStruct(wide.sha...]
    all_to_all x9 -> x6, starting transfers between devices: 61.1 us -> 43.9 us  [swap(): return lax.all_to_all(value, axes, 0, 0, tiled=True)]
    ppermute x1 -> x14, waiting for transfers between devices: 1.62 us -> 18 us  [the longest x3 10.7 us: to_first_column(): lax.ppermute(value, ('zh', 'y'), backward(pairs))]
    gather x4 -> x2, local copies, waits for them, and re-layouts: 9.45 us -> 3.32 us  [row_products(): near = jnp.take(blocks, slots, axis=0) * keep[:, None, None]]
  transfers between devices with their start and end apart: 11 -> 22, of which waited for: 11 -> 9; matrix products, arithmetic and copies ran while one was open for 7% -> 7% of each run, Pallas kernels for 0% -> 5%
where the time goes in v2:
time: 282 us; the launch traced here: 280 us
  blocking collectives  92.8 us (33%)
  starting transfers between devices  80.7 us (29%)
  waiting for transfers between devices  44.6 us (16%)
  Pallas kernels  19.9 us (7%)
  between operations  16.4 us (6%)
  local copies, waits for them, and re-layouts  10.4 us (4%)
  matrix products  9.64 us (3%)
  other arithmetic  6.04 us (2%)
    all_to_all x5, blocking collectives, swap(): return lax.all_to_all(value, axes, 0, 0, tiled=True)  92.8 us
    all_to_all x6, starting transfers between devices, swap(): return lax.all_to_all(value, axes, 0, 0, tiled=True)  43.9 us
    all_to_all x6, waiting for transfers between devices, swap(): return lax.all_to_all(value, axes, 0, 0, tiled=True)  26.5 us
    ppermute x3, starting transfers between devices, from_first_column(): far = sum((lax.ppermute(block, ('zh', 'y'), pairs) for pairs in FAR))  15.8 us
    pallas_call x2, Pallas kernels, normalise(): pl.pallas_call(normalise_kernel, out_shape=(jax.ShapeDtypeStruct(wide.sha...  11.9 us
    ppermute x3, waiting for transfers between devices, to_first_column(): lax.ppermute(value, ('zh', 'y'), backward(pairs))  10.7 us
    pallas_call x2, Pallas kernels, column_products(): pl.pallas_call(functools.partial(column_kernel, by_x), out_shape=jax.Shap...  8 us
  transfers between devices with their start and end apart: 22, of which 9 were waited for; matrix products, arithmetic and copies ran while one was open for 7% of the time, Pallas kernels for 5%

profile of v2, /device:TPU:1, one launch (start us, length us, event | category | flops | bytes accessed | tf_op | source)
XLA Modules:
  0.0 280.5 jit_solution(4349716508990422332)
XLA Ops:
  6.5 2.1 broadcast_in_dim.61
  8.6 10.4 %all-to-all-start.1 = ((bf16[16,256,128]{2,1,0:T(8,128)(2,1)}), bf16[16,256,128]{2,1,0:T(8,128)(2,1)S(1)}, u32[]{:S(2)}, u32[]{:S(2)}) async-start(bf16[16,256,128]{2,1,0:T(8,128)(2,1)} %broadcast_in_dim.61), calls=%async_computation.1 | async-start | bytes 2097152 | tf_op jit(solution)/shard_map/all_to_all | solution.py:17
  19.0 13.2 %collective-permute-start.2 = (bf16[256,128]{1,0:T(8,128)(2,1)S(1)}, bf16[256,128]{1,0:T(8,128)(2,1)S(1)}, u32[]{:S(2)}, u32[]{:S(2)}) collective-permute-start(bf16[256,128]{1,0:T(8,128)(2,1)S(1)} %copy-done.2), channel_id=1, source_target_pairs={{0,24},{1,25},{32,56},{33,57},{64,88},{65,89},{96,120},{97,121},{1... | collective-permute-start | bytes 196616 | tf_op jit(solution)/shard_map/ppermute | solution.py:34
  32.2 1.3 collective-permute-start
  47.7 4.0 %column_products.2 = bf16[16,256,128]{2,1,0:T(8,128)(2,1)} custom-call(s32[16]{0:T(128)} %bitcast.65, s32[1]{0:T(128)} %bitcast.1.place_ref, bf16[16,256,256]{2,1,0:T(8,128)(2,1)} %bitcast.57, bf16[256,128]{1,0:T(8,128)(2,1)} %broadcast_select_fusion.1.band_ref), custom_call_target="tpu_custom_call" | custom-call | flops 268435456 | bytes 8388608 | tf_op jit(solution)/shard_map/column_products/pallas_call | solution.py:75
  51.7 8.6 %all-to-all-start = ((bf16[16,256,128]{2,1,0:T(8,128)(2,1)}), bf16[16,256,128]{2,1,0:T(8,128)(2,1)}, u32[]{:S(2)}, u32[]{:S(2)}) async-start(bf16[16,256,128]{2,1,0:T(8,128)(2,1)} %column_products.2), calls=%async_computation | async-start | bytes 2097152 | tf_op jit(solution)/shard_map/all_to_all | solution.py:17
  60.4 1.7 gather_fusion
  62.1 2.0 convolution_bitcast_fusion.1
  64.4 3.9 %collective-permute-start.7 = (f32[128,128]{1,0:T(8,128)S(1)}, f32[128,128]{1,0:T(8,128)S(1)}, u32[]{:S(2)}, u32[]{:S(2)}) collective-permute-start(f32[128,128]{1,0:T(8,128)S(1)} %constant_dynamic-slice_fusion), channel_id=1, source_target_pairs={{0,1},{1,0},{2,3},{3,2},{4,5},{5,4},{6,7},{7,6},{8,9},{9,8},{10,11... | collective-permute-start | bytes 196616 | tf_op jit(solution)/shard_map/ppermute | solution.py:47
  73.0 2.4 collective-permute-done.10
  75.4 2.0 collective-permute-done.8
  82.1 10.7 %collective-permute-done.13 = f32[128,128]{1,0:T(8,128)S(1)} collective-permute-done((f32[128,128]{1,0:T(8,128)S(1)}, f32[128,128]{1,0:T(8,128)S(1)}, u32[]{:S(2)}, u32[]{:S(2)}) %collective-permute-start.13) | collective-permute-done | bytes 65568 | tf_op jit(solution)/shard_map/ppermute | solution.py:49
  92.9 4.2 %collective-permute-start.14 = (f32[128,128]{1,0:T(8,128)S(1)}, f32[128,128]{1,0:T(8,128)S(1)}, u32[]{:S(2)}, u32[]{:S(2)}) collective-permute-start(f32[128,128]{1,0:T(8,128)S(1)} %add_add_fusion), channel_id=1, source_target_pairs={{1,0},{3,2},{5,4},{7,6},{9,8},{11,10},{13,12},{15,14},{17,16},{19,... | collective-permute-start | bytes 196616 | tf_op jit(solution)/shard_map/ppermute | solution.py:50
  97.1 1.4 convert_reduce_fusion
  99.6 18.4 %all_to_all.55 = f32[32,12,128]{2,1,0:T(8,128)S(1)} all-to-all(f32[32,12,128]{2,1,0:T(8,128)S(1)} %pad_maximum_fusion), channel_id=1, replica_groups=mesh['zl'=4,'x'=4,'zh'=2,'y'=8,'core'=2] {'zh','y','core'}, dimensions={0} | all-to-all | bytes 393216 | tf_op jit(solution)/shard_map/all_to_all | solution.py:17
  118.7 6.8 %all-to-all-start.3 = ((f32[16,4,128]{2,1,0:T(4,128)}), f32[16,4,128]{2,1,0:T(4,128)S(1)}, u32[]{:S(2)}, u32[]{:S(2)}) async-start(f32[16,4,128]{2,1,0:T(4,128)} %broadcast_in_dim.63), calls=%async_computation.3 | async-start | bytes 65536 | tf_op jit(solution)/shard_map/all_to_all | solution.py:17
  125.5 7.0 %all-to-all-done.3 = f32[16,4,128]{2,1,0:T(4,128)S(1)} async-done(((f32[16,4,128]{2,1,0:T(4,128)}), f32[16,4,128]{2,1,0:T(4,128)S(1)}, u32[]{:S(2)}, u32[]{:S(2)}) %all-to-all-start.3) | async-done | bytes 32800 | tf_op jit(solution)/shard_map/all_to_all | solution.py:17
  132.6 21.6 %all_to_all.56 = f32[32,12,128]{2,1,0:T(8,128)S(1)} all-to-all(f32[32,12,128]{2,1,0:T(8,128)S(1)} %broadcast_in_dim.64), channel_id=1, replica_groups=mesh['zl'=4,'x'=4,'zh'=2,'y'=8,'core'=2] {'zh','y','core'}, dimensions={0} | all-to-all | bytes 393216 | tf_op jit(solution)/shard_map/all_to_all | solution.py:17
  155.4 5.9 %normalise.2 = (bf16[256,128]{1,0:T(8,128)(2,1)}, f32[128,128]{1,0:T(8,128)}) custom-call(f32[128,128]{1,0:T(8,128)} %bitcast.64, f32[256,128]{1,0:T(8,128)} %slice_bitcast_fusion.1.wide_ref), custom_call_target="tpu_custom_call" | custom-call | tf_op jit(solution)/shard_map/normalise/pallas_call | solution.py:137
  161.4 4.0 %column_products.3 = bf16[16,256,128]{2,1,0:T(8,128)(2,1)} custom-call(s32[16]{0:T(128)} %bitcast.66, s32[1]{0:T(128)} %bitcast.1.place_ref, bf16[16,256,256]{2,1,0:T(8,128)(2,1)} %bitcast.58, bf16[256,128]{1,0:T(8,128)(2,1)} %get-tuple-element.17.band_ref), custom_call_target="tpu_custom_call" | custom-call | flops 268435456 | bytes 8388608 | tf_op jit(solution)/shard_map/column_products/pallas_call | solution.py:75
  165.4 17.6 %all_to_all.57 = bf16[4,4,256,128]{3,2,1,0:T(8,128)(2,1)S(1)} all-to-all(bf16[4,4,256,128]{3,2,1,0:T(8,128)(2,1)} %bitcast.59), channel_id=1, replica_groups=mesh['zl'=4,'x'=4,'zh'=2,'y'=8,'core'=2] {'x'}, dimensions={0} | all-to-all | bytes 2097152 | tf_op jit(solution)/shard_map/all_to_all | solution.py:17
  183.8 3.6 %all-to-all-start.6 = ((bf16[4,256,128]{2,1,0:T(8,128)(2,1)}), bf16[4,256,128]{2,1,0:T(8,128)(2,1)S(1)}, u32[]{:S(2)}, u32[]{:S(2)}) async-start(bf16[4,256,128]{2,1,0:T(8,128)(2,1)} %reduce_sum.80), calls=%async_computation.6 | async-start | bytes 524288 | tf_op jit(solution)/shard_map/all_to_all | solution.py:17
  187.4 3.5 %convolution_convert_fusion = bf16[16,256,128]{2,1,0:T(8,128)(2,1)S(1)} fusion(f32[16,256,128]{2,1,0:T(8,128)} %all-gather.2.cloned.1.call-done, f32[128,128]{1,0:T(8,128)} %get-tuple-element.20), kind=kOutput, calls=%fused_computation.3 | convolution fusion | flops 805830656 | bytes 3211264 | tf_op jit(solution)/shard_map/dot_general | solution.py:194
  191.0 1.6 gather_fusion.1
  192.6 2.0 convolution_bitcast_fusion
  195.7 11.1 %all-to-all-start.7 = ((f32[32,8,128]{2,1,0:T(8,128)}), f32[32,8,128]{2,1,0:T(8,128)S(1)}, u32[]{:S(2)}, u32[]{:S(2)}) async-start(f32[32,8,128]{2,1,0:T(8,128)} %fusion.1), calls=%async_computation.7 | async-start | bytes 262144 | tf_op jit(solution)/shard_map/all_to_all | solution.py:17
  206.8 13.0 %all-to-all-done.7 = f32[32,8,128]{2,1,0:T(8,128)S(1)} async-done(((f32[32,8,128]{2,1,0:T(8,128)}), f32[32,8,128]{2,1,0:T(8,128)S(1)}, u32[]{:S(2)}, u32[]{:S(2)}) %all-to-all-start.7) | async-done | bytes 131104 | tf_op jit(solution)/shard_map/all_to_all | solution.py:17
  220.3 13.7 %all_to_all.58 = f32[16,8,128]{2,1,0:T(8,128)S(1)} all-to-all(f32[16,8,128]{2,1,0:T(8,128)S(1)} %convolution_bitcast_fusion.2), channel_id=1, replica_groups=mesh['zl'=4,'x'=4,'zh'=2,'y'=8,'core'=2] {'zl','x'}, dimensions={0} | all-to-all | bytes 131072 | tf_op jit(solution)/shard_map/all_to_all | solution.py:17
  234.0 21.6 %all_to_all.59 = f32[32,16,128]{2,1,0:T(8,128)S(1)} all-to-all(f32[32,16,128]{2,1,0:T(8,128)S(1)} %broadcast_in_dim.66), channel_id=1, replica_groups=mesh['zl'=4,'x'=4,'zh'=2,'y'=8,'core'=2] {'zh','y','core'}, dimensions={0} | all-to-all | bytes 524288 | tf_op jit(solution)/shard_map/all_to_all | solution.py:17
  256.3 3.5 %all-to-all-start.10 = ((f32[16,8,128]{2,1,0:T(8,128)}), f32[16,8,128]{2,1,0:T(8,128)S(1)}, u32[]{:S(2)}, u32[]{:S(2)}) async-start(f32[16,8,128]{2,1,0:T(8,128)} %broadcast_in_dim.67), calls=%async_computation.10 | async-start | bytes 131072 | tf_op jit(solution)/shard_map/all_to_all | solution.py:17
  260.5 6.5 %all-to-all-done.10 = f32[16,8,128]{2,1,0:T(8,128)S(1)} async-done(((f32[16,8,128]{2,1,0:T(8,128)}), f32[16,8,128]{2,1,0:T(8,128)S(1)}, u32[]{:S(2)}, u32[]{:S(2)}) %all-to-all-start.10) | async-done | bytes 65568 | tf_op jit(solution)/shard_map/all_to_all | solution.py:17
  267.7 6.0 %normalise.3 = (f32[256,128]{1,0:T(8,128)}, f32[128,128]{1,0:T(8,128)}) custom-call(f32[128,128]{1,0:T(8,128)} %bitcast.63, f32[256,128]{1,0:T(8,128)} %fusion.16.wide_ref), custom_call_target="tpu_custom_call" | custom-call | tf_op jit(solution)/shard_map/normalise/pallas_call | solution.py:137
  (86 shorter events, 28.9 us)
Async XLA Ops:
  6.5 12.5 %copy-start.2 = (bf16[256,128]{1,0:T(8,128)(2,1)S(1)}, bf16[256,128]{1,0:T(8,128)(2,1)}, u32[]{:S(2)}) copy-start(bf16[256,128]{1,0:T(8,128)(2,1)} %param.7) | copy-start | bytes 196612
  6.5 28.3 %copy-start.7 = (s32[1,1,1,16]{3,2,1,0:T(1,128)S(1)}, s32[1,1,1,16]{3,2,1,0:T(1,128)}, u32[]{:S(2)}) copy-start(s32[1,1,1,16]{3,2,1,0:T(1,128)} %param.6) | copy-start | bytes 196
  8.6 43.1 %all-to-all-start.1 = ((bf16[16,256,128]{2,1,0:T(8,128)(2,1)}), bf16[16,256,128]{2,1,0:T(8,128)(2,1)S(1)}, u32[]{:S(2)}, u32[]{:S(2)}) async-start(bf16[16,256,128]{2,1,0:T(8,128)(2,1)} %broadcast_in_dim.61), calls=%async_computation.1 | async-start | bytes 2097152 | tf_op jit(solution)/shard_map/all_to_all | solution.py:17
  19.0 16.5 %collective-permute-start.2 = (bf16[256,128]{1,0:T(8,128)(2,1)S(1)}, bf16[256,128]{1,0:T(8,128)(2,1)S(1)}, u32[]{:S(2)}, u32[]{:S(2)}) collective-permute-start(bf16[256,128]{1,0:T(8,128)(2,1)S(1)} %copy-done.2), channel_id=1, source_target_pairs={{0,24},{1,25},{32,56},{33,57},{64,88},{65,89},{96,120},{97,121},{1... | collective-permute-start | bytes 196616 | tf_op jit(solution)/shard_map/ppermute | solution.py:34
  32.2 3.3 %collective-permute-start = (bf16[256,128]{1,0:T(8,128)(2,1)S(1)}, bf16[256,128]{1,0:T(8,128)(2,1)S(1)}, u32[]{:S(2)}, u32[]{:S(2)}) collective-permute-start(bf16[256,128]{1,0:T(8,128)(2,1)S(1)} %copy-done.2), channel_id=1, source_target_pairs={{0,8},{1,9},{32,40},{33,41},{64,72},{65,73},{96,104},{97,105},{128... | collective-permute-start | bytes 196616 | tf_op jit(solution)/shard_map/ppermute | solution.py:34
  33.5 3.3 %collective-permute-start.1 = (bf16[256,128]{1,0:T(8,128)(2,1)S(1)}, bf16[256,128]{1,0:T(8,128)(2,1)S(1)}, u32[]{:S(2)}, u32[]{:S(2)}) collective-permute-start(bf16[256,128]{1,0:T(8,128)(2,1)S(1)} %copy-done.2), channel_id=1, source_target_pairs={{0,16},{1,17},{32,48},{33,49},{64,80},{65,81},{96,112},{97,113},{1... | collective-permute-start | bytes 196616 | tf_op jit(solution)/shard_map/ppermute | solution.py:34
  36.8 6.5 %collective-permute-start.5 = (bf16[256,128]{1,0:T(8,128)(2,1)S(1)}, bf16[256,128]{1,0:T(8,128)(2,1)S(1)}, u32[]{:S(2)}, u32[]{:S(2)}) collective-permute-start(bf16[256,128]{1,0:T(8,128)(2,1)S(1)} %add_select_fusion.1), channel_id=1, source_target_pairs={{0,4},{8,12},{1,5},{9,13},{16,20},{24,28},{17,21},{25,29},{32,36},... | collective-permute-start | bytes 196616 | tf_op jit(solution)/shard_map/ppermute | solution.py:36
  38.1 5.2 %collective-permute-start.3 = (bf16[256,128]{1,0:T(8,128)(2,1)S(1)}, bf16[256,128]{1,0:T(8,128)(2,1)S(1)}, u32[]{:S(2)}, u32[]{:S(2)}) collective-permute-start(bf16[256,128]{1,0:T(8,128)(2,1)S(1)} %add_select_fusion.1), channel_id=1, source_target_pairs={{0,2},{8,10},{1,3},{9,11},{16,18},{24,26},{17,19},{25,27},{32,34},... | collective-permute-start | bytes 196616 | tf_op jit(solution)/shard_map/ppermute | solution.py:36
  39.4 3.9 %collective-permute-start.4 = (bf16[256,128]{1,0:T(8,128)(2,1)S(1)}, bf16[256,128]{1,0:T(8,128)(2,1)S(1)}, u32[]{:S(2)}, u32[]{:S(2)}) collective-permute-start(bf16[256,128]{1,0:T(8,128)(2,1)S(1)} %add_select_fusion.1), channel_id=1, source_target_pairs={{0,14},{8,6},{1,15},{9,7},{16,30},{24,22},{17,31},{25,23},{32,46},... | collective-permute-start | bytes 196616 | tf_op jit(solution)/shard_map/ppermute | solution.py:36
  43.4 3.7 %collective-permute-start.6 = (bf16[256,128]{1,0:T(8,128)(2,1)S(1)}, bf16[256,128]{1,0:T(8,128)(2,1)S(1)}, u32[]{:S(2)}, u32[]{:S(2)}) collective-permute-start(bf16[256,128]{1,0:T(8,128)(2,1)S(1)} %add_select_fusion), channel_id=1, source_target_pairs={{0,1},{2,3},{4,5},{6,7},{8,9},{10,11},{12,13},{14,15},{16,17},{18,... | collective-permute-start | bytes 196616 | tf_op jit(solution)/shard_map/ppermute | solution.py:38
  47.7 12.6 %copy-start.8 = (s32[1,1,1,16]{3,2,1,0:T(1,128)S(1)}, s32[1,1,1,16]{3,2,1,0:T(1,128)}, u32[]{:S(2)}) copy-start(s32[1,1,1,16]{3,2,1,0:T(1,128)} %param.6) | copy-start | bytes 196
  51.7 10.3 %copy-start = (bf16[1,1,16,256,256]{4,3,2,1,0:T(8,128)(2,1)S(1)}, bf16[1,1,16,256,256]{4,3,2,1,0:T(8,128)(2,1)}, u32[]{:S(2)}) copy-start(bf16[1,1,16,256,256]{4,3,2,1,0:T(8,128)(2,1)} %param.5) | copy-start | bytes 6291460
  51.7 45.3 %all-to-all-start = ((bf16[16,256,128]{2,1,0:T(8,128)(2,1)}), bf16[16,256,128]{2,1,0:T(8,128)(2,1)}, u32[]{:S(2)}, u32[]{:S(2)}) async-start(bf16[16,256,128]{2,1,0:T(8,128)(2,1)} %column_products.2), calls=%async_computation | async-start | bytes 2097152 | tf_op jit(solution)/shard_map/all_to_all | solution.py:17
  60.3 123.5 %all-gather.2.cloned.1.call-start = ((), (), s32[]{:S(2)}) async-start(), calls=%async_computation.11 | async-start | bytes 2228224 | tf_op jit(solution)/shard_map/all_gather | solution.py:180
  62.1 2.0 copy-start.4
  64.4 4.7 %collective-permute-start.7 = (f32[128,128]{1,0:T(8,128)S(1)}, f32[128,128]{1,0:T(8,128)S(1)}, u32[]{:S(2)}, u32[]{:S(2)}) collective-permute-start(f32[128,128]{1,0:T(8,128)S(1)} %constant_dynamic-slice_fusion), channel_id=1, source_target_pairs={{0,1},{1,0},{2,3},{3,2},{4,5},{5,4},{6,7},{7,6},{8,9},{9,8},{10,11... | collective-permute-start | bytes 196616 | tf_op jit(solution)/shard_map/ppermute | solution.py:47
  69.1 6.3 %collective-permute-start.10 = (f32[128,128]{1,0:T(8,128)S(1)}, f32[128,128]{1,0:T(8,128)S(1)}, u32[]{:S(2)}, u32[]{:S(2)}) collective-permute-start(f32[128,128]{1,0:T(8,128)S(1)} %dynamic-slice_add_fusion), channel_id=1, source_target_pairs={{4,0},{12,8},{5,1},{13,9},{20,16},{28,24},{21,17},{29,25},{36,32},... | collective-permute-start | bytes 196616 | tf_op jit(solution)/shard_map/ppermute | solution.py:48
  70.4 7.0 %collective-permute-start.8 = (f32[128,128]{1,0:T(8,128)S(1)}, f32[128,128]{1,0:T(8,128)S(1)}, u32[]{:S(2)}, u32[]{:S(2)}) collective-permute-start(f32[128,128]{1,0:T(8,128)S(1)} %dynamic-slice_add_fusion), channel_id=1, source_target_pairs={{2,0},{10,8},{3,1},{11,9},{18,16},{26,24},{19,17},{27,25},{34,32},... | collective-permute-start | bytes 196616 | tf_op jit(solution)/shard_map/ppermute | solution.py:48
  71.7 6.4 %collective-permute-start.9 = (f32[128,128]{1,0:T(8,128)S(1)}, f32[128,128]{1,0:T(8,128)S(1)}, u32[]{:S(2)}, u32[]{:S(2)}) collective-permute-start(f32[128,128]{1,0:T(8,128)S(1)} %dynamic-slice_add_fusion), channel_id=1, source_target_pairs={{14,0},{6,8},{15,1},{7,9},{30,16},{22,24},{31,17},{23,25},{46,32},... | collective-permute-start | bytes 196616 | tf_op jit(solution)/shard_map/ppermute | solution.py:48
  78.2 14.6 %collective-permute-start.13 = (f32[128,128]{1,0:T(8,128)S(1)}, f32[128,128]{1,0:T(8,128)S(1)}, u32[]{:S(2)}, u32[]{:S(2)}) collective-permute-start(f32[128,128]{1,0:T(8,128)S(1)} %add_add_fusion.1), channel_id=1, source_target_pairs={{24,0},{25,1},{56,32},{57,33},{88,64},{89,65},{120,96},{121,97},{1... | collective-permute-start | bytes 196616 | tf_op jit(solution)/shard_map/ppermute | solution.py:49
  79.5 13.3 %collective-permute-start.11 = (f32[128,128]{1,0:T(8,128)S(1)}, f32[128,128]{1,0:T(8,128)S(1)}, u32[]{:S(2)}, u32[]{:S(2)}) collective-permute-start(f32[128,128]{1,0:T(8,128)S(1)} %add_add_fusion.1), channel_id=1, source_target_pairs={{8,0},{9,1},{40,32},{41,33},{72,64},{73,65},{104,96},{105,97},{136... | collective-permute-start | bytes 196616 | tf_op jit(solution)/shard_map/ppermute | solution.py:49
  80.8 12.0 %collective-permute-start.12 = (f32[128,128]{1,0:T(8,128)S(1)}, f32[128,128]{1,0:T(8,128)S(1)}, u32[]{:S(2)}, u32[]{:S(2)}) collective-permute-start(f32[128,128]{1,0:T(8,128)S(1)} %add_add_fusion.1), channel_id=1, source_target_pairs={{16,0},{17,1},{48,32},{49,33},{80,64},{81,65},{112,96},{113,97},{1... | collective-permute-start | bytes 196616 | tf_op jit(solution)/shard_map/ppermute | solution.py:49
  92.9 5.6 %collective-permute-start.14 = (f32[128,128]{1,0:T(8,128)S(1)}, f32[128,128]{1,0:T(8,128)S(1)}, u32[]{:S(2)}, u32[]{:S(2)}) collective-permute-start(f32[128,128]{1,0:T(8,128)S(1)} %add_add_fusion), channel_id=1, source_target_pairs={{1,0},{3,2},{5,4},{7,6},{9,8},{11,10},{13,12},{15,14},{17,16},{19,... | collective-permute-start | bytes 196616 | tf_op jit(solution)/shard_map/ppermute | solution.py:50
  118.7 13.8 %all-to-all-start.3 = ((f32[16,4,128]{2,1,0:T(4,128)}), f32[16,4,128]{2,1,0:T(4,128)S(1)}, u32[]{:S(2)}, u32[]{:S(2)}) async-start(f32[16,4,128]{2,1,0:T(4,128)} %broadcast_in_dim.63), calls=%async_computation.3 | async-start | bytes 65536 | tf_op jit(solution)/shard_map/all_to_all | solution.py:17
  183.8 10.8 %all-to-all-start.6 = ((bf16[4,256,128]{2,1,0:T(8,128)(2,1)}), bf16[4,256,128]{2,1,0:T(8,128)(2,1)S(1)}, u32[]{:S(2)}, u32[]{:S(2)}) async-start(bf16[4,256,128]{2,1,0:T(8,128)(2,1)} %reduce_sum.80), calls=%async_computation.6 | async-start | bytes 524288 | tf_op jit(solution)/shard_map/all_to_all | solution.py:17
  187.4 5.2 %copy-start.1 = (bf16[1,1,16,256,256]{4,3,2,1,0:T(8,128)(2,1)S(1)}, bf16[1,1,16,256,256]{4,3,2,1,0:T(8,128)(2,1)}, u32[]{:S(2)}) copy-start(bf16[1,1,16,256,256]{4,3,2,1,0:T(8,128)(2,1)} %param.5) | copy-start | bytes 6291460
  192.6 2.1 copy-start.5
  192.6 2.1 copy-start.6
  195.7 24.1 %all-to-all-start.7 = ((f32[32,8,128]{2,1,0:T(8,128)}), f32[32,8,128]{2,1,0:T(8,128)S(1)}, u32[]{:S(2)}, u32[]{:S(2)}) async-start(f32[32,8,128]{2,1,0:T(8,128)} %fusion.1), calls=%async_computation.7 | async-start | bytes 262144 | tf_op jit(solution)/shard_map/all_to_all | solution.py:17
  256.3 10.7 %all-to-all-start.10 = ((f32[16,8,128]{2,1,0:T(8,128)}), f32[16,8,128]{2,1,0:T(8,128)S(1)}, u32[]{:S(2)}, u32[]{:S(2)}) async-start(f32[16,8,128]{2,1,0:T(8,128)} %broadcast_in_dim.67), calls=%async_computation.10 | async-start | bytes 131072 | tf_op jit(solution)/shard_map/all_to_all | solution.py:17
  267.1 0.6 copy-start.3
Sparse Core Ops, SparseCore 0:
  99.3 72.2 all-gather.1

commit v3 on v2

--- a/solution.py
+++ b/solution.py
@@ -9,6 +9,8 @@
 
 ROW = ("zl", "x")
 COL = ("zh", "y", "core")
+PLANE = ("y", "core")
+ACROSS = ROW + ("zh",)
 HIGHEST = lax.Precision.HIGHEST
 PANEL = 32
 
@@ -179,12 +181,15 @@
 
     blocks = lax.all_gather(own, ROW, axis=0)
     gram = jnp.dot(own.T, own, precision=HIGHEST)
-    both = jnp.concatenate([gram.reshape(32, 4, 128), own.reshape(32, 8, 128)], axis=1)
-    both = swap(both, COL)
-    piece = total(swap(copies_of(total(both[:, :4]), 16), ROW))
-    both = swap(copies_of(jnp.concatenate([piece, both[0, 4:]], axis=0), 32), COL)
-    gram = both[:, :4].reshape(128, 128)
-    band = both[:, 4:].reshape(256, 128)
+    both = jnp.concatenate([gram.reshape(16, 8, 128), own.reshape(16, 16, 128)], axis=1)
+    both = swap(both, PLANE)
+    lines = both[0, 8:]
+    other = lax.ppermute(lines, "zh", [(0, 1)])
+    lines = jnp.where(lax.axis_index("zh") == 0, lines, other)
+    piece = total(swap(copies_of(total(both[:, :8]), 32), ACROSS))
+    both = swap(copies_of(jnp.concatenate([piece, lines], axis=0), 16), PLANE)
+    gram = both[:, :8].reshape(128, 128)
+    band = both[:, 8:].reshape(256, 128)
     band_block, factor = normalise(gram, band, jnp.bfloat16)
 
     placed = column_products(tiles, slots, place, band_block, True)
@@ -202,10 +207,14 @@
     band_rows = total(swap(row_part.reshape(32, 8, 128), COL))
     stacked = jnp.concatenate([rest, band_rows], axis=0)
     gram = jnp.dot(stacked.T, stacked, precision=HIGHEST)
-    piece = total(swap(gram.reshape(16, 8, 128), ROW))
-    both = swap(copies_of(jnp.concatenate([piece, band_rows], axis=0), 32), COL)
-    gram = swap(copies_of(total(both[:, :8]), 16), ROW).reshape(128, 128)
-    own = jnp.where(first_col, both[:, 8:].reshape(256, 128), rest)
+    piece = total(swap(gram.reshape(16, 8, 128), PLANE))
+    piece = total(swap(copies_of(piece, 32), ACROSS))
+    other = lax.ppermute(band_rows, "zh", [(1, 0)])
+    both = jnp.concatenate([piece, band_rows, other], axis=0)
+    both = swap(copies_of(both, 16), PLANE)
+    gram = both[:, :8].reshape(128, 128)
+    band = both[:, 8:].reshape(16, 2, 8, 128).swapaxes(0, 1).reshape(256, 128)
+    own = jnp.where(first_col, band, rest)
     return normalise(gram, own, jnp.float32)[0]
 
 

time: 282 us -> 275 us (0.975)
  blocking collectives: 92.8 us -> 75.3 us
  starting transfers between devices: 80.7 us -> 93.5 us
    all_to_all x5, blocking collectives: 92.8 us -> 75.3 us  [swap(): return lax.all_to_all(value, axes, 0, 0, tiled=True)]
    ppermute x0 -> x2, starting transfers between devices: none -> 8.33 us  [the longest x1 7.04 us: local(): other = lax.ppermute(lines, 'zh', [(0, 1)])]
    all_to_all x6, starting transfers between devices: 43.9 us -> 48.4 us  [swap(): return lax.all_to_all(value, axes, 0, 0, tiled=True)]
  transfers between devices with their start and end apart: 22 -> 24, of which waited for: 9 -> 10; matrix products, arithmetic and copies ran while one was open for 7% -> 7% of each run, Pallas kernels for 5% -> 5%
where the time goes in v3:
time: 275 us; the launch traced here: 274 us
  starting transfers between devices  93.5 us (34%)
  blocking collectives  75.3 us (27%)
  waiting for transfers between devices  42.9 us (16%)
  Pallas kernels  19.9 us (7%)
  between operations  16.5 us (6%)
  local copies, waits for them, and re-layouts  10.4 us (4%)
  matrix products  9.64 us (4%)
  other arithmetic  5.94 us (2%)
    all_to_all x5, blocking collectives, swap(): return lax.all_to_all(value, axes, 0, 0, tiled=True)  75.3 us
    all_to_all x6, starting transfers between devices, swap(): return lax.all_to_all(value, axes, 0, 0, tiled=True)  48.4 us
    all_to_all x6, waiting for transfers between devices, swap(): return lax.all_to_all(value, axes, 0, 0, tiled=True)  24.1 us
    ppermute x3, starting transfers between devices, from_first_column(): far = sum((lax.ppermute(block, ('zh', 'y'), pairs) for pairs in FAR))  15.8 us
    pallas_call x2, Pallas kernels, normalise(): pl.pallas_call(normalise_kernel, out_shape=(jax.ShapeDtypeStruct(wide.sha...  11.9 us
    ppermute x3, waiting for transfers between devices, to_first_column(): lax.ppermute(value, ('zh', 'y'), backward(pairs))  10.7 us
    pallas_call x2, Pallas kernels, column_products(): pl.pallas_call(functools.partial(column_kernel, by_x), out_shape=jax.Shap...  7.99 us
    ppermute x1, starting transfers between devices, local(): other = lax.ppermute(lines, 'zh', [(0, 1)])  7.04 us
  transfers between devices with their start and end apart: 24, of which 10 were waited for; matrix products, arithmetic and copies ran while one was open for 7% of the time, Pallas kernels for 5%

profile of v3, /device:TPU:1, one launch (start us, length us, event | category | flops | bytes accessed | tf_op | source)
XLA Modules:
  0.0 274.1 jit_solution(16575025234175990759)
XLA Ops:
  6.5 2.1 broadcast_in_dim.61
  8.6 10.4 %all-to-all-start.1 = ((bf16[16,256,128]{2,1,0:T(8,128)(2,1)}), bf16[16,256,128]{2,1,0:T(8,128)(2,1)S(1)}, u32[]{:S(2)}, u32[]{:S(2)}) async-start(bf16[16,256,128]{2,1,0:T(8,128)(2,1)} %broadcast_in_dim.61), calls=%async_computation.1 | async-start | bytes 2097152 | tf_op jit(solution)/shard_map/all_to_all | solution.py:19
  19.0 13.2 %collective-permute-start.2 = (bf16[256,128]{1,0:T(8,128)(2,1)S(1)}, bf16[256,128]{1,0:T(8,128)(2,1)S(1)}, u32[]{:S(2)}, u32[]{:S(2)}) collective-permute-start(bf16[256,128]{1,0:T(8,128)(2,1)S(1)} %copy-done.2), channel_id=1, source_target_pairs={{0,24},{1,25},{32,56},{33,57},{64,88},{65,89},{96,120},{97,121},{1... | collective-permute-start | bytes 196616 | tf_op jit(solution)/shard_map/ppermute | solution.py:36
  47.7 4.0 %column_products.2 = bf16[16,256,128]{2,1,0:T(8,128)(2,1)} custom-call(s32[16]{0:T(128)} %bitcast.71, s32[1]{0:T(128)} %bitcast.1.place_ref, bf16[16,256,256]{2,1,0:T(8,128)(2,1)} %bitcast.64, bf16[256,128]{1,0:T(8,128)(2,1)} %broadcast_select_fusion.1.band_ref), custom_call_target="tpu_custom_call" | custom-call | flops 268435456 | bytes 8388608 | tf_op jit(solution)/shard_map/column_products/pallas_call | solution.py:77
  51.7 8.6 %all-to-all-start = ((bf16[16,256,128]{2,1,0:T(8,128)(2,1)}), bf16[16,256,128]{2,1,0:T(8,128)(2,1)}, u32[]{:S(2)}, u32[]{:S(2)}) async-start(bf16[16,256,128]{2,1,0:T(8,128)(2,1)} %column_products.2), calls=%async_computation | async-start | bytes 2097152 | tf_op jit(solution)/shard_map/all_to_all | solution.py:19
  60.4 1.7 gather_fusion
  62.1 2.0 convolution_bitcast_fusion.1
  64.4 3.8 %collective-permute-start.7 = (f32[128,128]{1,0:T(8,128)S(1)}, f32[128,128]{1,0:T(8,128)S(1)}, u32[]{:S(2)}, u32[]{:S(2)}) collective-permute-start(f32[128,128]{1,0:T(8,128)S(1)} %constant_dynamic-slice_fusion), channel_id=1, source_target_pairs={{0,1},{1,0},{2,3},{3,2},{4,5},{5,4},{6,7},{7,6},{8,9},{9,8},{10,11... | collective-permute-start | bytes 196616 | tf_op jit(solution)/shard_map/ppermute | solution.py:49
  73.0 2.4 collective-permute-done.10
  75.4 2.0 collective-permute-done.8
  82.0 10.7 %collective-permute-done.13 = f32[128,128]{1,0:T(8,128)S(1)} collective-permute-done((f32[128,128]{1,0:T(8,128)S(1)}, f32[128,128]{1,0:T(8,128)S(1)}, u32[]{:S(2)}, u32[]{:S(2)}) %collective-permute-start.13) | collective-permute-done | bytes 65568 | tf_op jit(solution)/shard_map/ppermute | solution.py:51
  92.8 4.2 %collective-permute-start.14 = (f32[128,128]{1,0:T(8,128)S(1)}, f32[128,128]{1,0:T(8,128)S(1)}, u32[]{:S(2)}, u32[]{:S(2)}) collective-permute-start(f32[128,128]{1,0:T(8,128)S(1)} %add_add_fusion), channel_id=1, source_target_pairs={{1,0},{3,2},{5,4},{7,6},{9,8},{11,10},{13,12},{15,14},{17,16},{19,... | collective-permute-start | bytes 196616 | tf_op jit(solution)/shard_map/ppermute | solution.py:52
  97.0 1.4 convert_reduce_fusion
  99.5 12.8 %all_to_all.55 = f32[16,24,128]{2,1,0:T(8,128)S(1)} all-to-all(f32[16,24,128]{2,1,0:T(8,128)S(1)} %pad_maximum_fusion), channel_id=1, replica_groups=mesh['zl'=4,'x'=4,'zh'=2,'y'=8,'core'=2] {'y','core'}, dimensions={0} | all-to-all | bytes 393216 | tf_op jit(solution)/shard_map/all_to_all | solution.py:19
  113.0 7.1 %all-to-all-start.3 = ((f32[32,8,128]{2,1,0:T(8,128)}), f32[32,8,128]{2,1,0:T(8,128)S(1)}, u32[]{:S(2)}, u32[]{:S(2)}) async-start(f32[32,8,128]{2,1,0:T(8,128)} %broadcast_in_dim.63), calls=%async_computation.3 | async-start | bytes 262144 | tf_op jit(solution)/shard_map/all_to_all | solution.py:19
  120.1 7.0 %collective-permute-start.15 = (f32[16,128]{1,0:T(8,128)S(1)}, f32[16,128]{1,0:T(8,128)S(1)}, u32[]{:S(2)}, u32[]{:S(2)}) collective-permute-start(f32[16,128]{1,0:T(8,128)S(1)} %slice_bitcast_fusion.3), channel_id=1, source_target_pairs={{0,16},{1,17},{2,18},{3,19},{4,20},{5,21},{6,22},{7,23},{8,24},{9,... | collective-permute-start | bytes 24584 | tf_op jit(solution)/shard_map/ppermute | solution.py:187
  128.0 3.3 %all-to-all-done.3 = f32[32,8,128]{2,1,0:T(8,128)S(1)} async-done(((f32[32,8,128]{2,1,0:T(8,128)}), f32[32,8,128]{2,1,0:T(8,128)S(1)}, u32[]{:S(2)}, u32[]{:S(2)}) %all-to-all-start.3) | async-done | bytes 131104 | tf_op jit(solution)/shard_map/all_to_all | solution.py:19
  131.3 13.8 %all_to_all.56 = f32[16,24,128]{2,1,0:T(8,128)S(1)} all-to-all(f32[16,24,128]{2,1,0:T(8,128)S(1)} %broadcast_in_dim.64), channel_id=1, replica_groups=mesh['zl'=4,'x'=4,'zh'=2,'y'=8,'core'=2] {'y','core'}, dimensions={0} | all-to-all | bytes 393216 | tf_op jit(solution)/shard_map/all_to_all | solution.py:19
  146.4 5.9 %normalise.2 = (bf16[256,128]{1,0:T(8,128)(2,1)}, f32[128,128]{1,0:T(8,128)}) custom-call(f32[128,128]{1,0:T(8,128)} %slice_bitcast_fusion.2.gram_ref, f32[256,128]{1,0:T(8,128)} %bitcast.69), custom_call_target="tpu_custom_call" | custom-call | tf_op jit(solution)/shard_map/normalise/pallas_call | solution.py:139
  152.4 4.0 %column_products.3 = bf16[16,256,128]{2,1,0:T(8,128)(2,1)} custom-call(s32[16]{0:T(128)} %bitcast.72, s32[1]{0:T(128)} %bitcast.1.place_ref, bf16[16,256,256]{2,1,0:T(8,128)(2,1)} %bitcast.65, bf16[256,128]{1,0:T(8,128)(2,1)} %get-tuple-element.17.band_ref), custom_call_target="tpu_custom_call" | custom-call | flops 268435456 | bytes 8388608 | tf_op jit(solution)/shard_map/column_products/pallas_call | solution.py:77
  156.4 22.3 %all_to_all.57 = bf16[4,4,256,128]{3,2,1,0:T(8,128)(2,1)S(1)} all-to-all(bf16[4,4,256,128]{3,2,1,0:T(8,128)(2,1)} %bitcast.66), channel_id=1, replica_groups=mesh['zl'=4,'x'=4,'zh'=2,'y'=8,'core'=2] {'x'}, dimensions={0} | all-to-all | bytes 2097152 | tf_op jit(solution)/shard_map/all_to_all | solution.py:19
  179.5 3.6 %all-to-all-start.6 = ((bf16[4,256,128]{2,1,0:T(8,128)(2,1)}), bf16[4,256,128]{2,1,0:T(8,128)(2,1)S(1)}, u32[]{:S(2)}, u32[]{:S(2)}) async-start(bf16[4,256,128]{2,1,0:T(8,128)(2,1)} %reduce_sum.80), calls=%async_computation.6 | async-start | bytes 524288 | tf_op jit(solution)/shard_map/all_to_all | solution.py:19
  183.1 3.5 %convolution_convert_fusion = bf16[16,256,128]{2,1,0:T(8,128)(2,1)S(1)} fusion(f32[16,256,128]{2,1,0:T(8,128)} %all-gather.2.cloned.1.call-done, f32[128,128]{1,0:T(8,128)} %get-tuple-element.20), kind=kOutput, calls=%fused_computation.3 | convolution fusion | flops 805830656 | bytes 3211264 | tf_op jit(solution)/shard_map/dot_general | solution.py:199
  186.7 1.7 gather_fusion.1
  188.3 2.0 convolution_bitcast_fusion
  191.4 11.5 %all-to-all-start.7 = ((f32[32,8,128]{2,1,0:T(8,128)}), f32[32,8,128]{2,1,0:T(8,128)S(1)}, u32[]{:S(2)}, u32[]{:S(2)}) async-start(f32[32,8,128]{2,1,0:T(8,128)} %fusion.1), calls=%async_computation.7 | async-start | bytes 262144 | tf_op jit(solution)/shard_map/all_to_all | solution.py:19
  202.9 13.0 %all-to-all-done.7 = f32[32,8,128]{2,1,0:T(8,128)S(1)} async-done(((f32[32,8,128]{2,1,0:T(8,128)}), f32[32,8,128]{2,1,0:T(8,128)S(1)}, u32[]{:S(2)}, u32[]{:S(2)}) %all-to-all-start.7) | async-done | bytes 131104 | tf_op jit(solution)/shard_map/all_to_all | solution.py:19
  216.4 11.9 %all_to_all.58 = f32[16,8,128]{2,1,0:T(8,128)S(1)} all-to-all(f32[16,8,128]{2,1,0:T(8,128)S(1)} %convolution_bitcast_fusion.2), channel_id=1, replica_groups=mesh['zl'=4,'x'=4,'zh'=2,'y'=8,'core'=2] {'y','core'}, dimensions={0} | all-to-all | bytes 131072 | tf_op jit(solution)/shard_map/all_to_all | solution.py:19
  228.9 7.2 %all-to-all-start.9 = ((f32[32,8,128]{2,1,0:T(8,128)}), f32[32,8,128]{2,1,0:T(8,128)S(1)}, u32[]{:S(2)}, u32[]{:S(2)}) async-start(f32[32,8,128]{2,1,0:T(8,128)} %broadcast_in_dim.66), calls=%async_computation.9 | async-start | bytes 262144 | tf_op jit(solution)/shard_map/all_to_all | solution.py:19
  237.5 7.8 %all-to-all-done.9 = f32[32,8,128]{2,1,0:T(8,128)S(1)} async-done(((f32[32,8,128]{2,1,0:T(8,128)}), f32[32,8,128]{2,1,0:T(8,128)S(1)}, u32[]{:S(2)}, u32[]{:S(2)}) %all-to-all-start.9) | async-done | bytes 131104 | tf_op jit(solution)/shard_map/all_to_all | solution.py:19
  245.4 14.6 %all_to_all.59 = f32[16,24,128]{2,1,0:T(8,128)S(1)} all-to-all(f32[16,24,128]{2,1,0:T(8,128)S(1)} %broadcast_in_dim.67), channel_id=1, replica_groups=mesh['zl'=4,'x'=4,'zh'=2,'y'=8,'core'=2] {'y','core'}, dimensions={0} | all-to-all | bytes 393216 | tf_op jit(solution)/shard_map/all_to_all | solution.py:19
  261.3 6.0 %normalise.3 = (f32[256,128]{1,0:T(8,128)}, f32[128,128]{1,0:T(8,128)}) custom-call(f32[128,128]{1,0:T(8,128)} %slice_bitcast_fusion.1.gram_ref, f32[256,128]{1,0:T(8,128)} %bitcast_select_fusion.wide_ref), custom_call_target="tpu_custom_call" | custom-call | tf_op jit(solution)/shard_map/normalise/pallas_call | solution.py:139
  (92 shorter events, 32.2 us)
Async XLA Ops:
  6.5 12.5 %copy-start.2 = (bf16[256,128]{1,0:T(8,128)(2,1)S(1)}, bf16[256,128]{1,0:T(8,128)(2,1)}, u32[]{:S(2)}) copy-start(bf16[256,128]{1,0:T(8,128)(2,1)} %param.7) | copy-start | bytes 196612
  6.5 28.3 %copy-start.6 = (s32[1,1,1,16]{3,2,1,0:T(1,128)S(1)}, s32[1,1,1,16]{3,2,1,0:T(1,128)}, u32[]{:S(2)}) copy-start(s32[1,1,1,16]{3,2,1,0:T(1,128)} %param.6) | copy-start | bytes 196
  8.6 43.1 %all-to-all-start.1 = ((bf16[16,256,128]{2,1,0:T(8,128)(2,1)}), bf16[16,256,128]{2,1,0:T(8,128)(2,1)S(1)}, u32[]{:S(2)}, u32[]{:S(2)}) async-start(bf16[16,256,128]{2,1,0:T(8,128)(2,1)} %broadcast_in_dim.61), calls=%async_computation.1 | async-start | bytes 2097152 | tf_op jit(solution)/shard_map/all_to_all | solution.py:19
  19.0 16.5 %collective-permute-start.2 = (bf16[256,128]{1,0:T(8,128)(2,1)S(1)}, bf16[256,128]{1,0:T(8,128)(2,1)S(1)}, u32[]{:S(2)}, u32[]{:S(2)}) collective-permute-start(bf16[256,128]{1,0:T(8,128)(2,1)S(1)} %copy-done.2), channel_id=1, source_target_pairs={{0,24},{1,25},{32,56},{33,57},{64,88},{65,89},{96,120},{97,121},{1... | collective-permute-start | bytes 196616 | tf_op jit(solution)/shard_map/ppermute | solution.py:36
  32.2 3.3 %collective-permute-start = (bf16[256,128]{1,0:T(8,128)(2,1)S(1)}, bf16[256,128]{1,0:T(8,128)(2,1)S(1)}, u32[]{:S(2)}, u32[]{:S(2)}) collective-permute-start(bf16[256,128]{1,0:T(8,128)(2,1)S(1)} %copy-done.2), channel_id=1, source_target_pairs={{0,8},{1,9},{32,40},{33,41},{64,72},{65,73},{96,104},{97,105},{128... | collective-permute-start | bytes 196616 | tf_op jit(solution)/shard_map/ppermute | solution.py:36
  33.5 3.3 %collective-permute-start.1 = (bf16[256,128]{1,0:T(8,128)(2,1)S(1)}, bf16[256,128]{1,0:T(8,128)(2,1)S(1)}, u32[]{:S(2)}, u32[]{:S(2)}) collective-permute-start(bf16[256,128]{1,0:T(8,128)(2,1)S(1)} %copy-done.2), channel_id=1, source_target_pairs={{0,16},{1,17},{32,48},{33,49},{64,80},{65,81},{96,112},{97,113},{1... | collective-permute-start | bytes 196616 | tf_op jit(solution)/shard_map/ppermute | solution.py:36
  36.8 6.5 %collective-permute-start.5 = (bf16[256,128]{1,0:T(8,128)(2,1)S(1)}, bf16[256,128]{1,0:T(8,128)(2,1)S(1)}, u32[]{:S(2)}, u32[]{:S(2)}) collective-permute-start(bf16[256,128]{1,0:T(8,128)(2,1)S(1)} %add_select_fusion.1), channel_id=1, source_target_pairs={{0,4},{8,12},{1,5},{9,13},{16,20},{24,28},{17,21},{25,29},{32,36},... | collective-permute-start | bytes 196616 | tf_op jit(solution)/shard_map/ppermute | solution.py:38
  38.1 5.2 %collective-permute-start.3 = (bf16[256,128]{1,0:T(8,128)(2,1)S(1)}, bf16[256,128]{1,0:T(8,128)(2,1)S(1)}, u32[]{:S(2)}, u32[]{:S(2)}) collective-permute-start(bf16[256,128]{1,0:T(8,128)(2,1)S(1)} %add_select_fusion.1), channel_id=1, source_target_pairs={{0,2},{8,10},{1,3},{9,11},{16,18},{24,26},{17,19},{25,27},{32,34},... | collective-permute-start | bytes 196616 | tf_op jit(solution)/shard_map/ppermute | solution.py:38
  39.4 3.9 %collective-permute-start.4 = (bf16[256,128]{1,0:T(8,128)(2,1)S(1)}, bf16[256,128]{1,0:T(8,128)(2,1)S(1)}, u32[]{:S(2)}, u32[]{:S(2)}) collective-permute-start(bf16[256,128]{1,0:T(8,128)(2,1)S(1)} %add_select_fusion.1), channel_id=1, source_target_pairs={{0,14},{8,6},{1,15},{9,7},{16,30},{24,22},{17,31},{25,23},{32,46},... | collective-permute-start | bytes 196616 | tf_op jit(solution)/shard_map/ppermute | solution.py:38
  43.4 3.6 %collective-permute-start.6 = (bf16[256,128]{1,0:T(8,128)(2,1)S(1)}, bf16[256,128]{1,0:T(8,128)(2,1)S(1)}, u32[]{:S(2)}, u32[]{:S(2)}) collective-permute-start(bf16[256,128]{1,0:T(8,128)(2,1)S(1)} %add_select_fusion), channel_id=1, source_target_pairs={{0,1},{2,3},{4,5},{6,7},{8,9},{10,11},{12,13},{14,15},{16,17},{18,... | collective-permute-start | bytes 196616 | tf_op jit(solution)/shard_map/ppermute | solution.py:40
  47.7 12.7 %copy-start.7 = (s32[1,1,1,16]{3,2,1,0:T(1,128)S(1)}, s32[1,1,1,16]{3,2,1,0:T(1,128)}, u32[]{:S(2)}) copy-start(s32[1,1,1,16]{3,2,1,0:T(1,128)} %param.6) | copy-start | bytes 196
  51.7 10.4 %copy-start = (bf16[1,1,16,256,256]{4,3,2,1,0:T(8,128)(2,1)S(1)}, bf16[1,1,16,256,256]{4,3,2,1,0:T(8,128)(2,1)}, u32[]{:S(2)}) copy-start(bf16[1,1,16,256,256]{4,3,2,1,0:T(8,128)(2,1)} %param.5) | copy-start | bytes 6291460
  51.7 45.3 %all-to-all-start = ((bf16[16,256,128]{2,1,0:T(8,128)(2,1)}), bf16[16,256,128]{2,1,0:T(8,128)(2,1)}, u32[]{:S(2)}, u32[]{:S(2)}) async-start(bf16[16,256,128]{2,1,0:T(8,128)(2,1)} %column_products.2), calls=%async_computation | async-start | bytes 2097152 | tf_op jit(solution)/shard_map/all_to_all | solution.py:19
  60.3 119.2 %all-gather.2.cloned.1.call-start = ((), (), s32[]{:S(2)}) async-start(), calls=%async_computation.11 | async-start | bytes 2228224 | tf_op jit(solution)/shard_map/all_gather | solution.py:182
  62.1 2.0 copy-start.3
  64.4 4.7 %collective-permute-start.7 = (f32[128,128]{1,0:T(8,128)S(1)}, f32[128,128]{1,0:T(8,128)S(1)}, u32[]{:S(2)}, u32[]{:S(2)}) collective-permute-start(f32[128,128]{1,0:T(8,128)S(1)} %constant_dynamic-slice_fusion), channel_id=1, source_target_pairs={{0,1},{1,0},{2,3},{3,2},{4,5},{5,4},{6,7},{7,6},{8,9},{9,8},{10,11... | collective-permute-start | bytes 196616 | tf_op jit(solution)/shard_map/ppermute | solution.py:49
  69.1 6.3 %collective-permute-start.10 = (f32[128,128]{1,0:T(8,128)S(1)}, f32[128,128]{1,0:T(8,128)S(1)}, u32[]{:S(2)}, u32[]{:S(2)}) collective-permute-start(f32[128,128]{1,0:T(8,128)S(1)} %dynamic-slice_add_fusion), channel_id=1, source_target_pairs={{4,0},{12,8},{5,1},{13,9},{20,16},{28,24},{21,17},{29,25},{36,32},... | collective-permute-start | bytes 196616 | tf_op jit(solution)/shard_map/ppermute | solution.py:50
  70.4 7.0 %collective-permute-start.8 = (f32[128,128]{1,0:T(8,128)S(1)}, f32[128,128]{1,0:T(8,128)S(1)}, u32[]{:S(2)}, u32[]{:S(2)}) collective-permute-start(f32[128,128]{1,0:T(8,128)S(1)} %dynamic-slice_add_fusion), channel_id=1, source_target_pairs={{2,0},{10,8},{3,1},{11,9},{18,16},{26,24},{19,17},{27,25},{34,32},... | collective-permute-start | bytes 196616 | tf_op jit(solution)/shard_map/ppermute | solution.py:50
  71.7 6.4 %collective-permute-start.9 = (f32[128,128]{1,0:T(8,128)S(1)}, f32[128,128]{1,0:T(8,128)S(1)}, u32[]{:S(2)}, u32[]{:S(2)}) collective-permute-start(f32[128,128]{1,0:T(8,128)S(1)} %dynamic-slice_add_fusion), channel_id=1, source_target_pairs={{14,0},{6,8},{15,1},{7,9},{30,16},{22,24},{31,17},{23,25},{46,32},... | collective-permute-start | bytes 196616 | tf_op jit(solution)/shard_map/ppermute | solution.py:50
  78.1 14.6 %collective-permute-start.13 = (f32[128,128]{1,0:T(8,128)S(1)}, f32[128,128]{1,0:T(8,128)S(1)}, u32[]{:S(2)}, u32[]{:S(2)}) collective-permute-start(f32[128,128]{1,0:T(8,128)S(1)} %add_add_fusion.1), channel_id=1, source_target_pairs={{24,0},{25,1},{56,32},{57,33},{88,64},{89,65},{120,96},{121,97},{1... | collective-permute-start | bytes 196616 | tf_op jit(solution)/shard_map/ppermute | solution.py:51
  79.4 13.3 %collective-permute-start.11 = (f32[128,128]{1,0:T(8,128)S(1)}, f32[128,128]{1,0:T(8,128)S(1)}, u32[]{:S(2)}, u32[]{:S(2)}) collective-permute-start(f32[128,128]{1,0:T(8,128)S(1)} %add_add_fusion.1), channel_id=1, source_target_pairs={{8,0},{9,1},{40,32},{41,33},{72,64},{73,65},{104,96},{105,97},{136... | collective-permute-start | bytes 196616 | tf_op jit(solution)/shard_map/ppermute | solution.py:51
  80.7 12.0 %collective-permute-start.12 = (f32[128,128]{1,0:T(8,128)S(1)}, f32[128,128]{1,0:T(8,128)S(1)}, u32[]{:S(2)}, u32[]{:S(2)}) collective-permute-start(f32[128,128]{1,0:T(8,128)S(1)} %add_add_fusion.1), channel_id=1, source_target_pairs={{16,0},{17,1},{48,32},{49,33},{80,64},{81,65},{112,96},{113,97},{1... | collective-permute-start | bytes 196616 | tf_op jit(solution)/shard_map/ppermute | solution.py:51
  92.8 5.6 %collective-permute-start.14 = (f32[128,128]{1,0:T(8,128)S(1)}, f32[128,128]{1,0:T(8,128)S(1)}, u32[]{:S(2)}, u32[]{:S(2)}) collective-permute-start(f32[128,128]{1,0:T(8,128)S(1)} %add_add_fusion), channel_id=1, source_target_pairs={{1,0},{3,2},{5,4},{7,6},{9,8},{11,10},{13,12},{15,14},{17,16},{19,... | collective-permute-start | bytes 196616 | tf_op jit(solution)/shard_map/ppermute | solution.py:52
  113.0 18.2 %all-to-all-start.3 = ((f32[32,8,128]{2,1,0:T(8,128)}), f32[32,8,128]{2,1,0:T(8,128)S(1)}, u32[]{:S(2)}, u32[]{:S(2)}) async-start(f32[32,8,128]{2,1,0:T(8,128)} %broadcast_in_dim.63), calls=%async_computation.3 | async-start | bytes 262144 | tf_op jit(solution)/shard_map/all_to_all | solution.py:19
  120.1 7.8 %collective-permute-start.15 = (f32[16,128]{1,0:T(8,128)S(1)}, f32[16,128]{1,0:T(8,128)S(1)}, u32[]{:S(2)}, u32[]{:S(2)}) collective-permute-start(f32[16,128]{1,0:T(8,128)S(1)} %slice_bitcast_fusion.3), channel_id=1, source_target_pairs={{0,16},{1,17},{2,18},{3,19},{4,20},{5,21},{6,22},{7,23},{8,24},{9,... | collective-permute-start | bytes 24584 | tf_op jit(solution)/shard_map/ppermute | solution.py:187
  179.5 10.9 %all-to-all-start.6 = ((bf16[4,256,128]{2,1,0:T(8,128)(2,1)}), bf16[4,256,128]{2,1,0:T(8,128)(2,1)S(1)}, u32[]{:S(2)}, u32[]{:S(2)}) async-start(bf16[4,256,128]{2,1,0:T(8,128)(2,1)} %reduce_sum.80), calls=%async_computation.6 | async-start | bytes 524288 | tf_op jit(solution)/shard_map/all_to_all | solution.py:19
  183.1 5.2 %copy-start.1 = (bf16[1,1,16,256,256]{4,3,2,1,0:T(8,128)(2,1)S(1)}, bf16[1,1,16,256,256]{4,3,2,1,0:T(8,128)(2,1)}, u32[]{:S(2)}) copy-start(bf16[1,1,16,256,256]{4,3,2,1,0:T(8,128)(2,1)} %param.5) | copy-start | bytes 6291460
  188.3 2.1 copy-start.4
  188.3 2.1 copy-start.5
  191.4 24.5 %all-to-all-start.7 = ((f32[32,8,128]{2,1,0:T(8,128)}), f32[32,8,128]{2,1,0:T(8,128)S(1)}, u32[]{:S(2)}, u32[]{:S(2)}) async-start(f32[32,8,128]{2,1,0:T(8,128)} %fusion.1), calls=%async_computation.7 | async-start | bytes 262144 | tf_op jit(solution)/shard_map/all_to_all | solution.py:19
  228.9 16.4 %all-to-all-start.9 = ((f32[32,8,128]{2,1,0:T(8,128)}), f32[32,8,128]{2,1,0:T(8,128)S(1)}, u32[]{:S(2)}, u32[]{:S(2)}) async-start(f32[32,8,128]{2,1,0:T(8,128)} %broadcast_in_dim.66), calls=%async_computation.9 | async-start | bytes 262144 | tf_op jit(solution)/shard_map/all_to_all | solution.py:19
  236.2 9.2 %collective-permute-start.16 = (f32[8,128]{1,0:T(8,128)S(1)}, f32[8,128]{1,0:T(8,128)S(1)}, u32[]{:S(2)}, u32[]{:S(2)}) collective-permute-start(f32[8,128]{1,0:T(8,128)S(1)} %reduce_sum.83), channel_id=1, source_target_pairs={{16,0},{17,1},{18,2},{19,3},{20,4},{21,5},{22,6},{23,7},{24,8},{25... | collective-permute-start | bytes 12296 | tf_op jit(solution)/shard_map/ppermute | solution.py:212
Sparse Core Ops, SparseCore 0:
  99.2 70.2 all-gather.1

commit v4 on v3

--- a/solution.py
+++ b/solution.py
@@ -41,14 +41,19 @@
     return jnp.where(core == 0, block, other)
 
 
-def to_first_column(value):
+def over_cores(value):
     half = value.shape[0] // 2
     core = lax.axis_index("core")
     given = lax.dynamic_slice_in_dim(value, (1 - core) * half, half)
     value = lax.dynamic_slice_in_dim(value, core * half, half)
-    value = value + lax.ppermute(given, "core", [(0, 1), (1, 0)])
+    return value + lax.ppermute(given, "core", [(0, 1), (1, 0)])
+
+
+def to_first_column(value):
     value = value + sum(lax.ppermute(value, "y", backward(pairs)) for pairs in NEAR)
-    value = value + sum(lax.ppermute(value, ("zh", "y"), backward(pairs)) for pairs in FAR)
+    sent = value.astype(jnp.bfloat16)
+    far = [lax.ppermute(sent, ("zh", "y"), backward(pairs)) for pairs in FAR]
+    value = value + sum(part.astype(jnp.float32) for part in far)
     return jnp.concatenate([value, lax.ppermute(value, "core", [(1, 0)])], axis=0)
 
 
@@ -57,18 +62,13 @@
 
 
 def column_kernel(by_x, slots_ref, place_ref, tiles_ref, band_ref, out_ref):
-    band = band_ref[...]
-
-    def one(t, carry):
+    band = band_ref[...].astype(jnp.float32).T.astype(jnp.bfloat16)
+    for t in range(tiles_ref.shape[0]):
         slot = slots_ref[t]
-        product = lax.dot_general(
-            tiles_ref[t], band, (((0,), (0,)), ((), ())), preferred_element_type=jnp.float32
-        )
+        product = jnp.dot(band, tiles_ref[t], preferred_element_type=jnp.float32)
+        product = jnp.where(slot > place_ref[0], product, 0.0).astype(jnp.bfloat16)
         where = lax.rem(slot, 4) * 4 + lax.div(slot, 4) if by_x else slot
-        out_ref[where] = jnp.where(slot > place_ref[0], product, 0.0).astype(jnp.bfloat16)
-        return carry
-
-    lax.fori_loop(0, tiles_ref.shape[0], one, 0, unroll=4)
+        out_ref[where] = product.T
 
 
 def column_products(tiles, slots, place, band_block, by_x):
@@ -79,6 +79,7 @@
         out_shape=jax.ShapeDtypeStruct(shape, jnp.bfloat16),
         in_specs=[SMEM, SMEM, VMEM, VMEM],
         out_specs=VMEM,
+        compiler_params=pltpu.CompilerParams(vmem_limit_bytes=1 << 24),
         cost_estimate=pl.CostEstimate(
             flops=2 * count * tile * tile * shape[2], bytes_accessed=1 << 23, transcendentals=0
         ),
@@ -86,9 +87,16 @@
     )(slots, place, tiles, band_block)
 
 
-def normalise_kernel(gram_ref, wide_ref, out_ref, inverse_ref, work):
-    size = gram_ref.shape[0]
-    work[:, :size] = gram_ref[...]
+def normalise_kernel(both_ref, *refs):
+    size = both_ref.shape[2]
+    if len(refs) == 3:
+        out_ref, inverse_ref, work = refs
+        wide = both_ref[:, 8:].reshape(2 * size, size)
+    else:
+        first_ref, rest_ref, out_ref, work = refs
+        halves = [both_ref[:, low : low + 8].reshape(size, size) for low in (8, 16)]
+        wide = jnp.where(first_ref[0] == 0, jnp.concatenate(halves, axis=0), rest_ref[...])
+    work[:, :size] = both_ref[:, :8].reshape(size, size)
     down = lax.broadcasted_iota(jnp.int32, (size, size), 0)
     across = lax.broadcasted_iota(jnp.int32, (size, size), 1)
     work[:, size:] = (down == across).astype(jnp.float32)
@@ -103,7 +111,6 @@
         for k in range(PANEL):
             pivot = jnp.broadcast_to(lanes[k][k : k + 1], (PANEL, size))
             scale = lax.rsqrt(pivot)
-            scale = scale * (1.5 - 0.5 * pivot * scale * scale)
             below = jnp.where(rows > k, lanes[k] * scale, 0.0)
             for j in range(k + 1, PANEL):
                 lanes[j] = lanes[j] - below * jnp.broadcast_to(below[j : j + 1], (PANEL, size))
@@ -124,35 +131,73 @@
             )
             work[after:, :] = work[after:, :] - update[after:, :]
     out = lax.dot_general(
-        wide_ref[...],
+        wide,
         work[:, size:],
         (((1,), (1,)), ((), ())),
         precision=HIGHEST,
         preferred_element_type=jnp.float32,
     )
     out_ref[...] = out.astype(out_ref.dtype)
-    inverse_ref[...] = work[:, size:]
-
-
-def normalise(gram, wide, dtype):
-    size = gram.shape[0]
+    if len(refs) == 3:
+        inverse_ref[...] = work[:, size:]
+
+
+def normalise(both, *own):
+    size = both.shape[2]
+    block = jax.ShapeDtypeStruct((2 * size, size), jnp.float32 if own else jnp.bfloat16)
+    square = jax.ShapeDtypeStruct((size, size), jnp.float32)
     return pl.pallas_call(
         normalise_kernel,
-        out_shape=(
-            jax.ShapeDtypeStruct(wide.shape, dtype),
-            jax.ShapeDtypeStruct(gram.shape, jnp.float32),
+        out_shape=block if own else (block, square),
+        in_specs=[VMEM, SMEM, VMEM] if own else [VMEM],
+        out_specs=VMEM if own else (VMEM, VMEM),
+        scratch_shapes=[pltpu.VMEM((size, 2 * size), jnp.float32)],
+        compiler_params=pltpu.CompilerParams(vmem_limit_bytes=1 << 24),
+        name="normalise",
+    )(both, *own)
+
+
+def row_kernel(slots_ref, place_ref, tiles_ref, blocks_ref, correction_ref, band_ref, *rest):
+    weight_ref, out_ref = rest if len(rest) == 2 else (None, rest[0])
+    width = out_ref.shape[1]
+    out = jnp.dot(correction_ref[...], band_ref[...], preferred_element_type=jnp.float32)
+    for t in range(tiles_ref.shape[0]):
+        slot = slots_ref[t]
+        block = blocks_ref[slot]
+        if weight_ref is not None:
+            high = block.astype(jnp.bfloat16)
+            low = (block - high.astype(jnp.float32)).astype(jnp.bfloat16)
+            block = jnp.dot(
+                jnp.concatenate([high, low], axis=1),
+                weight_ref[...],
+                preferred_element_type=jnp.float32,
+            )
+            block = block[:, :width] + block[:, width:]
+        block = jnp.where(slot >= place_ref[0], block, 0.0).astype(jnp.bfloat16)
+        out = out + jnp.dot(tiles_ref[t], block, preferred_element_type=jnp.float32)
+    out_ref[...] = out
+
+
+def row_products(tiles, slots, place, blocks, correction, band_block, *weight):
+    count, tile = tiles.shape[:2]
+    width = band_block.shape[1]
+    return pl.pallas_call(
+        row_kernel,
+        out_shape=jax.ShapeDtypeStruct((tile, width), jnp.float32),
+        in_specs=[SMEM, SMEM] + [VMEM] * (4 + len(weight)),
+        out_specs=VMEM,
+        compiler_params=pltpu.CompilerParams(vmem_limit_bytes=1 << 24),
+        cost_estimate=pl.CostEstimate(
+            flops=2 * count * tile * tile * width, bytes_accessed=1 << 23, transcendentals=0
         ),
-        in_specs=[pl.BlockSpec(memory_space=pltpu.VMEM)] * 2,
-        out_specs=[pl.BlockSpec(memory_space=pltpu.VMEM)] * 2,
-        scratch_shapes=[pltpu.VMEM((size, 2 * size), jnp.float32)],
-        name="normalise",
-    )(gram, wide)
-
-
-def row_products(tiles, slots, place, blocks):
-    keep = (slots >= place).astype(jnp.bfloat16)
-    near = jnp.take(blocks, slots, axis=0) * keep[:, None, None]
-    return jnp.einsum("tab,tbn->an", tiles, near, preferred_element_type=jnp.float32)
+        name="row_products",
+    )(slots, place, tiles, blocks, correction, band_block, *weight)
+
+
+def weight_of(factor):
+    high = factor.T.astype(jnp.bfloat16)
+    low = (factor.T - high.astype(jnp.float32)).astype(jnp.bfloat16)
+    return jnp.block([[high, low], [high, jnp.zeros_like(high)]])
 
 
 def total(received):
@@ -174,9 +219,8 @@
     blocks = swap(copies, ROW)
     band_block = from_first_column(sketch)
     received = swap(column_products(tiles, slots, place, band_block, False), ROW)
-    row_part = row_products(tiles, slots, place, blocks)
-    row_part = row_part + jnp.dot(correction, sketch, preferred_element_type=jnp.float32)
-    band = to_first_column(row_part)
+    row_part = row_products(tiles, slots, place, blocks, correction, sketch)
+    band = to_first_column(over_cores(row_part))
     own = total(received) + jnp.where(first_col, band, 0.0)
 
     blocks = lax.all_gather(own, ROW, axis=0)
@@ -188,19 +232,15 @@
     lines = jnp.where(lax.axis_index("zh") == 0, lines, other)
     piece = total(swap(copies_of(total(both[:, :8]), 32), ACROSS))
     both = swap(copies_of(jnp.concatenate([piece, lines], axis=0), 16), PLANE)
-    gram = both[:, :8].reshape(128, 128)
-    band = both[:, 8:].reshape(256, 128)
-    band_block, factor = normalise(gram, band, jnp.bfloat16)
+    band_block, factor = normalise(both)
 
     placed = column_products(tiles, slots, place, band_block, True)
     received = total(swap(placed.reshape(4, 4, 256, 128), "x")).astype(jnp.bfloat16)
     received, blocks = lax.optimization_barrier((received, blocks))
     received = swap(received, "zl")
-    blocks = lax.dot_general(
-        blocks, factor, (((2,), (1,)), ((), ())), precision=HIGHEST
-    ).astype(jnp.bfloat16)
-    row_part = row_products(tiles, slots, place, blocks)
-    row_part = row_part + jnp.dot(correction, band_block, preferred_element_type=jnp.float32)
+    row_part = row_products(
+        tiles, slots, place, blocks, correction, band_block, weight_of(factor)
+    )
     col_sum = total(received)
     row_part = row_part + jnp.where(first_col, col_sum, 0.0)
     rest = jnp.where(first_col, 0.0, col_sum)
@@ -212,10 +252,7 @@
     other = lax.ppermute(band_rows, "zh", [(1, 0)])
     both = jnp.concatenate([piece, band_rows, other], axis=0)
     both = swap(copies_of(both, 16), PLANE)
-    gram = both[:, :8].reshape(128, 128)
-    band = both[:, 8:].reshape(16, 2, 8, 128).swapaxes(0, 1).reshape(256, 128)
-    own = jnp.where(first_col, band, rest)
-    return normalise(gram, own, jnp.float32)[0]
+    return normalise(both, col_id[None], rest)
 
 
 def solution(mesh):

time: 275 us -> 266 us (0.967)
  blocking collectives: 75.3 us -> 106 us
  starting transfers between devices: 93.5 us -> 79.9 us
  matrix products: 9.64 us -> 0.89 us
  waiting for transfers between devices: 42.9 us -> 35.2 us
  Pallas kernels: 19.9 us -> 14.1 us
  local copies, waits for them, and re-layouts: 10.4 us -> 6.35 us
    all_to_all x5 -> x6, blocking collectives: 75.3 us -> 106 us  [swap(): return lax.all_to_all(value, axes, 0, 0, tiled=True)]
    all_to_all x6 -> x5, starting transfers between devices: 48.4 us -> 36 us  [swap(): return lax.all_to_all(value, axes, 0, 0, tiled=True)]
    all_to_all x6 -> x5, waiting for transfers between devices: 24.1 us -> 12.9 us  [swap(): return lax.all_to_all(value, axes, 0, 0, tiled=True)]
    dot_general x5 -> x0, matrix products: 8.76 us -> none  [the longest x2 4.06 us: row_products(): jnp.einsum('tab,tbn->an', tiles, near, preferred_element_type=jnp.float32)]
    pallas_call x2, Pallas kernels: 7.99 us -> 2.26 us  [column_products(): pl.pallas_call(functools.partial(column_kernel, by_x), out_shape=jax.Shap...]
    gather x2 -> x0, local copies, waits for them, and re-layouts: 3.32 us -> none  [row_products(): near = jnp.take(blocks, slots, axis=0) * keep[:, None, None]]
    ppermute x1, waiting for transfers between devices: 0.01 us -> 2.82 us  [from_first_column(): other = lax.ppermute(block, 'core', [(0, 1)])]
    pallas_call x2 -> x4, Pallas kernels: 11.9 us -> 11.9 us  [the longest x2 8.55 us: normalise(): pl.pallas_call(normalise_kernel, out_shape=block if own else (block, squa...]
  transfers between devices with their start and end apart: 24 -> 23, of which waited for: 10 -> 14; matrix products, arithmetic and copies ran while one was open for 7% -> 2% of each run, Pallas kernels for 5% -> 4%
where the time goes in v4:
time: 266 us; the launch traced here: 264 us
  blocking collectives  106 us (40%)
  starting transfers between devices  79.9 us (30%)
  waiting for transfers between devices  35.2 us (13%)
  between operations  16.4 us (6%)
  Pallas kernels  14.1 us (5%)
  local copies, waits for them, and re-layouts  6.35 us (2%)
  other arithmetic  6.03 us (2%)
    all_to_all x6, blocking collectives, swap(): return lax.all_to_all(value, axes, 0, 0, tiled=True)  106 us
    all_to_all x5, starting transfers between devices, swap(): return lax.all_to_all(value, axes, 0, 0, tiled=True)  36 us
    ppermute x3, starting transfers between devices, from_first_column(): far = sum((lax.ppermute(block, ('zh', 'y'), pairs) for pairs in FAR))  15.8 us
    all_to_all x5, waiting for transfers between devices, swap(): return lax.all_to_all(value, axes, 0, 0, tiled=True)  12.9 us
    ppermute x3, waiting for transfers between devices, to_first_column(): far = [lax.ppermute(sent, ('zh', 'y'), backward(pairs)) for pairs in FAR]  9.57 us
    pallas_call x2, Pallas kernels, normalise(): pl.pallas_call(normalise_kernel, out_shape=block if own else (block, squa...  8.55 us
    ppermute x1, starting transfers between devices, local(): other = lax.ppermute(lines, 'zh', [(0, 1)])  7.04 us
  transfers between devices with their start and end apart: 23, of which 14 were waited for; matrix products, arithmetic and copies ran while one was open for 2% of the time, Pallas kernels for 4%

profile of v4, /device:TPU:1, one launch (start us, length us, event | category | flops | bytes accessed | tf_op | source)
XLA Modules:
  0.0 264.5 jit_solution(11968982368090008222)
XLA Ops:
  6.5 2.2 broadcast_in_dim.54
  8.8 10.4 %all-to-all-start.1 = ((bf16[16,256,128]{2,1,0:T(8,128)(2,1)}), bf16[16,256,128]{2,1,0:T(8,128)(2,1)S(1)}, u32[]{:S(2)}, u32[]{:S(2)}) async-start(bf16[16,256,128]{2,1,0:T(8,128)(2,1)} %broadcast_in_dim.54), calls=%async_computation.1 | async-start | bytes 2097152 | tf_op jit(solution)/shard_map/all_to_all | solution.py:19
  19.2 13.2 %collective-permute-start.2 = (bf16[256,128]{1,0:T(8,128)(2,1)S(1)}, bf16[256,128]{1,0:T(8,128)(2,1)S(1)}, u32[]{:S(2)}, u32[]{:S(2)}) collective-permute-start(bf16[256,128]{1,0:T(8,128)(2,1)S(1)} %copy-done.3), channel_id=1, source_target_pairs={{0,24},{1,25},{32,56},{33,57},{64,88},{65,89},{96,120},{97,121},{1... | collective-permute-start | bytes 196616 | tf_op jit(solution)/shard_map/ppermute | solution.py:36
  32.4 1.3 collective-permute-start
  33.7 1.3 collective-permute-start.1
  35.4 1.5 collective-permute-done.1
  43.5 2.8 %collective-permute-done.6 = bf16[256,128]{1,0:T(8,128)(2,1)S(1)} collective-permute-done((bf16[256,128]{1,0:T(8,128)(2,1)S(1)}, bf16[256,128]{1,0:T(8,128)(2,1)S(1)}, u32[]{:S(2)}, u32[]{:S(2)}) %collective-permute-start.6) | collective-permute-done | bytes 65568 | tf_op jit(solution)/shard_map/ppermute | solution.py:40
  48.5 8.5 %all-to-all-start = ((bf16[16,256,128]{2,1,0:T(8,128)(2,1)}), bf16[16,256,128]{2,1,0:T(8,128)(2,1)}, u32[]{:S(2)}, u32[]{:S(2)}) async-start(bf16[16,256,128]{2,1,0:T(8,128)(2,1)} %copy-done.1), calls=%async_computation | async-start | bytes 2097152 | tf_op jit(solution)/shard_map/all_to_all | solution.py:19
  62.5 2.3 collective-permute-start.7
  69.7 2.4 collective-permute-done.10
  72.1 1.8 collective-permute-done.8
  78.5 9.6 %collective-permute-done.13 = bf16[128,128]{1,0:T(8,128)(2,1)S(1)} collective-permute-done((bf16[128,128]{1,0:T(8,128)(2,1)S(1)}, bf16[128,128]{1,0:T(8,128)(2,1)S(1)}, u32[]{:S(2)}, u32[]{:S(2)}) %collective-permute-start.13) | collective-permute-done | bytes 32800 | tf_op jit(solution)/shard_map/ppermute | solution.py:55
  88.1 4.5 %collective-permute-start.14 = (f32[128,128]{1,0:T(8,128)S(1)}, f32[128,128]{1,0:T(8,128)S(1)}, u32[]{:S(2)}, u32[]{:S(2)}) collective-permute-start(f32[128,128]{1,0:T(8,128)S(1)} %add_add_fusion), channel_id=1, source_target_pairs={{1,0},{3,2},{5,4},{7,6},{9,8},{11,10},{13,12},{15,14},{17,16},{19,... | collective-permute-start | bytes 196616 | tf_op jit(solution)/shard_map/ppermute | solution.py:57
  92.6 1.4 convert_reduce_fusion
  95.1 12.8 %all_to_all.55 = f32[16,24,128]{2,1,0:T(8,128)S(1)} all-to-all(f32[16,24,128]{2,1,0:T(8,128)S(1)} %pad_maximum_fusion), channel_id=1, replica_groups=mesh['zl'=4,'x'=4,'zh'=2,'y'=8,'core'=2] {'y','core'}, dimensions={0} | all-to-all | bytes 393216 | tf_op jit(solution)/shard_map/all_to_all | solution.py:19
  108.6 7.5 %all-to-all-start.3 = ((f32[32,8,128]{2,1,0:T(8,128)}), f32[32,8,128]{2,1,0:T(8,128)S(1)}, u32[]{:S(2)}, u32[]{:S(2)}) async-start(f32[32,8,128]{2,1,0:T(8,128)} %broadcast_in_dim.56), calls=%async_computation.3 | async-start | bytes 262144 | tf_op jit(solution)/shard_map/all_to_all | solution.py:19
  116.1 7.0 %collective-permute-start.15 = (f32[16,128]{1,0:T(8,128)S(1)}, f32[16,128]{1,0:T(8,128)S(1)}, u32[]{:S(2)}, u32[]{:S(2)}) collective-permute-start(f32[16,128]{1,0:T(8,128)S(1)} %slice_bitcast_fusion), channel_id=1, source_target_pairs={{0,16},{1,17},{2,18},{3,19},{4,20},{5,21},{6,22},{7,23},{8,24},{9,... | collective-permute-start | bytes 24584 | tf_op jit(solution)/shard_map/ppermute | solution.py:231
  123.9 3.3 %all-to-all-done.3 = f32[32,8,128]{2,1,0:T(8,128)S(1)} async-done(((f32[32,8,128]{2,1,0:T(8,128)}), f32[32,8,128]{2,1,0:T(8,128)S(1)}, u32[]{:S(2)}, u32[]{:S(2)}) %all-to-all-start.3) | async-done | bytes 131104 | tf_op jit(solution)/shard_map/all_to_all | solution.py:19
  127.3 13.9 %all_to_all.56.both_ref = f32[16,24,128]{2,1,0:T(8,128)S(1)} all-to-all(f32[16,24,128]{2,1,0:T(8,128)S(1)} %broadcast_in_dim.57), channel_id=1, replica_groups=mesh['zl'=4,'x'=4,'zh'=2,'y'=8,'core'=2] {'y','core'}, dimensions={0} | all-to-all | bytes 393216 | tf_op jit(solution)/shard_map/all_to_all | solution.py:19
  141.1 3.9 %normalise.2 = (bf16[256,128]{1,0:T(8,128)(2,1)S(1)}, f32[128,128]{1,0:T(8,128)S(1)}) custom-call(f32[16,24,128]{2,1,0:T(8,128)S(1)} %all_to_all.56.both_ref), custom_call_target="tpu_custom_call" | custom-call | tf_op jit(solution)/shard_map/normalise/pallas_call | solution.py:149
  146.2 23.2 %all_to_all.57 = bf16[4,4,256,128]{3,2,1,0:T(8,128)(2,1)} all-to-all(bf16[4,4,256,128]{3,2,1,0:T(8,128)(2,1)S(1)} %bitcast.39), channel_id=1, replica_groups=mesh['zl'=4,'x'=4,'zh'=2,'y'=8,'core'=2] {'x'}, dimensions={0} | all-to-all | bytes 2097152 | tf_op jit(solution)/shard_map/all_to_all | solution.py:19
  169.5 2.1 reduce_sum.80
  171.6 3.4 %all-to-all-start.6 = ((bf16[4,256,128]{2,1,0:T(8,128)(2,1)}), bf16[4,256,128]{2,1,0:T(8,128)(2,1)S(1)}, u32[]{:S(2)}, u32[]{:S(2)}) async-start(bf16[4,256,128]{2,1,0:T(8,128)(2,1)} %reduce_sum.80), calls=%async_computation.6 | async-start | bytes 524288 | tf_op jit(solution)/shard_map/all_to_all | solution.py:19
  175.2 1.6 copy-done.2
  176.8 2.0 row_products.3
  178.8 1.8 all-to-all-done.6
  180.7 29.2 %all_to_all.58 = f32[32,8,128]{2,1,0:T(8,128)S(1)} all-to-all(f32[32,8,128]{2,1,0:T(8,128)S(1)} %get-tuple-element.24), channel_id=1, replica_groups=mesh['zl'=4,'x'=4,'zh'=2,'y'=8,'core'=2] {'zh','y','core'}, dimensions={0} | all-to-all | bytes 262144 | tf_op jit(solution)/shard_map/all_to_all | solution.py:19
  210.4 11.9 %all_to_all.59 = f32[16,8,128]{2,1,0:T(8,128)S(1)} all-to-all(f32[16,8,128]{2,1,0:T(8,128)S(1)} %convolution_bitcast_fusion), channel_id=1, replica_groups=mesh['zl'=4,'x'=4,'zh'=2,'y'=8,'core'=2] {'y','core'}, dimensions={0} | all-to-all | bytes 131072 | tf_op jit(solution)/shard_map/all_to_all | solution.py:19
  223.0 6.2 %all-to-all-start.9 = ((f32[32,8,128]{2,1,0:T(8,128)}), f32[32,8,128]{2,1,0:T(8,128)S(1)}, u32[]{:S(2)}, u32[]{:S(2)}) async-start(f32[32,8,128]{2,1,0:T(8,128)} %broadcast_in_dim.59), calls=%async_computation.9 | async-start | bytes 262144 | tf_op jit(solution)/shard_map/all_to_all | solution.py:19
  230.5 7.8 %all-to-all-done.9 = f32[32,8,128]{2,1,0:T(8,128)S(1)} async-done(((f32[32,8,128]{2,1,0:T(8,128)}), f32[32,8,128]{2,1,0:T(8,128)S(1)}, u32[]{:S(2)}, u32[]{:S(2)}) %all-to-all-start.9) | async-done | bytes 131104 | tf_op jit(solution)/shard_map/all_to_all | solution.py:19
  238.4 14.6 %all_to_all.60.both_ref = f32[16,24,128]{2,1,0:T(8,128)S(1)} all-to-all(f32[16,24,128]{2,1,0:T(8,128)S(1)} %broadcast_in_dim.60), channel_id=1, replica_groups=mesh['zl'=4,'x'=4,'zh'=2,'y'=8,'core'=2] {'y','core'}, dimensions={0} | all-to-all | bytes 393216 | tf_op jit(solution)/shard_map/all_to_all | solution.py:19
  253.0 4.6 %normalise.3 = f32[256,128]{1,0:T(8,128)} custom-call(f32[16,24,128]{2,1,0:T(8,128)S(1)} %all_to_all.60.both_ref, s32[1]{0:T(128)} %bitcast.15.refs_0_, f32[256,128]{1,0:T(8,128)S(1)} %get-tuple-element.23.refs_1_), custom_call_target="tpu_custom_call" | custom-call | tf_op jit(solution)/shard_map/normalise/pallas_call | solution.py:149
  (76 shorter events, 27.8 us)
Async XLA Ops:
  6.5 12.6 %copy-start.3 = (bf16[256,128]{1,0:T(8,128)(2,1)S(1)}, bf16[256,128]{1,0:T(8,128)(2,1)}, u32[]{:S(2)}) copy-start(bf16[256,128]{1,0:T(8,128)(2,1)} %band_ref) | copy-start | bytes 196612
  6.5 39.8 %copy-start.4 = (s32[1,1,1,16]{3,2,1,0:T(1,128)S(1)}, s32[1,1,1,16]{3,2,1,0:T(1,128)}, u32[]{:S(2)}) copy-start(s32[1,1,1,16]{3,2,1,0:T(1,128)} %param.4) | copy-start | bytes 196
  6.5 39.8 %copy-start = (bf16[1,1,16,256,256]{4,3,2,1,0:T(8,128)(2,1)S(1)}, bf16[1,1,16,256,256]{4,3,2,1,0:T(8,128)(2,1)}, u32[]{:S(2)}) copy-start(bf16[1,1,16,256,256]{4,3,2,1,0:T(8,128)(2,1)} %param.3) | copy-start | bytes 6291460
  8.8 39.7 %all-to-all-start.1 = ((bf16[16,256,128]{2,1,0:T(8,128)(2,1)}), bf16[16,256,128]{2,1,0:T(8,128)(2,1)S(1)}, u32[]{:S(2)}, u32[]{:S(2)}) async-start(bf16[16,256,128]{2,1,0:T(8,128)(2,1)} %broadcast_in_dim.54), calls=%async_computation.1 | async-start | bytes 2097152 | tf_op jit(solution)/shard_map/all_to_all | solution.py:19
  19.2 15.8 %collective-permute-start.2 = (bf16[256,128]{1,0:T(8,128)(2,1)S(1)}, bf16[256,128]{1,0:T(8,128)(2,1)S(1)}, u32[]{:S(2)}, u32[]{:S(2)}) collective-permute-start(bf16[256,128]{1,0:T(8,128)(2,1)S(1)} %copy-done.3), channel_id=1, source_target_pairs={{0,24},{1,25},{32,56},{33,57},{64,88},{65,89},{96,120},{97,121},{1... | collective-permute-start | bytes 196616 | tf_op jit(solution)/shard_map/ppermute | solution.py:36
  32.4 3.1 %collective-permute-start = (bf16[256,128]{1,0:T(8,128)(2,1)S(1)}, bf16[256,128]{1,0:T(8,128)(2,1)S(1)}, u32[]{:S(2)}, u32[]{:S(2)}) collective-permute-start(bf16[256,128]{1,0:T(8,128)(2,1)S(1)} %copy-done.3), channel_id=1, source_target_pairs={{0,8},{1,9},{32,40},{33,41},{64,72},{65,73},{96,104},{97,105},{128... | collective-permute-start | bytes 196616 | tf_op jit(solution)/shard_map/ppermute | solution.py:36
  33.7 3.3 %collective-permute-start.1 = (bf16[256,128]{1,0:T(8,128)(2,1)S(1)}, bf16[256,128]{1,0:T(8,128)(2,1)S(1)}, u32[]{:S(2)}, u32[]{:S(2)}) collective-permute-start(bf16[256,128]{1,0:T(8,128)(2,1)S(1)} %copy-done.3), channel_id=1, source_target_pairs={{0,16},{1,17},{32,48},{33,49},{64,80},{65,81},{96,112},{97,113},{1... | collective-permute-start | bytes 196616 | tf_op jit(solution)/shard_map/ppermute | solution.py:36
  37.0 3.9 %collective-permute-start.5 = (bf16[256,128]{1,0:T(8,128)(2,1)S(1)}, bf16[256,128]{1,0:T(8,128)(2,1)S(1)}, u32[]{:S(2)}, u32[]{:S(2)}) collective-permute-start(bf16[256,128]{1,0:T(8,128)(2,1)S(1)} %add_select_fusion.1), channel_id=1, source_target_pairs={{0,4},{8,12},{1,5},{9,13},{16,20},{24,28},{17,21},{25,29},{32,36},... | collective-permute-start | bytes 196616 | tf_op jit(solution)/shard_map/ppermute | solution.py:38
  38.3 2.8 %collective-permute-start.3 = (bf16[256,128]{1,0:T(8,128)(2,1)S(1)}, bf16[256,128]{1,0:T(8,128)(2,1)S(1)}, u32[]{:S(2)}, u32[]{:S(2)}) collective-permute-start(bf16[256,128]{1,0:T(8,128)(2,1)S(1)} %add_select_fusion.1), channel_id=1, source_target_pairs={{0,2},{8,10},{1,3},{9,11},{16,18},{24,26},{17,19},{25,27},{32,34},... | collective-permute-start | bytes 196616 | tf_op jit(solution)/shard_map/ppermute | solution.py:38
  39.6 2.6 collective-permute-start.4
  42.2 4.1 %collective-permute-start.6 = (bf16[256,128]{1,0:T(8,128)(2,1)S(1)}, bf16[256,128]{1,0:T(8,128)(2,1)S(1)}, u32[]{:S(2)}, u32[]{:S(2)}) collective-permute-start(bf16[256,128]{1,0:T(8,128)(2,1)S(1)} %add_select_fusion), channel_id=1, source_target_pairs={{0,1},{2,3},{4,5},{6,7},{8,9},{10,11},{12,13},{14,15},{16,17},{18,... | collective-permute-start | bytes 196616 | tf_op jit(solution)/shard_map/ppermute | solution.py:40
  47.5 1.0 copy-start.1
  48.5 44.1 %all-to-all-start = ((bf16[16,256,128]{2,1,0:T(8,128)(2,1)}), bf16[16,256,128]{2,1,0:T(8,128)(2,1)}, u32[]{:S(2)}, u32[]{:S(2)}) async-start(bf16[16,256,128]{2,1,0:T(8,128)(2,1)} %copy-done.1), calls=%async_computation | async-start | bytes 2097152 | tf_op jit(solution)/shard_map/all_to_all | solution.py:19
  57.1 114.6 %all-gather.2.cloned.1.call-start = ((), (), s32[]{:S(2)}) async-start(), calls=%async_computation.11 | async-start | bytes 2228224 | tf_op jit(solution)/shard_map/all_gather | solution.py:226
  62.5 3.2 %collective-permute-start.7 = (f32[128,128]{1,0:T(8,128)S(1)}, f32[128,128]{1,0:T(8,128)S(1)}, u32[]{:S(2)}, u32[]{:S(2)}) collective-permute-start(f32[128,128]{1,0:T(8,128)S(1)} %constant_dynamic-slice_fusion), channel_id=1, source_target_pairs={{0,1},{1,0},{2,3},{3,2},{4,5},{5,4},{6,7},{7,6},{8,9},{9,8},{10,11... | collective-permute-start | bytes 196616 | tf_op jit(solution)/shard_map/ppermute | solution.py:49
  65.8 6.3 %collective-permute-start.10 = (f32[128,128]{1,0:T(8,128)S(1)}, f32[128,128]{1,0:T(8,128)S(1)}, u32[]{:S(2)}, u32[]{:S(2)}) collective-permute-start(f32[128,128]{1,0:T(8,128)S(1)} %dynamic-slice_add_fusion), channel_id=1, source_target_pairs={{4,0},{12,8},{5,1},{13,9},{20,16},{28,24},{21,17},{29,25},{36,32},... | collective-permute-start | bytes 196616 | tf_op jit(solution)/shard_map/ppermute | solution.py:53
  67.1 6.9 %collective-permute-start.8 = (f32[128,128]{1,0:T(8,128)S(1)}, f32[128,128]{1,0:T(8,128)S(1)}, u32[]{:S(2)}, u32[]{:S(2)}) collective-permute-start(f32[128,128]{1,0:T(8,128)S(1)} %dynamic-slice_add_fusion), channel_id=1, source_target_pairs={{2,0},{10,8},{3,1},{11,9},{18,16},{26,24},{19,17},{27,25},{34,32},... | collective-permute-start | bytes 196616 | tf_op jit(solution)/shard_map/ppermute | solution.py:53
  68.4 6.2 %collective-permute-start.9 = (f32[128,128]{1,0:T(8,128)S(1)}, f32[128,128]{1,0:T(8,128)S(1)}, u32[]{:S(2)}, u32[]{:S(2)}) collective-permute-start(f32[128,128]{1,0:T(8,128)S(1)} %dynamic-slice_add_fusion), channel_id=1, source_target_pairs={{14,0},{6,8},{15,1},{7,9},{30,16},{22,24},{31,17},{23,25},{46,32},... | collective-permute-start | bytes 196616 | tf_op jit(solution)/shard_map/ppermute | solution.py:53
  74.6 13.5 %collective-permute-start.13 = (bf16[128,128]{1,0:T(8,128)(2,1)S(1)}, bf16[128,128]{1,0:T(8,128)(2,1)S(1)}, u32[]{:S(2)}, u32[]{:S(2)}) collective-permute-start(bf16[128,128]{1,0:T(8,128)(2,1)S(1)} %get-tuple-element.21), channel_id=1, source_target_pairs={{24,0},{25,1},{56,32},{57,33},{88,64},{89,65},{120,96},{121,97},{1... | collective-permute-start | bytes 98312 | tf_op jit(solution)/shard_map/ppermute | solution.py:55
  75.9 12.2 %collective-permute-start.12 = (bf16[128,128]{1,0:T(8,128)(2,1)S(1)}, bf16[128,128]{1,0:T(8,128)(2,1)S(1)}, u32[]{:S(2)}, u32[]{:S(2)}) collective-permute-start(bf16[128,128]{1,0:T(8,128)(2,1)S(1)} %get-tuple-element.21), channel_id=1, source_target_pairs={{16,0},{17,1},{48,32},{49,33},{80,64},{81,65},{112,96},{113,97},{1... | collective-permute-start | bytes 98312 | tf_op jit(solution)/shard_map/ppermute | solution.py:55
  77.2 10.9 %collective-permute-start.11 = (bf16[128,128]{1,0:T(8,128)(2,1)S(1)}, bf16[128,128]{1,0:T(8,128)(2,1)S(1)}, u32[]{:S(2)}, u32[]{:S(2)}) collective-permute-start(bf16[128,128]{1,0:T(8,128)(2,1)S(1)} %get-tuple-element.21), channel_id=1, source_target_pairs={{8,0},{9,1},{40,32},{41,33},{72,64},{73,65},{104,96},{105,97},{136... | collective-permute-start | bytes 98312 | tf_op jit(solution)/shard_map/ppermute | solution.py:55
  88.1 5.9 %collective-permute-start.14 = (f32[128,128]{1,0:T(8,128)S(1)}, f32[128,128]{1,0:T(8,128)S(1)}, u32[]{:S(2)}, u32[]{:S(2)}) collective-permute-start(f32[128,128]{1,0:T(8,128)S(1)} %add_add_fusion), channel_id=1, source_target_pairs={{1,0},{3,2},{5,4},{7,6},{9,8},{11,10},{13,12},{15,14},{17,16},{19,... | collective-permute-start | bytes 196616 | tf_op jit(solution)/shard_map/ppermute | solution.py:57
  108.6 18.6 %all-to-all-start.3 = ((f32[32,8,128]{2,1,0:T(8,128)}), f32[32,8,128]{2,1,0:T(8,128)S(1)}, u32[]{:S(2)}, u32[]{:S(2)}) async-start(f32[32,8,128]{2,1,0:T(8,128)} %broadcast_in_dim.56), calls=%async_computation.3 | async-start | bytes 262144 | tf_op jit(solution)/shard_map/all_to_all | solution.py:19
  116.1 7.8 %collective-permute-start.15 = (f32[16,128]{1,0:T(8,128)S(1)}, f32[16,128]{1,0:T(8,128)S(1)}, u32[]{:S(2)}, u32[]{:S(2)}) collective-permute-start(f32[16,128]{1,0:T(8,128)S(1)} %slice_bitcast_fusion), channel_id=1, source_target_pairs={{0,16},{1,17},{2,18},{3,19},{4,20},{5,21},{6,22},{7,23},{8,24},{9,... | collective-permute-start | bytes 24584 | tf_op jit(solution)/shard_map/ppermute | solution.py:231
  171.6 9.0 %all-to-all-start.6 = ((bf16[4,256,128]{2,1,0:T(8,128)(2,1)}), bf16[4,256,128]{2,1,0:T(8,128)(2,1)S(1)}, u32[]{:S(2)}, u32[]{:S(2)}) async-start(bf16[4,256,128]{2,1,0:T(8,128)(2,1)} %reduce_sum.80), calls=%async_computation.6 | async-start | bytes 524288 | tf_op jit(solution)/shard_map/all_to_all | solution.py:19
  175.2 1.6 copy-start.2
  223.0 15.4 %all-to-all-start.9 = ((f32[32,8,128]{2,1,0:T(8,128)}), f32[32,8,128]{2,1,0:T(8,128)S(1)}, u32[]{:S(2)}, u32[]{:S(2)}) async-start(f32[32,8,128]{2,1,0:T(8,128)} %broadcast_in_dim.59), calls=%async_computation.9 | async-start | bytes 262144 | tf_op jit(solution)/shard_map/all_to_all | solution.py:19
  229.2 9.2 %collective-permute-start.16 = (f32[8,128]{1,0:T(8,128)S(1)}, f32[8,128]{1,0:T(8,128)S(1)}, u32[]{:S(2)}, u32[]{:S(2)}) collective-permute-start(f32[8,128]{1,0:T(8,128)S(1)} %reduce_sum.83), channel_id=1, source_target_pairs={{16,0},{17,1},{18,2},{19,3},{20,4},{21,5},{22,6},{23,7},{24,8},{25... | collective-permute-start | bytes 12296 | tf_op jit(solution)/shard_map/ppermute | solution.py:252
Sparse Core Ops, SparseCore 0:
  94.8 70.5 all-gather.1

commit v5 on v4

--- a/solution.py
+++ b/solution.py
@@ -51,9 +51,7 @@
 
 def to_first_column(value):
     value = value + sum(lax.ppermute(value, "y", backward(pairs)) for pairs in NEAR)
-    sent = value.astype(jnp.bfloat16)
-    far = [lax.ppermute(sent, ("zh", "y"), backward(pairs)) for pairs in FAR]
-    value = value + sum(part.astype(jnp.float32) for part in far)
+    value = value + sum(lax.ppermute(value, ("zh", "y"), backward(pairs)) for pairs in FAR)
     return jnp.concatenate([value, lax.ppermute(value, "core", [(1, 0)])], axis=0)
 
 
@@ -236,7 +234,6 @@
 
     placed = column_products(tiles, slots, place, band_block, True)
     received = total(swap(placed.reshape(4, 4, 256, 128), "x")).astype(jnp.bfloat16)
-    received, blocks = lax.optimization_barrier((received, blocks))
     received = swap(received, "zl")
     row_part = row_products(
         tiles, slots, place, blocks, correction, band_block, weight_of(factor)

time: 266 us -> 262 us (0.985)
  waiting for transfers between devices: 35.2 us -> 44.8 us
  blocking collectives: 106 us -> 97.4 us
  starting transfers between devices: 79.9 us -> 74.7 us
    all_to_all x6, blocking collectives: 106 us -> 97.4 us  [swap(): return lax.all_to_all(value, axes, 0, 0, tiled=True)]
    all_to_all x5, waiting for transfers between devices: 12.9 us -> 18.1 us  [swap(): return lax.all_to_all(value, axes, 0, 0, tiled=True)]
    all_to_all x5, starting transfers between devices: 36 us -> 31.9 us  [swap(): return lax.all_to_all(value, axes, 0, 0, tiled=True)]
    ppermute x3, waiting for transfers between devices: 9.57 us -> 12.7 us  [to_first_column(): lax.ppermute(value, ('zh', 'y'), backward(pairs))]
  transfers between devices with their start and end apart: 23 -> 23, of which waited for: 14 -> 14; matrix products, arithmetic and copies ran while one was open for 2% -> 3% of each run, Pallas kernels for 4% -> 3%
where the time goes in v5:
time: 262 us; the launch traced here: 261 us
  blocking collectives  97.4 us (37%)
  starting transfers between devices  74.7 us (29%)
  waiting for transfers between devices  44.8 us (17%)
  between operations  16.4 us (6%)
  Pallas kernels  14.1 us (5%)
  local copies, waits for them, and re-layouts  6.37 us (2%)
  other arithmetic  6.07 us (2%)
    all_to_all x6, blocking collectives, swap(): return lax.all_to_all(value, axes, 0, 0, tiled=True)  97.4 us
    all_to_all x5, starting transfers between devices, swap(): return lax.all_to_all(value, axes, 0, 0, tiled=True)  31.9 us
    all_to_all x5, waiting for transfers between devices, swap(): return lax.all_to_all(value, axes, 0, 0, tiled=True)  18.1 us
    ppermute x3, starting transfers between devices, from_first_column(): far = sum((lax.ppermute(block, ('zh', 'y'), pairs) for pairs in FAR))  14.5 us
    ppermute x3, waiting for transfers between devices, to_first_column(): lax.ppermute(value, ('zh', 'y'), backward(pairs))  12.7 us
    pallas_call x2, Pallas kernels, normalise(): pl.pallas_call(normalise_kernel, out_shape=block if own else (block, squa...  8.55 us
    ppermute x1, starting transfers between devices, local(): other = lax.ppermute(lines, 'zh', [(0, 1)])  7.04 us
  transfers between devices with their start and end apart: 23, of which 14 were waited for; matrix products, arithmetic and copies ran while one was open for 3% of the time, Pallas kernels for 3%

profile of v5, /device:TPU:1, one launch (start us, length us, event | category | flops | bytes accessed | tf_op | source)
XLA Modules:
  0.0 260.7 jit_solution(12252067739419595854)
XLA Ops:
  6.5 2.2 broadcast_in_dim.54
  8.8 10.4 %all-to-all-start.1 = ((bf16[16,256,128]{2,1,0:T(8,128)(2,1)}), bf16[16,256,128]{2,1,0:T(8,128)(2,1)S(1)}, u32[]{:S(2)}, u32[]{:S(2)}) async-start(bf16[16,256,128]{2,1,0:T(8,128)(2,1)} %broadcast_in_dim.54), calls=%async_computation.1 | async-start | bytes 2097152 | tf_op jit(solution)/shard_map/all_to_all | solution.py:19
  19.2 7.5 %collective-permute-start = (bf16[256,128]{1,0:T(8,128)(2,1)S(1)}, bf16[256,128]{1,0:T(8,128)(2,1)S(1)}, u32[]{:S(2)}, u32[]{:S(2)}) collective-permute-start(bf16[256,128]{1,0:T(8,128)(2,1)S(1)} %copy-done.3), channel_id=1, source_target_pairs={{0,8},{1,9},{32,40},{33,41},{64,72},{65,73},{96,104},{97,105},{128... | collective-permute-start | bytes 196616 | tf_op jit(solution)/shard_map/ppermute | solution.py:36
  27.9 5.8 %collective-permute-start.2 = (bf16[256,128]{1,0:T(8,128)(2,1)S(1)}, bf16[256,128]{1,0:T(8,128)(2,1)S(1)}, u32[]{:S(2)}, u32[]{:S(2)}) collective-permute-start(bf16[256,128]{1,0:T(8,128)(2,1)S(1)} %copy-done.3), channel_id=1, source_target_pairs={{0,24},{1,25},{32,56},{33,57},{64,88},{65,89},{96,120},{97,121},{1... | collective-permute-start | bytes 196616 | tf_op jit(solution)/shard_map/ppermute | solution.py:36
  33.7 3.2 %collective-permute-done.1 = bf16[256,128]{1,0:T(8,128)(2,1)S(1)} collective-permute-done((bf16[256,128]{1,0:T(8,128)(2,1)S(1)}, bf16[256,128]{1,0:T(8,128)(2,1)S(1)}, u32[]{:S(2)}, u32[]{:S(2)}) %collective-permute-start.1) | collective-permute-done | bytes 65568 | tf_op jit(solution)/shard_map/ppermute | solution.py:36
  43.5 2.8 %collective-permute-done.6 = bf16[256,128]{1,0:T(8,128)(2,1)S(1)} collective-permute-done((bf16[256,128]{1,0:T(8,128)(2,1)S(1)}, bf16[256,128]{1,0:T(8,128)(2,1)S(1)}, u32[]{:S(2)}, u32[]{:S(2)}) %collective-permute-start.6) | collective-permute-done | bytes 65568 | tf_op jit(solution)/shard_map/ppermute | solution.py:40
  48.5 7.1 %all-to-all-start = ((bf16[16,256,128]{2,1,0:T(8,128)(2,1)}), bf16[16,256,128]{2,1,0:T(8,128)(2,1)}, u32[]{:S(2)}, u32[]{:S(2)}) async-start(bf16[16,256,128]{2,1,0:T(8,128)(2,1)} %copy-done.1), calls=%async_computation | async-start | bytes 2097152 | tf_op jit(solution)/shard_map/all_to_all | solution.py:19
  61.1 2.3 collective-permute-start.7
  68.2 2.4 collective-permute-done.10
  70.7 1.8 collective-permute-done.8
  77.1 5.0 %collective-permute-done.11 = f32[128,128]{1,0:T(8,128)S(1)} collective-permute-done((f32[128,128]{1,0:T(8,128)S(1)}, f32[128,128]{1,0:T(8,128)S(1)}, u32[]{:S(2)}, u32[]{:S(2)}) %collective-permute-start.11) | collective-permute-done | bytes 65568 | tf_op jit(solution)/shard_map/ppermute | solution.py:54
  82.1 1.6 collective-permute-done.12
  83.7 6.1 %collective-permute-done.13 = f32[128,128]{1,0:T(8,128)S(1)} collective-permute-done((f32[128,128]{1,0:T(8,128)S(1)}, f32[128,128]{1,0:T(8,128)S(1)}, u32[]{:S(2)}, u32[]{:S(2)}) %collective-permute-start.13) | collective-permute-done | bytes 65568 | tf_op jit(solution)/shard_map/ppermute | solution.py:54
  89.8 4.6 %collective-permute-start.14 = (f32[128,128]{1,0:T(8,128)S(1)}, f32[128,128]{1,0:T(8,128)S(1)}, u32[]{:S(2)}, u32[]{:S(2)}) collective-permute-start(f32[128,128]{1,0:T(8,128)S(1)} %add_add_fusion), channel_id=1, source_target_pairs={{1,0},{3,2},{5,4},{7,6},{9,8},{11,10},{13,12},{15,14},{17,16},{19,... | collective-permute-start | bytes 196616 | tf_op jit(solution)/shard_map/ppermute | solution.py:55
  96.9 12.8 %all_to_all.55 = f32[16,24,128]{2,1,0:T(8,128)S(1)} all-to-all(f32[16,24,128]{2,1,0:T(8,128)S(1)} %pad_maximum_fusion), channel_id=1, replica_groups=mesh['zl'=4,'x'=4,'zh'=2,'y'=8,'core'=2] {'y','core'}, dimensions={0} | all-to-all | bytes 393216 | tf_op jit(solution)/shard_map/all_to_all | solution.py:19
  110.4 7.2 %all-to-all-start.3 = ((f32[32,8,128]{2,1,0:T(8,128)}), f32[32,8,128]{2,1,0:T(8,128)S(1)}, u32[]{:S(2)}, u32[]{:S(2)}) async-start(f32[32,8,128]{2,1,0:T(8,128)} %broadcast_in_dim.56), calls=%async_computation.3 | async-start | bytes 262144 | tf_op jit(solution)/shard_map/all_to_all | solution.py:19
  117.6 7.0 %collective-permute-start.15 = (f32[16,128]{1,0:T(8,128)S(1)}, f32[16,128]{1,0:T(8,128)S(1)}, u32[]{:S(2)}, u32[]{:S(2)}) collective-permute-start(f32[16,128]{1,0:T(8,128)S(1)} %slice_bitcast_fusion), channel_id=1, source_target_pairs={{0,16},{1,17},{2,18},{3,19},{4,20},{5,21},{6,22},{7,23},{8,24},{9,... | collective-permute-start | bytes 24584 | tf_op jit(solution)/shard_map/ppermute | solution.py:229
  125.5 3.3 %all-to-all-done.3 = f32[32,8,128]{2,1,0:T(8,128)S(1)} async-done(((f32[32,8,128]{2,1,0:T(8,128)}), f32[32,8,128]{2,1,0:T(8,128)S(1)}, u32[]{:S(2)}, u32[]{:S(2)}) %all-to-all-start.3) | async-done | bytes 131104 | tf_op jit(solution)/shard_map/all_to_all | solution.py:19
  128.8 13.8 %all_to_all.56.both_ref = f32[16,24,128]{2,1,0:T(8,128)S(1)} all-to-all(f32[16,24,128]{2,1,0:T(8,128)S(1)} %broadcast_in_dim.57), channel_id=1, replica_groups=mesh['zl'=4,'x'=4,'zh'=2,'y'=8,'core'=2] {'y','core'}, dimensions={0} | all-to-all | bytes 393216 | tf_op jit(solution)/shard_map/all_to_all | solution.py:19
  142.6 3.9 %normalise.2 = (bf16[256,128]{1,0:T(8,128)(2,1)S(1)}, f32[128,128]{1,0:T(8,128)S(1)}) custom-call(f32[16,24,128]{2,1,0:T(8,128)S(1)} %all_to_all.56.both_ref), custom_call_target="tpu_custom_call" | custom-call | tf_op jit(solution)/shard_map/normalise/pallas_call | solution.py:147
  147.7 23.2 %all_to_all.57 = bf16[4,4,256,128]{3,2,1,0:T(8,128)(2,1)} all-to-all(bf16[4,4,256,128]{3,2,1,0:T(8,128)(2,1)S(1)} %bitcast.39), channel_id=1, replica_groups=mesh['zl'=4,'x'=4,'zh'=2,'y'=8,'core'=2] {'x'}, dimensions={0} | all-to-all | bytes 2097152 | tf_op jit(solution)/shard_map/all_to_all | solution.py:19
  171.0 2.2 reduce_sum.80
  173.1 3.4 %all-to-all-start.6 = ((bf16[4,256,128]{2,1,0:T(8,128)(2,1)}), bf16[4,256,128]{2,1,0:T(8,128)(2,1)S(1)}, u32[]{:S(2)}, u32[]{:S(2)}) async-start(bf16[4,256,128]{2,1,0:T(8,128)(2,1)} %reduce_sum.80), calls=%async_computation.6 | async-start | bytes 524288 | tf_op jit(solution)/shard_map/all_to_all | solution.py:19
  176.7 7.2 %all-to-all-done.6 = bf16[4,256,128]{2,1,0:T(8,128)(2,1)S(1)} async-done(((bf16[4,256,128]{2,1,0:T(8,128)(2,1)}), bf16[4,256,128]{2,1,0:T(8,128)(2,1)S(1)}, u32[]{:S(2)}, u32[]{:S(2)}) %all-to-all-start.6) | async-done | bytes 262176 | tf_op jit(solution)/shard_map/all_to_all | solution.py:19
  184.0 1.6 copy-done.2
  185.6 2.0 row_products.3
  187.6 20.9 %all_to_all.58 = f32[32,8,128]{2,1,0:T(8,128)S(1)} all-to-all(f32[32,8,128]{2,1,0:T(8,128)S(1)} %get-tuple-element.18), channel_id=1, replica_groups=mesh['zl'=4,'x'=4,'zh'=2,'y'=8,'core'=2] {'zh','y','core'}, dimensions={0} | all-to-all | bytes 262144 | tf_op jit(solution)/shard_map/all_to_all | solution.py:19
  209.1 11.9 %all_to_all.59 = f32[16,8,128]{2,1,0:T(8,128)S(1)} all-to-all(f32[16,8,128]{2,1,0:T(8,128)S(1)} %convolution_bitcast_fusion), channel_id=1, replica_groups=mesh['zl'=4,'x'=4,'zh'=2,'y'=8,'core'=2] {'y','core'}, dimensions={0} | all-to-all | bytes 131072 | tf_op jit(solution)/shard_map/all_to_all | solution.py:19
  221.6 3.9 %all-to-all-start.9 = ((f32[32,8,128]{2,1,0:T(8,128)}), f32[32,8,128]{2,1,0:T(8,128)S(1)}, u32[]{:S(2)}, u32[]{:S(2)}) async-start(f32[32,8,128]{2,1,0:T(8,128)} %broadcast_in_dim.59), calls=%async_computation.9 | async-start | bytes 262144 | tf_op jit(solution)/shard_map/all_to_all | solution.py:19
  226.8 7.7 %all-to-all-done.9 = f32[32,8,128]{2,1,0:T(8,128)S(1)} async-done(((f32[32,8,128]{2,1,0:T(8,128)}), f32[32,8,128]{2,1,0:T(8,128)S(1)}, u32[]{:S(2)}, u32[]{:S(2)}) %all-to-all-start.9) | async-done | bytes 131104 | tf_op jit(solution)/shard_map/all_to_all | solution.py:19
  234.5 14.7 %all_to_all.60.both_ref = f32[16,24,128]{2,1,0:T(8,128)S(1)} all-to-all(f32[16,24,128]{2,1,0:T(8,128)S(1)} %broadcast_in_dim.60), channel_id=1, replica_groups=mesh['zl'=4,'x'=4,'zh'=2,'y'=8,'core'=2] {'y','core'}, dimensions={0} | all-to-all | bytes 393216 | tf_op jit(solution)/shard_map/all_to_all | solution.py:19
  249.2 4.6 %normalise.3 = f32[256,128]{1,0:T(8,128)} custom-call(f32[16,24,128]{2,1,0:T(8,128)S(1)} %all_to_all.60.both_ref, s32[1]{0:T(128)} %bitcast.15.refs_0_, f32[256,128]{1,0:T(8,128)S(1)} %get-tuple-element.17.refs_1_), custom_call_target="tpu_custom_call" | custom-call | tf_op jit(solution)/shard_map/normalise/pallas_call | solution.py:147
  (76 shorter events, 30.1 us)
Async XLA Ops:
  6.5 12.6 %copy-start.3 = (bf16[256,128]{1,0:T(8,128)(2,1)S(1)}, bf16[256,128]{1,0:T(8,128)(2,1)}, u32[]{:S(2)}) copy-start(bf16[256,128]{1,0:T(8,128)(2,1)} %band_ref) | copy-start | bytes 196612
  6.5 39.8 %copy-start.4 = (s32[1,1,1,16]{3,2,1,0:T(1,128)S(1)}, s32[1,1,1,16]{3,2,1,0:T(1,128)}, u32[]{:S(2)}) copy-start(s32[1,1,1,16]{3,2,1,0:T(1,128)} %param.4) | copy-start | bytes 196
  6.5 39.9 %copy-start = (bf16[1,1,16,256,256]{4,3,2,1,0:T(8,128)(2,1)S(1)}, bf16[1,1,16,256,256]{4,3,2,1,0:T(8,128)(2,1)}, u32[]{:S(2)}) copy-start(bf16[1,1,16,256,256]{4,3,2,1,0:T(8,128)(2,1)} %param.3) | copy-start | bytes 6291460
  8.8 39.8 %all-to-all-start.1 = ((bf16[16,256,128]{2,1,0:T(8,128)(2,1)}), bf16[16,256,128]{2,1,0:T(8,128)(2,1)S(1)}, u32[]{:S(2)}, u32[]{:S(2)}) async-start(bf16[16,256,128]{2,1,0:T(8,128)(2,1)} %broadcast_in_dim.54), calls=%async_computation.1 | async-start | bytes 2097152 | tf_op jit(solution)/shard_map/all_to_all | solution.py:19
  19.2 14.6 %collective-permute-start = (bf16[256,128]{1,0:T(8,128)(2,1)S(1)}, bf16[256,128]{1,0:T(8,128)(2,1)S(1)}, u32[]{:S(2)}, u32[]{:S(2)}) collective-permute-start(bf16[256,128]{1,0:T(8,128)(2,1)S(1)} %copy-done.3), channel_id=1, source_target_pairs={{0,8},{1,9},{32,40},{33,41},{64,72},{65,73},{96,104},{97,105},{128... | collective-permute-start | bytes 196616 | tf_op jit(solution)/shard_map/ppermute | solution.py:36
  26.6 10.3 %collective-permute-start.1 = (bf16[256,128]{1,0:T(8,128)(2,1)S(1)}, bf16[256,128]{1,0:T(8,128)(2,1)S(1)}, u32[]{:S(2)}, u32[]{:S(2)}) collective-permute-start(bf16[256,128]{1,0:T(8,128)(2,1)S(1)} %copy-done.3), channel_id=1, source_target_pairs={{0,16},{1,17},{32,48},{33,49},{64,80},{65,81},{96,112},{97,113},{1... | collective-permute-start | bytes 196616 | tf_op jit(solution)/shard_map/ppermute | solution.py:36
  27.9 9.0 %collective-permute-start.2 = (bf16[256,128]{1,0:T(8,128)(2,1)S(1)}, bf16[256,128]{1,0:T(8,128)(2,1)S(1)}, u32[]{:S(2)}, u32[]{:S(2)}) collective-permute-start(bf16[256,128]{1,0:T(8,128)(2,1)S(1)} %copy-done.3), channel_id=1, source_target_pairs={{0,24},{1,25},{32,56},{33,57},{64,88},{65,89},{96,120},{97,121},{1... | collective-permute-start | bytes 196616 | tf_op jit(solution)/shard_map/ppermute | solution.py:36
  37.0 3.9 %collective-permute-start.3 = (bf16[256,128]{1,0:T(8,128)(2,1)S(1)}, bf16[256,128]{1,0:T(8,128)(2,1)S(1)}, u32[]{:S(2)}, u32[]{:S(2)}) collective-permute-start(bf16[256,128]{1,0:T(8,128)(2,1)S(1)} %add_select_fusion.1), channel_id=1, source_target_pairs={{0,2},{8,10},{1,3},{9,11},{16,18},{24,26},{17,19},{25,27},{32,34},... | collective-permute-start | bytes 196616 | tf_op jit(solution)/shard_map/ppermute | solution.py:38
  38.3 2.6 %collective-permute-start.4 = (bf16[256,128]{1,0:T(8,128)(2,1)S(1)}, bf16[256,128]{1,0:T(8,128)(2,1)S(1)}, u32[]{:S(2)}, u32[]{:S(2)}) collective-permute-start(bf16[256,128]{1,0:T(8,128)(2,1)S(1)} %add_select_fusion.1), channel_id=1, source_target_pairs={{0,14},{8,6},{1,15},{9,7},{16,30},{24,22},{17,31},{25,23},{32,46},... | collective-permute-start | bytes 196616 | tf_op jit(solution)/shard_map/ppermute | solution.py:38
  39.6 2.6 %collective-permute-start.5 = (bf16[256,128]{1,0:T(8,128)(2,1)S(1)}, bf16[256,128]{1,0:T(8,128)(2,1)S(1)}, u32[]{:S(2)}, u32[]{:S(2)}) collective-permute-start(bf16[256,128]{1,0:T(8,128)(2,1)S(1)} %add_select_fusion.1), channel_id=1, source_target_pairs={{0,4},{8,12},{1,5},{9,13},{16,20},{24,28},{17,21},{25,29},{32,36},... | collective-permute-start | bytes 196616 | tf_op jit(solution)/shard_map/ppermute | solution.py:38
  42.2 4.1 %collective-permute-start.6 = (bf16[256,128]{1,0:T(8,128)(2,1)S(1)}, bf16[256,128]{1,0:T(8,128)(2,1)S(1)}, u32[]{:S(2)}, u32[]{:S(2)}) collective-permute-start(bf16[256,128]{1,0:T(8,128)(2,1)S(1)} %add_select_fusion), channel_id=1, source_target_pairs={{0,1},{2,3},{4,5},{6,7},{8,9},{10,11},{12,13},{14,15},{16,17},{18,... | collective-permute-start | bytes 196616 | tf_op jit(solution)/shard_map/ppermute | solution.py:40
  47.5 1.0 copy-start.1
  48.5 45.8 %all-to-all-start = ((bf16[16,256,128]{2,1,0:T(8,128)(2,1)}), bf16[16,256,128]{2,1,0:T(8,128)(2,1)}, u32[]{:S(2)}, u32[]{:S(2)}) async-start(bf16[16,256,128]{2,1,0:T(8,128)(2,1)} %copy-done.1), calls=%async_computation | async-start | bytes 2097152 | tf_op jit(solution)/shard_map/all_to_all | solution.py:19
  55.6 128.3 %all-gather.2.cloned.1.call-start = ((), (), s32[]{:S(2)}) async-start(), calls=%async_computation.11 | async-start | bytes 2228224 | tf_op jit(solution)/shard_map/all_gather | solution.py:224
  61.1 3.2 %collective-permute-start.7 = (f32[128,128]{1,0:T(8,128)S(1)}, f32[128,128]{1,0:T(8,128)S(1)}, u32[]{:S(2)}, u32[]{:S(2)}) collective-permute-start(f32[128,128]{1,0:T(8,128)S(1)} %constant_dynamic-slice_fusion), channel_id=1, source_target_pairs={{0,1},{1,0},{2,3},{3,2},{4,5},{5,4},{6,7},{7,6},{8,9},{9,8},{10,11... | collective-permute-start | bytes 196616 | tf_op jit(solution)/shard_map/ppermute | solution.py:49
  64.3 6.3 %collective-permute-start.10 = (f32[128,128]{1,0:T(8,128)S(1)}, f32[128,128]{1,0:T(8,128)S(1)}, u32[]{:S(2)}, u32[]{:S(2)}) collective-permute-start(f32[128,128]{1,0:T(8,128)S(1)} %dynamic-slice_add_fusion), channel_id=1, source_target_pairs={{4,0},{12,8},{5,1},{13,9},{20,16},{28,24},{21,17},{29,25},{36,32},... | collective-permute-start | bytes 196616 | tf_op jit(solution)/shard_map/ppermute | solution.py:53
  65.6 6.9 %collective-permute-start.8 = (f32[128,128]{1,0:T(8,128)S(1)}, f32[128,128]{1,0:T(8,128)S(1)}, u32[]{:S(2)}, u32[]{:S(2)}) collective-permute-start(f32[128,128]{1,0:T(8,128)S(1)} %dynamic-slice_add_fusion), channel_id=1, source_target_pairs={{2,0},{10,8},{3,1},{11,9},{18,16},{26,24},{19,17},{27,25},{34,32},... | collective-permute-start | bytes 196616 | tf_op jit(solution)/shard_map/ppermute | solution.py:53
  66.9 6.2 %collective-permute-start.9 = (f32[128,128]{1,0:T(8,128)S(1)}, f32[128,128]{1,0:T(8,128)S(1)}, u32[]{:S(2)}, u32[]{:S(2)}) collective-permute-start(f32[128,128]{1,0:T(8,128)S(1)} %dynamic-slice_add_fusion), channel_id=1, source_target_pairs={{14,0},{6,8},{15,1},{7,9},{30,16},{22,24},{31,17},{23,25},{46,32},... | collective-permute-start | bytes 196616 | tf_op jit(solution)/shard_map/ppermute | solution.py:53
  73.2 8.9 %collective-permute-start.11 = (f32[128,128]{1,0:T(8,128)S(1)}, f32[128,128]{1,0:T(8,128)S(1)}, u32[]{:S(2)}, u32[]{:S(2)}) collective-permute-start(f32[128,128]{1,0:T(8,128)S(1)} %add_add_fusion.1), channel_id=1, source_target_pairs={{8,0},{9,1},{40,32},{41,33},{72,64},{73,65},{104,96},{105,97},{136... | collective-permute-start | bytes 196616 | tf_op jit(solution)/shard_map/ppermute | solution.py:54
  74.5 9.2 %collective-permute-start.12 = (f32[128,128]{1,0:T(8,128)S(1)}, f32[128,128]{1,0:T(8,128)S(1)}, u32[]{:S(2)}, u32[]{:S(2)}) collective-permute-start(f32[128,128]{1,0:T(8,128)S(1)} %add_add_fusion.1), channel_id=1, source_target_pairs={{16,0},{17,1},{48,32},{49,33},{80,64},{81,65},{112,96},{113,97},{1... | collective-permute-start | bytes 196616 | tf_op jit(solution)/shard_map/ppermute | solution.py:54
  75.8 14.0 %collective-permute-start.13 = (f32[128,128]{1,0:T(8,128)S(1)}, f32[128,128]{1,0:T(8,128)S(1)}, u32[]{:S(2)}, u32[]{:S(2)}) collective-permute-start(f32[128,128]{1,0:T(8,128)S(1)} %add_add_fusion.1), channel_id=1, source_target_pairs={{24,0},{25,1},{56,32},{57,33},{88,64},{89,65},{120,96},{121,97},{1... | collective-permute-start | bytes 196616 | tf_op jit(solution)/shard_map/ppermute | solution.py:54
  89.8 6.0 %collective-permute-start.14 = (f32[128,128]{1,0:T(8,128)S(1)}, f32[128,128]{1,0:T(8,128)S(1)}, u32[]{:S(2)}, u32[]{:S(2)}) collective-permute-start(f32[128,128]{1,0:T(8,128)S(1)} %add_add_fusion), channel_id=1, source_target_pairs={{1,0},{3,2},{5,4},{7,6},{9,8},{11,10},{13,12},{15,14},{17,16},{19,... | collective-permute-start | bytes 196616 | tf_op jit(solution)/shard_map/ppermute | solution.py:55
  110.4 18.3 %all-to-all-start.3 = ((f32[32,8,128]{2,1,0:T(8,128)}), f32[32,8,128]{2,1,0:T(8,128)S(1)}, u32[]{:S(2)}, u32[]{:S(2)}) async-start(f32[32,8,128]{2,1,0:T(8,128)} %broadcast_in_dim.56), calls=%async_computation.3 | async-start | bytes 262144 | tf_op jit(solution)/shard_map/all_to_all | solution.py:19
  117.6 7.8 %collective-permute-start.15 = (f32[16,128]{1,0:T(8,128)S(1)}, f32[16,128]{1,0:T(8,128)S(1)}, u32[]{:S(2)}, u32[]{:S(2)}) collective-permute-start(f32[16,128]{1,0:T(8,128)S(1)} %slice_bitcast_fusion), channel_id=1, source_target_pairs={{0,16},{1,17},{2,18},{3,19},{4,20},{5,21},{6,22},{7,23},{8,24},{9,... | collective-permute-start | bytes 24584 | tf_op jit(solution)/shard_map/ppermute | solution.py:229
  173.1 10.8 %all-to-all-start.6 = ((bf16[4,256,128]{2,1,0:T(8,128)(2,1)}), bf16[4,256,128]{2,1,0:T(8,128)(2,1)S(1)}, u32[]{:S(2)}, u32[]{:S(2)}) async-start(bf16[4,256,128]{2,1,0:T(8,128)(2,1)} %reduce_sum.80), calls=%async_computation.6 | async-start | bytes 524288 | tf_op jit(solution)/shard_map/all_to_all | solution.py:19
  184.0 1.6 copy-start.2
  221.6 12.8 %all-to-all-start.9 = ((f32[32,8,128]{2,1,0:T(8,128)}), f32[32,8,128]{2,1,0:T(8,128)S(1)}, u32[]{:S(2)}, u32[]{:S(2)}) async-start(f32[32,8,128]{2,1,0:T(8,128)} %broadcast_in_dim.59), calls=%async_computation.9 | async-start | bytes 262144 | tf_op jit(solution)/shard_map/all_to_all | solution.py:19
  225.5 9.0 %collective-permute-start.16 = (f32[8,128]{1,0:T(8,128)S(1)}, f32[8,128]{1,0:T(8,128)S(1)}, u32[]{:S(2)}, u32[]{:S(2)}) collective-permute-start(f32[8,128]{1,0:T(8,128)S(1)} %reduce_sum.83), channel_id=1, source_target_pairs={{16,0},{17,1},{18,2},{19,3},{20,4},{21,5},{22,6},{23,7},{24,8},{25... | collective-permute-start | bytes 12296 | tf_op jit(solution)/shard_map/ppermute | solution.py:249
Sparse Core Ops, SparseCore 0:
  96.6 70.2 all-gather.1

commit v6 on v5

--- a/solution.py
+++ b/solution.py
@@ -23,8 +23,12 @@
     return jnp.broadcast_to(block[None], (count,) + block.shape)
 
 
-FAR = [[(0, 4)], [(0, 8)], [(0, 12)]]
-NEAR = [[(0, 1), (4, 5)], [(0, 7), (4, 3)], [(0, 2), (4, 6)]]
+FAR = [[(0, 4)], [(0, 10)], [(0, 14)]]
+NEAR = [
+    [(0, 1), (4, 5), (10, 11), (14, 15)],
+    [(0, 7), (4, 3), (10, 9), (14, 13)],
+    [(0, 2), (4, 6), (10, 12), (14, 8)],
+]
 
 
 def backward(pairs):
@@ -35,8 +39,8 @@
     zh, y, core = (lax.axis_index(axis) for axis in COL)
     far = sum(lax.ppermute(block, ("zh", "y"), pairs) for pairs in FAR)
     block = jnp.where((zh == 0) & (y == 0), block, far)
-    near = sum(lax.ppermute(block, "y", pairs) for pairs in NEAR)
-    block = jnp.where(y % 4 == 0, block, near)
+    near = sum(lax.ppermute(block, ("zh", "y"), pairs) for pairs in NEAR)
+    block = jnp.where(y % 4 == 2 * zh, block, near)
     other = lax.ppermute(block, "core", [(0, 1)])
     return jnp.where(core == 0, block, other)
 
@@ -50,8 +54,12 @@
 
 
 def to_first_column(value):
-    value = value + sum(lax.ppermute(value, "y", backward(pairs)) for pairs in NEAR)
-    value = value + sum(lax.ppermute(value, ("zh", "y"), backward(pairs)) for pairs in FAR)
+    value = value + sum(lax.ppermute(value, ("zh", "y"), backward(pairs)) for pairs in NEAR)
+    sent = value.astype(jnp.bfloat16)
+    far = lax.ppermute(value, ("zh", "y"), backward(FAR[0]))
+    for pairs in FAR[1:]:
+        far = far + lax.ppermute(sent, ("zh", "y"), backward(pairs)).astype(jnp.float32)
+    value = value + far
     return jnp.concatenate([value, lax.ppermute(value, "core", [(1, 0)])], axis=0)
 
 

time: 262 us -> 257 us (0.981)
  waiting for transfers between devices: 44.8 us -> 41.1 us
    ppermute x3, waiting for transfers between devices: 12.7 us -> 4.92 us  [to_first_column(): lax.ppermute(value, ('zh', 'y'), backward(pairs))]
    ppermute x6, waiting for transfers between devices: 6.2 us -> 11.9 us  [the longest x2 10.6 us: to_first_column(): lax.ppermute(sent, ('zh', 'y'), backward(pairs)).astype(jnp.float32)]
  transfers between devices with their start and end apart: 23 -> 23, of which waited for: 14 -> 13; matrix products, arithmetic and copies ran while one was open for 3% -> 3% of each run, Pallas kernels for 3% -> 3%
where the time goes in v6:
time: 257 us; the launch traced here: 256 us
  blocking collectives  97.6 us (38%)
  starting transfers between devices  73.3 us (29%)
  waiting for transfers between devices  41.1 us (16%)
  between operations  16.4 us (6%)
  Pallas kernels  14.1 us (5%)
  local copies, waits for them, and re-layouts  6.35 us (2%)
  other arithmetic  6.04 us (2%)
    all_to_all x6, blocking collectives, swap(): return lax.all_to_all(value, axes, 0, 0, tiled=True)  97.6 us
    all_to_all x5, starting transfers between devices, swap(): return lax.all_to_all(value, axes, 0, 0, tiled=True)  32.3 us
    all_to_all x5, waiting for transfers between devices, swap(): return lax.all_to_all(value, axes, 0, 0, tiled=True)  18.3 us
    ppermute x3, starting transfers between devices, from_first_column(): far = sum((lax.ppermute(block, ('zh', 'y'), pairs) for pairs in FAR))  13 us
    ppermute x2, waiting for transfers between devices, to_first_column(): lax.ppermute(sent, ('zh', 'y'), backward(pairs)).astype(jnp.float32)  10.6 us
    pallas_call x2, Pallas kernels, normalise(): pl.pallas_call(normalise_kernel, out_shape=block if own else (block, squa...  8.55 us
    ppermute x1, starting transfers between devices, local(): other = lax.ppermute(lines, 'zh', [(0, 1)])  7.04 us
  transfers between devices with their start and end apart: 23, of which 13 were waited for; matrix products, arithmetic and copies ran while one was open for 3% of the time, Pallas kernels for 3%

profile of v6, /device:TPU:1, one launch (start us, length us, event | category | flops | bytes accessed | tf_op | source)
XLA Modules:
  0.0 255.9 jit_solution(11979080748519874226)
XLA Ops:
  6.5 2.2 broadcast_in_dim.54
  8.8 10.4 %all-to-all-start.1 = ((bf16[16,256,128]{2,1,0:T(8,128)(2,1)}), bf16[16,256,128]{2,1,0:T(8,128)(2,1)S(1)}, u32[]{:S(2)}, u32[]{:S(2)}) async-start(bf16[16,256,128]{2,1,0:T(8,128)(2,1)} %broadcast_in_dim.54), calls=%async_computation.1 | async-start | bytes 2097152 | tf_op jit(solution)/shard_map/all_to_all | solution.py:19
  19.2 7.5 %collective-permute-start = (bf16[256,128]{1,0:T(8,128)(2,1)S(1)}, bf16[256,128]{1,0:T(8,128)(2,1)S(1)}, u32[]{:S(2)}, u32[]{:S(2)}) collective-permute-start(bf16[256,128]{1,0:T(8,128)(2,1)S(1)} %copy-done.3), channel_id=1, source_target_pairs={{0,8},{1,9},{32,40},{33,41},{64,72},{65,73},{96,104},{97,105},{128... | collective-permute-start | bytes 196616 | tf_op jit(solution)/shard_map/ppermute | solution.py:40
  26.6 3.2 %collective-permute-start.1 = (bf16[256,128]{1,0:T(8,128)(2,1)S(1)}, bf16[256,128]{1,0:T(8,128)(2,1)S(1)}, u32[]{:S(2)}, u32[]{:S(2)}) collective-permute-start(bf16[256,128]{1,0:T(8,128)(2,1)S(1)} %copy-done.3), channel_id=1, source_target_pairs={{0,20},{1,21},{32,52},{33,53},{64,84},{65,85},{96,116},{97,117},{1... | collective-permute-start | bytes 196616 | tf_op jit(solution)/shard_map/ppermute | solution.py:40
  29.8 2.3 collective-permute-start.2
  40.0 3.1 %collective-permute-done.6 = bf16[256,128]{1,0:T(8,128)(2,1)S(1)} collective-permute-done((bf16[256,128]{1,0:T(8,128)(2,1)S(1)}, bf16[256,128]{1,0:T(8,128)(2,1)S(1)}, u32[]{:S(2)}, u32[]{:S(2)}) %collective-permute-start.6) | collective-permute-done | bytes 65568 | tf_op jit(solution)/shard_map/ppermute | solution.py:44
  45.3 7.3 %all-to-all-start = ((bf16[16,256,128]{2,1,0:T(8,128)(2,1)}), bf16[16,256,128]{2,1,0:T(8,128)(2,1)}, u32[]{:S(2)}, u32[]{:S(2)}) async-start(bf16[16,256,128]{2,1,0:T(8,128)(2,1)} %copy-done.1), calls=%async_computation | async-start | bytes 2097152 | tf_op jit(solution)/shard_map/all_to_all | solution.py:19
  58.0 2.3 collective-permute-start.7
  65.2 2.4 collective-permute-done.10
  67.6 1.9 collective-permute-done.8
  74.0 7.9 %collective-permute-done.12 = bf16[128,128]{1,0:T(8,128)(2,1)S(1)} collective-permute-done((bf16[128,128]{1,0:T(8,128)(2,1)S(1)}, bf16[128,128]{1,0:T(8,128)(2,1)S(1)}, u32[]{:S(2)}, u32[]{:S(2)}) %collective-permute-start.12) | collective-permute-done | bytes 32800 | tf_op jit(solution)/shard_map/ppermute | solution.py:61
  81.9 2.7 %collective-permute-done.13 = bf16[128,128]{1,0:T(8,128)(2,1)S(1)} collective-permute-done((bf16[128,128]{1,0:T(8,128)(2,1)S(1)}, bf16[128,128]{1,0:T(8,128)(2,1)S(1)}, u32[]{:S(2)}, u32[]{:S(2)}) %collective-permute-start.13) | collective-permute-done | bytes 32800 | tf_op jit(solution)/shard_map/ppermute | solution.py:61
  84.6 4.4 %collective-permute-start.14 = (f32[128,128]{1,0:T(8,128)S(1)}, f32[128,128]{1,0:T(8,128)S(1)}, u32[]{:S(2)}, u32[]{:S(2)}) collective-permute-start(f32[128,128]{1,0:T(8,128)S(1)} %add_add_fusion), channel_id=1, source_target_pairs={{1,0},{3,2},{5,4},{7,6},{9,8},{11,10},{13,12},{15,14},{17,16},{19,... | collective-permute-start | bytes 196616 | tf_op jit(solution)/shard_map/ppermute | solution.py:63
  89.0 1.4 convert_reduce_fusion
  91.6 12.8 %all_to_all.55 = f32[16,24,128]{2,1,0:T(8,128)S(1)} all-to-all(f32[16,24,128]{2,1,0:T(8,128)S(1)} %pad_maximum_fusion), channel_id=1, replica_groups=mesh['zl'=4,'x'=4,'zh'=2,'y'=8,'core'=2] {'y','core'}, dimensions={0} | all-to-all | bytes 393216 | tf_op jit(solution)/shard_map/all_to_all | solution.py:19
  105.1 7.4 %all-to-all-start.3 = ((f32[32,8,128]{2,1,0:T(8,128)}), f32[32,8,128]{2,1,0:T(8,128)S(1)}, u32[]{:S(2)}, u32[]{:S(2)}) async-start(f32[32,8,128]{2,1,0:T(8,128)} %broadcast_in_dim.56), calls=%async_computation.3 | async-start | bytes 262144 | tf_op jit(solution)/shard_map/all_to_all | solution.py:19
  112.5 7.0 %collective-permute-start.15 = (f32[16,128]{1,0:T(8,128)S(1)}, f32[16,128]{1,0:T(8,128)S(1)}, u32[]{:S(2)}, u32[]{:S(2)}) collective-permute-start(f32[16,128]{1,0:T(8,128)S(1)} %slice_bitcast_fusion), channel_id=1, source_target_pairs={{0,16},{1,17},{2,18},{3,19},{4,20},{5,21},{6,22},{7,23},{8,24},{9,... | collective-permute-start | bytes 24584 | tf_op jit(solution)/shard_map/ppermute | solution.py:237
  120.3 3.3 %all-to-all-done.3 = f32[32,8,128]{2,1,0:T(8,128)S(1)} async-done(((f32[32,8,128]{2,1,0:T(8,128)}), f32[32,8,128]{2,1,0:T(8,128)S(1)}, u32[]{:S(2)}, u32[]{:S(2)}) %all-to-all-start.3) | async-done | bytes 131104 | tf_op jit(solution)/shard_map/all_to_all | solution.py:19
  123.7 13.8 %all_to_all.56.both_ref = f32[16,24,128]{2,1,0:T(8,128)S(1)} all-to-all(f32[16,24,128]{2,1,0:T(8,128)S(1)} %broadcast_in_dim.57), channel_id=1, replica_groups=mesh['zl'=4,'x'=4,'zh'=2,'y'=8,'core'=2] {'y','core'}, dimensions={0} | all-to-all | bytes 393216 | tf_op jit(solution)/shard_map/all_to_all | solution.py:19
  137.5 3.9 %normalise.2 = (bf16[256,128]{1,0:T(8,128)(2,1)S(1)}, f32[128,128]{1,0:T(8,128)S(1)}) custom-call(f32[16,24,128]{2,1,0:T(8,128)S(1)} %all_to_all.56.both_ref), custom_call_target="tpu_custom_call" | custom-call | tf_op jit(solution)/shard_map/normalise/pallas_call | solution.py:155
  142.6 23.3 %all_to_all.57 = bf16[4,4,256,128]{3,2,1,0:T(8,128)(2,1)} all-to-all(bf16[4,4,256,128]{3,2,1,0:T(8,128)(2,1)S(1)} %bitcast.39), channel_id=1, replica_groups=mesh['zl'=4,'x'=4,'zh'=2,'y'=8,'core'=2] {'x'}, dimensions={0} | all-to-all | bytes 2097152 | tf_op jit(solution)/shard_map/all_to_all | solution.py:19
  165.9 2.1 reduce_sum.80
  168.0 3.4 %all-to-all-start.6 = ((bf16[4,256,128]{2,1,0:T(8,128)(2,1)}), bf16[4,256,128]{2,1,0:T(8,128)(2,1)S(1)}, u32[]{:S(2)}, u32[]{:S(2)}) async-start(bf16[4,256,128]{2,1,0:T(8,128)(2,1)} %reduce_sum.80), calls=%async_computation.6 | async-start | bytes 524288 | tf_op jit(solution)/shard_map/all_to_all | solution.py:19
  171.6 7.2 %all-to-all-done.6 = bf16[4,256,128]{2,1,0:T(8,128)(2,1)S(1)} async-done(((bf16[4,256,128]{2,1,0:T(8,128)(2,1)}), bf16[4,256,128]{2,1,0:T(8,128)(2,1)S(1)}, u32[]{:S(2)}, u32[]{:S(2)}) %all-to-all-start.6) | async-done | bytes 262176 | tf_op jit(solution)/shard_map/all_to_all | solution.py:19
  178.8 1.6 copy-done.2
  180.4 2.0 row_products.3
  182.5 21.2 %all_to_all.58 = f32[32,8,128]{2,1,0:T(8,128)S(1)} all-to-all(f32[32,8,128]{2,1,0:T(8,128)S(1)} %get-tuple-element.20), channel_id=1, replica_groups=mesh['zl'=4,'x'=4,'zh'=2,'y'=8,'core'=2] {'zh','y','core'}, dimensions={0} | all-to-all | bytes 262144 | tf_op jit(solution)/shard_map/all_to_all | solution.py:19
  204.2 11.9 %all_to_all.59 = f32[16,8,128]{2,1,0:T(8,128)S(1)} all-to-all(f32[16,8,128]{2,1,0:T(8,128)S(1)} %convolution_bitcast_fusion), channel_id=1, replica_groups=mesh['zl'=4,'x'=4,'zh'=2,'y'=8,'core'=2] {'y','core'}, dimensions={0} | all-to-all | bytes 131072 | tf_op jit(solution)/shard_map/all_to_all | solution.py:19
  216.8 3.9 %all-to-all-start.9 = ((f32[32,8,128]{2,1,0:T(8,128)}), f32[32,8,128]{2,1,0:T(8,128)S(1)}, u32[]{:S(2)}, u32[]{:S(2)}) async-start(f32[32,8,128]{2,1,0:T(8,128)} %broadcast_in_dim.59), calls=%async_computation.9 | async-start | bytes 262144 | tf_op jit(solution)/shard_map/all_to_all | solution.py:19
  222.0 7.8 %all-to-all-done.9 = f32[32,8,128]{2,1,0:T(8,128)S(1)} async-done(((f32[32,8,128]{2,1,0:T(8,128)}), f32[32,8,128]{2,1,0:T(8,128)S(1)}, u32[]{:S(2)}, u32[]{:S(2)}) %all-to-all-start.9) | async-done | bytes 131104 | tf_op jit(solution)/shard_map/all_to_all | solution.py:19
  229.8 14.6 %all_to_all.60.both_ref = f32[16,24,128]{2,1,0:T(8,128)S(1)} all-to-all(f32[16,24,128]{2,1,0:T(8,128)S(1)} %broadcast_in_dim.60), channel_id=1, replica_groups=mesh['zl'=4,'x'=4,'zh'=2,'y'=8,'core'=2] {'y','core'}, dimensions={0} | all-to-all | bytes 393216 | tf_op jit(solution)/shard_map/all_to_all | solution.py:19
  244.4 4.6 %normalise.3 = f32[256,128]{1,0:T(8,128)} custom-call(f32[16,24,128]{2,1,0:T(8,128)S(1)} %all_to_all.60.both_ref, s32[1]{0:T(128)} %bitcast.15.refs_0_, f32[256,128]{1,0:T(8,128)S(1)} %get-tuple-element.19.refs_1_), custom_call_target="tpu_custom_call" | custom-call | tf_op jit(solution)/shard_map/normalise/pallas_call | solution.py:155
  (76 shorter events, 28.7 us)
Async XLA Ops:
  6.5 12.6 %copy-start.3 = (bf16[256,128]{1,0:T(8,128)(2,1)S(1)}, bf16[256,128]{1,0:T(8,128)(2,1)}, u32[]{:S(2)}) copy-start(bf16[256,128]{1,0:T(8,128)(2,1)} %band_ref) | copy-start | bytes 196612
  6.5 36.6 %copy-start.4 = (s32[1,1,1,16]{3,2,1,0:T(1,128)S(1)}, s32[1,1,1,16]{3,2,1,0:T(1,128)}, u32[]{:S(2)}) copy-start(s32[1,1,1,16]{3,2,1,0:T(1,128)} %param.4) | copy-start | bytes 196
  6.5 36.6 %copy-start = (bf16[1,1,16,256,256]{4,3,2,1,0:T(8,128)(2,1)S(1)}, bf16[1,1,16,256,256]{4,3,2,1,0:T(8,128)(2,1)}, u32[]{:S(2)}) copy-start(bf16[1,1,16,256,256]{4,3,2,1,0:T(8,128)(2,1)} %param.3) | copy-start | bytes 6291460
  8.8 36.5 %all-to-all-start.1 = ((bf16[16,256,128]{2,1,0:T(8,128)(2,1)}), bf16[16,256,128]{2,1,0:T(8,128)(2,1)S(1)}, u32[]{:S(2)}, u32[]{:S(2)}) async-start(bf16[16,256,128]{2,1,0:T(8,128)(2,1)} %broadcast_in_dim.54), calls=%async_computation.1 | async-start | bytes 2097152 | tf_op jit(solution)/shard_map/all_to_all | solution.py:19
  19.2 13.0 %collective-permute-start = (bf16[256,128]{1,0:T(8,128)(2,1)S(1)}, bf16[256,128]{1,0:T(8,128)(2,1)S(1)}, u32[]{:S(2)}, u32[]{:S(2)}) collective-permute-start(bf16[256,128]{1,0:T(8,128)(2,1)S(1)} %copy-done.3), channel_id=1, source_target_pairs={{0,8},{1,9},{32,40},{33,41},{64,72},{65,73},{96,104},{97,105},{128... | collective-permute-start | bytes 196616 | tf_op jit(solution)/shard_map/ppermute | solution.py:40
  26.6 5.5 %collective-permute-start.1 = (bf16[256,128]{1,0:T(8,128)(2,1)S(1)}, bf16[256,128]{1,0:T(8,128)(2,1)S(1)}, u32[]{:S(2)}, u32[]{:S(2)}) collective-permute-start(bf16[256,128]{1,0:T(8,128)(2,1)S(1)} %copy-done.3), channel_id=1, source_target_pairs={{0,20},{1,21},{32,52},{33,53},{64,84},{65,85},{96,116},{97,117},{1... | collective-permute-start | bytes 196616 | tf_op jit(solution)/shard_map/ppermute | solution.py:40
  29.8 3.6 %collective-permute-start.2 = (bf16[256,128]{1,0:T(8,128)(2,1)S(1)}, bf16[256,128]{1,0:T(8,128)(2,1)S(1)}, u32[]{:S(2)}, u32[]{:S(2)}) collective-permute-start(bf16[256,128]{1,0:T(8,128)(2,1)S(1)} %copy-done.3), channel_id=1, source_target_pairs={{0,28},{1,29},{32,60},{33,61},{64,92},{65,93},{96,124},{97,125},{1... | collective-permute-start | bytes 196616 | tf_op jit(solution)/shard_map/ppermute | solution.py:40
  33.5 3.9 %collective-permute-start.3 = (bf16[256,128]{1,0:T(8,128)(2,1)S(1)}, bf16[256,128]{1,0:T(8,128)(2,1)S(1)}, u32[]{:S(2)}, u32[]{:S(2)}) collective-permute-start(bf16[256,128]{1,0:T(8,128)(2,1)S(1)} %add_select_fusion.1), channel_id=1, source_target_pairs={{0,2},{8,10},{20,22},{28,30},{1,3},{9,11},{21,23},{29,31},{32,34},... | collective-permute-start | bytes 196616 | tf_op jit(solution)/shard_map/ppermute | solution.py:42
  34.8 2.6 %collective-permute-start.4 = (bf16[256,128]{1,0:T(8,128)(2,1)S(1)}, bf16[256,128]{1,0:T(8,128)(2,1)S(1)}, u32[]{:S(2)}, u32[]{:S(2)}) collective-permute-start(bf16[256,128]{1,0:T(8,128)(2,1)S(1)} %add_select_fusion.1), channel_id=1, source_target_pairs={{0,14},{8,6},{20,18},{28,26},{1,15},{9,7},{21,19},{29,27},{32,46},... | collective-permute-start | bytes 196616 | tf_op jit(solution)/shard_map/ppermute | solution.py:42
  36.1 2.6 %collective-permute-start.5 = (bf16[256,128]{1,0:T(8,128)(2,1)S(1)}, bf16[256,128]{1,0:T(8,128)(2,1)S(1)}, u32[]{:S(2)}, u32[]{:S(2)}) collective-permute-start(bf16[256,128]{1,0:T(8,128)(2,1)S(1)} %add_select_fusion.1), channel_id=1, source_target_pairs={{0,4},{8,12},{20,24},{28,16},{1,5},{9,13},{21,25},{29,17},{32,36},... | collective-permute-start | bytes 196616 | tf_op jit(solution)/shard_map/ppermute | solution.py:42
  38.7 4.4 %collective-permute-start.6 = (bf16[256,128]{1,0:T(8,128)(2,1)S(1)}, bf16[256,128]{1,0:T(8,128)(2,1)S(1)}, u32[]{:S(2)}, u32[]{:S(2)}) collective-permute-start(bf16[256,128]{1,0:T(8,128)(2,1)S(1)} %add_select_fusion), channel_id=1, source_target_pairs={{0,1},{2,3},{4,5},{6,7},{8,9},{10,11},{12,13},{14,15},{16,17},{18,... | collective-permute-start | bytes 196616 | tf_op jit(solution)/shard_map/ppermute | solution.py:44
  44.3 1.0 copy-start.1
  45.3 43.8 %all-to-all-start = ((bf16[16,256,128]{2,1,0:T(8,128)(2,1)}), bf16[16,256,128]{2,1,0:T(8,128)(2,1)}, u32[]{:S(2)}, u32[]{:S(2)}) async-start(bf16[16,256,128]{2,1,0:T(8,128)(2,1)} %copy-done.1), calls=%async_computation | async-start | bytes 2097152 | tf_op jit(solution)/shard_map/all_to_all | solution.py:19
  52.5 126.3 %all-gather.2.cloned.1.call-start = ((), (), s32[]{:S(2)}) async-start(), calls=%async_computation.11 | async-start | bytes 2228224 | tf_op jit(solution)/shard_map/all_gather | solution.py:232
  58.0 3.2 %collective-permute-start.7 = (f32[128,128]{1,0:T(8,128)S(1)}, f32[128,128]{1,0:T(8,128)S(1)}, u32[]{:S(2)}, u32[]{:S(2)}) collective-permute-start(f32[128,128]{1,0:T(8,128)S(1)} %constant_dynamic-slice_fusion), channel_id=1, source_target_pairs={{0,1},{1,0},{2,3},{3,2},{4,5},{5,4},{6,7},{7,6},{8,9},{9,8},{10,11... | collective-permute-start | bytes 196616 | tf_op jit(solution)/shard_map/ppermute | solution.py:53
  61.3 6.3 %collective-permute-start.10 = (f32[128,128]{1,0:T(8,128)S(1)}, f32[128,128]{1,0:T(8,128)S(1)}, u32[]{:S(2)}, u32[]{:S(2)}) collective-permute-start(f32[128,128]{1,0:T(8,128)S(1)} %dynamic-slice_add_fusion), channel_id=1, source_target_pairs={{4,0},{12,8},{24,20},{16,28},{5,1},{13,9},{25,21},{17,29},{36,32},... | collective-permute-start | bytes 196616 | tf_op jit(solution)/shard_map/ppermute | solution.py:57
  62.6 6.9 %collective-permute-start.8 = (f32[128,128]{1,0:T(8,128)S(1)}, f32[128,128]{1,0:T(8,128)S(1)}, u32[]{:S(2)}, u32[]{:S(2)}) collective-permute-start(f32[128,128]{1,0:T(8,128)S(1)} %dynamic-slice_add_fusion), channel_id=1, source_target_pairs={{2,0},{10,8},{22,20},{30,28},{3,1},{11,9},{23,21},{31,29},{34,32},... | collective-permute-start | bytes 196616 | tf_op jit(solution)/shard_map/ppermute | solution.py:57
  63.9 6.2 %collective-permute-start.9 = (f32[128,128]{1,0:T(8,128)S(1)}, f32[128,128]{1,0:T(8,128)S(1)}, u32[]{:S(2)}, u32[]{:S(2)}) collective-permute-start(f32[128,128]{1,0:T(8,128)S(1)} %dynamic-slice_add_fusion), channel_id=1, source_target_pairs={{14,0},{6,8},{18,20},{26,28},{15,1},{7,9},{19,21},{27,29},{46,32},... | collective-permute-start | bytes 196616 | tf_op jit(solution)/shard_map/ppermute | solution.py:57
  70.1 14.5 %collective-permute-start.11 = (f32[128,128]{1,0:T(8,128)S(1)}, f32[128,128]{1,0:T(8,128)S(1)}, u32[]{:S(2)}, u32[]{:S(2)}) collective-permute-start(f32[128,128]{1,0:T(8,128)S(1)} %get-tuple-element.18), channel_id=1, source_target_pairs={{8,0},{9,1},{40,32},{41,33},{72,64},{73,65},{104,96},{105,97},{136... | collective-permute-start | bytes 196616 | tf_op jit(solution)/shard_map/ppermute | solution.py:59
  71.4 10.5 %collective-permute-start.12 = (bf16[128,128]{1,0:T(8,128)(2,1)S(1)}, bf16[128,128]{1,0:T(8,128)(2,1)S(1)}, u32[]{:S(2)}, u32[]{:S(2)}) collective-permute-start(bf16[128,128]{1,0:T(8,128)(2,1)S(1)} %get-tuple-element.17), channel_id=1, source_target_pairs={{20,0},{21,1},{52,32},{53,33},{84,64},{85,65},{116,96},{117,97},{1... | collective-permute-start | bytes 98312 | tf_op jit(solution)/shard_map/ppermute | solution.py:61
  72.7 11.9 %collective-permute-start.13 = (bf16[128,128]{1,0:T(8,128)(2,1)S(1)}, bf16[128,128]{1,0:T(8,128)(2,1)S(1)}, u32[]{:S(2)}, u32[]{:S(2)}) collective-permute-start(bf16[128,128]{1,0:T(8,128)(2,1)S(1)} %get-tuple-element.17), channel_id=1, source_target_pairs={{28,0},{29,1},{60,32},{61,33},{92,64},{93,65},{124,96},{125,97},{1... | collective-permute-start | bytes 98312 | tf_op jit(solution)/shard_map/ppermute | solution.py:61
  84.6 5.8 %collective-permute-start.14 = (f32[128,128]{1,0:T(8,128)S(1)}, f32[128,128]{1,0:T(8,128)S(1)}, u32[]{:S(2)}, u32[]{:S(2)}) collective-permute-start(f32[128,128]{1,0:T(8,128)S(1)} %add_add_fusion), channel_id=1, source_target_pairs={{1,0},{3,2},{5,4},{7,6},{9,8},{11,10},{13,12},{15,14},{17,16},{19,... | collective-permute-start | bytes 196616 | tf_op jit(solution)/shard_map/ppermute | solution.py:63
  105.1 18.5 %all-to-all-start.3 = ((f32[32,8,128]{2,1,0:T(8,128)}), f32[32,8,128]{2,1,0:T(8,128)S(1)}, u32[]{:S(2)}, u32[]{:S(2)}) async-start(f32[32,8,128]{2,1,0:T(8,128)} %broadcast_in_dim.56), calls=%async_computation.3 | async-start | bytes 262144 | tf_op jit(solution)/shard_map/all_to_all | solution.py:19
  112.5 7.8 %collective-permute-start.15 = (f32[16,128]{1,0:T(8,128)S(1)}, f32[16,128]{1,0:T(8,128)S(1)}, u32[]{:S(2)}, u32[]{:S(2)}) collective-permute-start(f32[16,128]{1,0:T(8,128)S(1)} %slice_bitcast_fusion), channel_id=1, source_target_pairs={{0,16},{1,17},{2,18},{3,19},{4,20},{5,21},{6,22},{7,23},{8,24},{9,... | collective-permute-start | bytes 24584 | tf_op jit(solution)/shard_map/ppermute | solution.py:237
  168.0 10.8 %all-to-all-start.6 = ((bf16[4,256,128]{2,1,0:T(8,128)(2,1)}), bf16[4,256,128]{2,1,0:T(8,128)(2,1)S(1)}, u32[]{:S(2)}, u32[]{:S(2)}) async-start(bf16[4,256,128]{2,1,0:T(8,128)(2,1)} %reduce_sum.80), calls=%async_computation.6 | async-start | bytes 524288 | tf_op jit(solution)/shard_map/all_to_all | solution.py:19
  178.8 1.6 copy-start.2
  216.8 12.9 %all-to-all-start.9 = ((f32[32,8,128]{2,1,0:T(8,128)}), f32[32,8,128]{2,1,0:T(8,128)S(1)}, u32[]{:S(2)}, u32[]{:S(2)}) async-start(f32[32,8,128]{2,1,0:T(8,128)} %broadcast_in_dim.59), calls=%async_computation.9 | async-start | bytes 262144 | tf_op jit(solution)/shard_map/all_to_all | solution.py:19
  220.7 9.1 %collective-permute-start.16 = (f32[8,128]{1,0:T(8,128)S(1)}, f32[8,128]{1,0:T(8,128)S(1)}, u32[]{:S(2)}, u32[]{:S(2)}) collective-permute-start(f32[8,128]{1,0:T(8,128)S(1)} %reduce_sum.83), channel_id=1, source_target_pairs={{16,0},{17,1},{18,2},{19,3},{20,4},{21,5},{22,6},{23,7},{24,8},{25... | collective-permute-start | bytes 12296 | tf_op jit(solution)/shard_map/ppermute | solution.py:257
Sparse Core Ops, SparseCore 0:
  91.3 70.5 all-gather.1

commit v7 on v6

--- a/solution.py
+++ b/solution.py
@@ -206,6 +206,11 @@
     return jnp.block([[high, low], [high, jnp.zeros_like(high)]])
 
 
+def total_of_four(received):
+    first, second, third, fourth = (received[i].astype(jnp.float32) for i in range(4))
+    return (first + second) + (third + fourth)
+
+
 def total(received):
     return jnp.sum(received.astype(jnp.float32), axis=0)
 
@@ -241,12 +246,12 @@
     band_block, factor = normalise(both)
 
     placed = column_products(tiles, slots, place, band_block, True)
-    received = total(swap(placed.reshape(4, 4, 256, 128), "x")).astype(jnp.bfloat16)
+    received = total_of_four(swap(placed.reshape(4, 4, 256, 128), "x")).astype(jnp.bfloat16)
     received = swap(received, "zl")
     row_part = row_products(
         tiles, slots, place, blocks, correction, band_block, weight_of(factor)
     )
-    col_sum = total(received)
+    col_sum = total_of_four(received)
     row_part = row_part + jnp.where(first_col, col_sum, 0.0)
     rest = jnp.where(first_col, 0.0, col_sum)
     band_rows = total(swap(row_part.reshape(32, 8, 128), COL))

time: 257 us -> 255 us (level)
  blocking collectives: 97.6 us -> 75.9 us
  starting transfers between devices: 73.3 us -> 86.9 us
  waiting for transfers between devices: 41.1 us -> 48.2 us
    all_to_all x6 -> x5, blocking collectives: 97.6 us -> 75.9 us  [swap(): return lax.all_to_all(value, axes, 0, 0, tiled=True)]
    all_to_all x5 -> x6, starting transfers between devices: 32.3 us -> 44.4 us  [swap(): return lax.all_to_all(value, axes, 0, 0, tiled=True)]
    all_to_all x5 -> x6, waiting for transfers between devices: 18.3 us -> 27.6 us  [swap(): return lax.all_to_all(value, axes, 0, 0, tiled=True)]
  transfers between devices with their start and end apart: 23 -> 24, of which waited for: 13 -> 13; matrix products, arithmetic and copies ran while one was open for 3% -> 2% of each run, Pallas kernels for 3% -> 4%
where the time goes in v7:
time: 255 us; the launch traced here: 254 us
  starting transfers between devices  86.9 us (34%)
  blocking collectives  75.9 us (30%)
  waiting for transfers between devices  48.2 us (19%)
  between operations  16.5 us (6%)
  Pallas kernels  14.1 us (6%)
  local copies, waits for them, and re-layouts  6.34 us (2%)
  other arithmetic  5.47 us (2%)
    all_to_all x5, blocking collectives, swap(): return lax.all_to_all(value, axes, 0, 0, tiled=True)  75.9 us
    all_to_all x6, starting transfers between devices, swap(): return lax.all_to_all(value, axes, 0, 0, tiled=True)  44.4 us
    all_to_all x6, waiting for transfers between devices, swap(): return lax.all_to_all(value, axes, 0, 0, tiled=True)  27.6 us
    ppermute x3, starting transfers between devices, from_first_column(): far = sum((lax.ppermute(block, ('zh', 'y'), pairs) for pairs in FAR))  14.2 us
    ppermute x2, waiting for transfers between devices, to_first_column(): lax.ppermute(sent, ('zh', 'y'), backward(pairs)).astype(jnp.float32)  9.5 us
    pallas_call x2, Pallas kernels, normalise(): pl.pallas_call(normalise_kernel, out_shape=block if own else (block, squa...  8.55 us
    ppermute x1, starting transfers between devices, local(): other = lax.ppermute(lines, 'zh', [(0, 1)])  7.04 us
  transfers between devices with their start and end apart: 24, of which 13 were waited for; matrix products, arithmetic and copies ran while one was open for 2% of the time, Pallas kernels for 4%

profile of v7, /device:TPU:1, one launch (start us, length us, event | category | flops | bytes accessed | tf_op | source)
XLA Modules:
  0.0 254.2 jit_solution(9481887967577641502)
XLA Ops:
  6.5 2.2 broadcast_in_dim.54
  8.8 10.4 %all-to-all-start.1 = ((bf16[16,256,128]{2,1,0:T(8,128)(2,1)}), bf16[16,256,128]{2,1,0:T(8,128)(2,1)S(1)}, u32[]{:S(2)}, u32[]{:S(2)}) async-start(bf16[16,256,128]{2,1,0:T(8,128)(2,1)} %broadcast_in_dim.54), calls=%async_computation.1 | async-start | bytes 2097152 | tf_op jit(solution)/shard_map/all_to_all | solution.py:19
  19.2 11.6 %collective-permute-start.2 = (bf16[256,128]{1,0:T(8,128)(2,1)S(1)}, bf16[256,128]{1,0:T(8,128)(2,1)S(1)}, u32[]{:S(2)}, u32[]{:S(2)}) collective-permute-start(bf16[256,128]{1,0:T(8,128)(2,1)S(1)} %copy-done.3), channel_id=1, source_target_pairs={{0,28},{1,29},{32,60},{33,61},{64,92},{65,93},{96,124},{97,125},{1... | collective-permute-start | bytes 196616 | tf_op jit(solution)/shard_map/ppermute | solution.py:40
  30.8 1.3 collective-permute-start.1
  32.1 1.3 collective-permute-start
  33.4 1.7 collective-permute-done
  35.2 1.3 collective-permute-start.5
  41.7 2.6 %collective-permute-done.6 = bf16[256,128]{1,0:T(8,128)(2,1)S(1)} collective-permute-done((bf16[256,128]{1,0:T(8,128)(2,1)S(1)}, bf16[256,128]{1,0:T(8,128)(2,1)S(1)}, u32[]{:S(2)}, u32[]{:S(2)}) %collective-permute-start.6) | collective-permute-done | bytes 65568 | tf_op jit(solution)/shard_map/ppermute | solution.py:44
  46.5 7.3 %all-to-all-start = ((bf16[16,256,128]{2,1,0:T(8,128)(2,1)}), bf16[16,256,128]{2,1,0:T(8,128)(2,1)}, u32[]{:S(2)}, u32[]{:S(2)}) async-start(bf16[16,256,128]{2,1,0:T(8,128)(2,1)} %copy-done.1), calls=%async_computation | async-start | bytes 2097152 | tf_op jit(solution)/shard_map/all_to_all | solution.py:19
  59.4 2.3 collective-permute-start.7
  66.5 2.4 collective-permute-done.10
  74.2 9.4 %collective-permute-done.13 = bf16[128,128]{1,0:T(8,128)(2,1)S(1)} collective-permute-done((bf16[128,128]{1,0:T(8,128)(2,1)S(1)}, bf16[128,128]{1,0:T(8,128)(2,1)S(1)}, u32[]{:S(2)}, u32[]{:S(2)}) %collective-permute-start.13) | collective-permute-done | bytes 32800 | tf_op jit(solution)/shard_map/ppermute | solution.py:61
  83.7 4.6 %collective-permute-start.14 = (f32[128,128]{1,0:T(8,128)S(1)}, f32[128,128]{1,0:T(8,128)S(1)}, u32[]{:S(2)}, u32[]{:S(2)}) collective-permute-start(f32[128,128]{1,0:T(8,128)S(1)} %add_add_fusion.1), channel_id=1, source_target_pairs={{1,0},{3,2},{5,4},{7,6},{9,8},{11,10},{13,12},{15,14},{17,16},{19,... | collective-permute-start | bytes 196616 | tf_op jit(solution)/shard_map/ppermute | solution.py:63
  88.3 1.4 convert_reduce_fusion
  90.8 12.8 %all_to_all.55 = f32[16,24,128]{2,1,0:T(8,128)S(1)} all-to-all(f32[16,24,128]{2,1,0:T(8,128)S(1)} %pad_maximum_fusion), channel_id=1, replica_groups=mesh['zl'=4,'x'=4,'zh'=2,'y'=8,'core'=2] {'y','core'}, dimensions={0} | all-to-all | bytes 393216 | tf_op jit(solution)/shard_map/all_to_all | solution.py:19
  104.3 7.2 %all-to-all-start.3 = ((f32[32,8,128]{2,1,0:T(8,128)}), f32[32,8,128]{2,1,0:T(8,128)S(1)}, u32[]{:S(2)}, u32[]{:S(2)}) async-start(f32[32,8,128]{2,1,0:T(8,128)} %broadcast_in_dim.57), calls=%async_computation.3 | async-start | bytes 262144 | tf_op jit(solution)/shard_map/all_to_all | solution.py:19
  111.6 7.0 %collective-permute-start.15 = (f32[16,128]{1,0:T(8,128)S(1)}, f32[16,128]{1,0:T(8,128)S(1)}, u32[]{:S(2)}, u32[]{:S(2)}) collective-permute-start(f32[16,128]{1,0:T(8,128)S(1)} %slice_bitcast_fusion), channel_id=1, source_target_pairs={{0,16},{1,17},{2,18},{3,19},{4,20},{5,21},{6,22},{7,23},{8,24},{9,... | collective-permute-start | bytes 24584 | tf_op jit(solution)/shard_map/ppermute | solution.py:242
  119.4 3.3 %all-to-all-done.3 = f32[32,8,128]{2,1,0:T(8,128)S(1)} async-done(((f32[32,8,128]{2,1,0:T(8,128)}), f32[32,8,128]{2,1,0:T(8,128)S(1)}, u32[]{:S(2)}, u32[]{:S(2)}) %all-to-all-start.3) | async-done | bytes 131104 | tf_op jit(solution)/shard_map/all_to_all | solution.py:19
  122.8 13.8 %all_to_all.56.both_ref = f32[16,24,128]{2,1,0:T(8,128)S(1)} all-to-all(f32[16,24,128]{2,1,0:T(8,128)S(1)} %broadcast_in_dim.58), channel_id=1, replica_groups=mesh['zl'=4,'x'=4,'zh'=2,'y'=8,'core'=2] {'y','core'}, dimensions={0} | all-to-all | bytes 393216 | tf_op jit(solution)/shard_map/all_to_all | solution.py:19
  136.6 3.9 %normalise.2 = (bf16[256,128]{1,0:T(8,128)(2,1)S(1)}, f32[128,128]{1,0:T(8,128)S(1)}) custom-call(f32[16,24,128]{2,1,0:T(8,128)S(1)} %all_to_all.56.both_ref), custom_call_target="tpu_custom_call" | custom-call | tf_op jit(solution)/shard_map/normalise/pallas_call | solution.py:155
  141.7 22.8 %all_to_all.57 = bf16[4,4,256,128]{3,2,1,0:T(8,128)(2,1)S(1)} all-to-all(bf16[4,4,256,128]{3,2,1,0:T(8,128)(2,1)S(1)} %bitcast.47), channel_id=1, replica_groups=mesh['zl'=4,'x'=4,'zh'=2,'y'=8,'core'=2] {'x'}, dimensions={0} | all-to-all | bytes 2097152 | tf_op jit(solution)/shard_map/all_to_all | solution.py:19
  165.3 3.4 %all-to-all-start.6 = ((bf16[4,256,128]{2,1,0:T(8,128)(2,1)}), bf16[4,256,128]{2,1,0:T(8,128)(2,1)S(1)}, u32[]{:S(2)}, u32[]{:S(2)}) async-start(bf16[4,256,128]{2,1,0:T(8,128)(2,1)} %fusion), calls=%async_computation.6 | async-start | bytes 524288 | tf_op jit(solution)/shard_map/all_to_all | solution.py:19
  168.9 1.6 copy-done.2
  170.5 2.0 row_products.3
  172.5 3.6 %all-to-all-done.6 = bf16[4,256,128]{2,1,0:T(8,128)(2,1)S(1)} async-done(((bf16[4,256,128]{2,1,0:T(8,128)(2,1)}), bf16[4,256,128]{2,1,0:T(8,128)(2,1)S(1)}, u32[]{:S(2)}, u32[]{:S(2)}) %all-to-all-start.6) | async-done | bytes 262176 | tf_op jit(solution)/shard_map/all_to_all | solution.py:19
  176.8 10.2 %all-to-all-start.7 = ((f32[32,8,128]{2,1,0:T(8,128)}), f32[32,8,128]{2,1,0:T(8,128)S(1)}, u32[]{:S(2)}, u32[]{:S(2)}) async-start(f32[32,8,128]{2,1,0:T(8,128)} %fusion.13), calls=%async_computation.7 | async-start | bytes 262144 | tf_op jit(solution)/shard_map/all_to_all | solution.py:19
  187.1 12.9 %all-to-all-done.7 = f32[32,8,128]{2,1,0:T(8,128)S(1)} async-done(((f32[32,8,128]{2,1,0:T(8,128)}), f32[32,8,128]{2,1,0:T(8,128)S(1)}, u32[]{:S(2)}, u32[]{:S(2)}) %all-to-all-start.7) | async-done | bytes 131104 | tf_op jit(solution)/shard_map/all_to_all | solution.py:19
  200.5 11.9 %all_to_all.58 = f32[16,8,128]{2,1,0:T(8,128)S(1)} all-to-all(f32[16,8,128]{2,1,0:T(8,128)S(1)} %convolution_bitcast_fusion), channel_id=1, replica_groups=mesh['zl'=4,'x'=4,'zh'=2,'y'=8,'core'=2] {'y','core'}, dimensions={0} | all-to-all | bytes 131072 | tf_op jit(solution)/shard_map/all_to_all | solution.py:19
  213.1 5.9 %all-to-all-start.9 = ((f32[32,8,128]{2,1,0:T(8,128)}), f32[32,8,128]{2,1,0:T(8,128)S(1)}, u32[]{:S(2)}, u32[]{:S(2)}) async-start(f32[32,8,128]{2,1,0:T(8,128)} %broadcast_in_dim.59), calls=%async_computation.9 | async-start | bytes 262144 | tf_op jit(solution)/shard_map/all_to_all | solution.py:19
  220.3 7.8 %all-to-all-done.9 = f32[32,8,128]{2,1,0:T(8,128)S(1)} async-done(((f32[32,8,128]{2,1,0:T(8,128)}), f32[32,8,128]{2,1,0:T(8,128)S(1)}, u32[]{:S(2)}, u32[]{:S(2)}) %all-to-all-start.9) | async-done | bytes 131104 | tf_op jit(solution)/shard_map/all_to_all | solution.py:19
  228.2 14.6 %all_to_all.59.both_ref = f32[16,24,128]{2,1,0:T(8,128)S(1)} all-to-all(f32[16,24,128]{2,1,0:T(8,128)S(1)} %broadcast_in_dim.60), channel_id=1, replica_groups=mesh['zl'=4,'x'=4,'zh'=2,'y'=8,'core'=2] {'y','core'}, dimensions={0} | all-to-all | bytes 393216 | tf_op jit(solution)/shard_map/all_to_all | solution.py:19
  242.8 4.6 %normalise.3 = f32[256,128]{1,0:T(8,128)} custom-call(f32[16,24,128]{2,1,0:T(8,128)S(1)} %all_to_all.59.both_ref, s32[1]{0:T(128)} %bitcast.18.refs_0_, f32[256,128]{1,0:T(8,128)S(1)} %select_bitcast_fusion.refs_1_), custom_call_target="tpu_custom_call" | custom-call | tf_op jit(solution)/shard_map/normalise/pallas_call | solution.py:155
  (77 shorter events, 28.4 us)
Async XLA Ops:
  6.5 12.6 %copy-start.3 = (bf16[256,128]{1,0:T(8,128)(2,1)S(1)}, bf16[256,128]{1,0:T(8,128)(2,1)}, u32[]{:S(2)}) copy-start(bf16[256,128]{1,0:T(8,128)(2,1)} %band_ref) | copy-start | bytes 196612
  6.5 37.8 %copy-start.4 = (s32[1,1,1,16]{3,2,1,0:T(1,128)S(1)}, s32[1,1,1,16]{3,2,1,0:T(1,128)}, u32[]{:S(2)}) copy-start(s32[1,1,1,16]{3,2,1,0:T(1,128)} %param.4) | copy-start | bytes 196
  6.5 37.9 %copy-start = (bf16[1,1,16,256,256]{4,3,2,1,0:T(8,128)(2,1)S(1)}, bf16[1,1,16,256,256]{4,3,2,1,0:T(8,128)(2,1)}, u32[]{:S(2)}) copy-start(bf16[1,1,16,256,256]{4,3,2,1,0:T(8,128)(2,1)} %param.3) | copy-start | bytes 6291460
  8.8 37.7 %all-to-all-start.1 = ((bf16[16,256,128]{2,1,0:T(8,128)(2,1)}), bf16[16,256,128]{2,1,0:T(8,128)(2,1)S(1)}, u32[]{:S(2)}, u32[]{:S(2)}) async-start(bf16[16,256,128]{2,1,0:T(8,128)(2,1)} %broadcast_in_dim.54), calls=%async_computation.1 | async-start | bytes 2097152 | tf_op jit(solution)/shard_map/all_to_all | solution.py:19
  19.2 14.3 %collective-permute-start.2 = (bf16[256,128]{1,0:T(8,128)(2,1)S(1)}, bf16[256,128]{1,0:T(8,128)(2,1)S(1)}, u32[]{:S(2)}, u32[]{:S(2)}) collective-permute-start(bf16[256,128]{1,0:T(8,128)(2,1)S(1)} %copy-done.3), channel_id=1, source_target_pairs={{0,28},{1,29},{32,60},{33,61},{64,92},{65,93},{96,124},{97,125},{1... | collective-permute-start | bytes 196616 | tf_op jit(solution)/shard_map/ppermute | solution.py:40
  30.8 2.6 %collective-permute-start.1 = (bf16[256,128]{1,0:T(8,128)(2,1)S(1)}, bf16[256,128]{1,0:T(8,128)(2,1)S(1)}, u32[]{:S(2)}, u32[]{:S(2)}) collective-permute-start(bf16[256,128]{1,0:T(8,128)(2,1)S(1)} %copy-done.3), channel_id=1, source_target_pairs={{0,20},{1,21},{32,52},{33,53},{64,84},{65,85},{96,116},{97,117},{1... | collective-permute-start | bytes 196616 | tf_op jit(solution)/shard_map/ppermute | solution.py:40
  32.1 3.1 %collective-permute-start = (bf16[256,128]{1,0:T(8,128)(2,1)S(1)}, bf16[256,128]{1,0:T(8,128)(2,1)S(1)}, u32[]{:S(2)}, u32[]{:S(2)}) collective-permute-start(bf16[256,128]{1,0:T(8,128)(2,1)S(1)} %copy-done.3), channel_id=1, source_target_pairs={{0,8},{1,9},{32,40},{33,41},{64,72},{65,73},{96,104},{97,105},{128... | collective-permute-start | bytes 196616 | tf_op jit(solution)/shard_map/ppermute | solution.py:40
  35.2 3.9 %collective-permute-start.5 = (bf16[256,128]{1,0:T(8,128)(2,1)S(1)}, bf16[256,128]{1,0:T(8,128)(2,1)S(1)}, u32[]{:S(2)}, u32[]{:S(2)}) collective-permute-start(bf16[256,128]{1,0:T(8,128)(2,1)S(1)} %add_select_fusion.1), channel_id=1, source_target_pairs={{0,4},{8,12},{20,24},{28,16},{1,5},{9,13},{21,25},{29,17},{32,36},... | collective-permute-start | bytes 196616 | tf_op jit(solution)/shard_map/ppermute | solution.py:42
  36.5 2.6 %collective-permute-start.4 = (bf16[256,128]{1,0:T(8,128)(2,1)S(1)}, bf16[256,128]{1,0:T(8,128)(2,1)S(1)}, u32[]{:S(2)}, u32[]{:S(2)}) collective-permute-start(bf16[256,128]{1,0:T(8,128)(2,1)S(1)} %add_select_fusion.1), channel_id=1, source_target_pairs={{0,14},{8,6},{20,18},{28,26},{1,15},{9,7},{21,19},{29,27},{32,46},... | collective-permute-start | bytes 196616 | tf_op jit(solution)/shard_map/ppermute | solution.py:42
  37.8 2.6 %collective-permute-start.3 = (bf16[256,128]{1,0:T(8,128)(2,1)S(1)}, bf16[256,128]{1,0:T(8,128)(2,1)S(1)}, u32[]{:S(2)}, u32[]{:S(2)}) collective-permute-start(bf16[256,128]{1,0:T(8,128)(2,1)S(1)} %add_select_fusion.1), channel_id=1, source_target_pairs={{0,2},{8,10},{20,22},{28,30},{1,3},{9,11},{21,23},{29,31},{32,34},... | collective-permute-start | bytes 196616 | tf_op jit(solution)/shard_map/ppermute | solution.py:42
  40.4 3.9 %collective-permute-start.6 = (bf16[256,128]{1,0:T(8,128)(2,1)S(1)}, bf16[256,128]{1,0:T(8,128)(2,1)S(1)}, u32[]{:S(2)}, u32[]{:S(2)}) collective-permute-start(bf16[256,128]{1,0:T(8,128)(2,1)S(1)} %add_select_fusion), channel_id=1, source_target_pairs={{0,1},{2,3},{4,5},{6,7},{8,9},{10,11},{12,13},{14,15},{16,17},{18,... | collective-permute-start | bytes 196616 | tf_op jit(solution)/shard_map/ppermute | solution.py:44
  45.5 1.0 copy-start.1
  46.5 41.8 %all-to-all-start = ((bf16[16,256,128]{2,1,0:T(8,128)(2,1)}), bf16[16,256,128]{2,1,0:T(8,128)(2,1)}, u32[]{:S(2)}, u32[]{:S(2)}) async-start(bf16[16,256,128]{2,1,0:T(8,128)(2,1)} %copy-done.1), calls=%async_computation | async-start | bytes 2097152 | tf_op jit(solution)/shard_map/all_to_all | solution.py:19
  53.8 115.1 %all-gather.2.cloned.1.call-start = ((), (), s32[]{:S(2)}) async-start(), calls=%async_computation.11 | async-start | bytes 2228224 | tf_op jit(solution)/shard_map/all_gather | solution.py:237
  59.4 3.2 %collective-permute-start.7 = (f32[128,128]{1,0:T(8,128)S(1)}, f32[128,128]{1,0:T(8,128)S(1)}, u32[]{:S(2)}, u32[]{:S(2)}) collective-permute-start(f32[128,128]{1,0:T(8,128)S(1)} %constant_dynamic-slice_fusion), channel_id=1, source_target_pairs={{0,1},{1,0},{2,3},{3,2},{4,5},{5,4},{6,7},{7,6},{8,9},{9,8},{10,11... | collective-permute-start | bytes 196616 | tf_op jit(solution)/shard_map/ppermute | solution.py:53
  62.6 6.3 %collective-permute-start.10 = (f32[128,128]{1,0:T(8,128)S(1)}, f32[128,128]{1,0:T(8,128)S(1)}, u32[]{:S(2)}, u32[]{:S(2)}) collective-permute-start(f32[128,128]{1,0:T(8,128)S(1)} %dynamic-slice_add_fusion), channel_id=1, source_target_pairs={{4,0},{12,8},{24,20},{16,28},{5,1},{13,9},{25,21},{17,29},{36,32},... | collective-permute-start | bytes 196616 | tf_op jit(solution)/shard_map/ppermute | solution.py:57
  63.9 6.3 %collective-permute-start.9 = (f32[128,128]{1,0:T(8,128)S(1)}, f32[128,128]{1,0:T(8,128)S(1)}, u32[]{:S(2)}, u32[]{:S(2)}) collective-permute-start(f32[128,128]{1,0:T(8,128)S(1)} %dynamic-slice_add_fusion), channel_id=1, source_target_pairs={{14,0},{6,8},{18,20},{26,28},{15,1},{7,9},{19,21},{27,29},{46,32},... | collective-permute-start | bytes 196616 | tf_op jit(solution)/shard_map/ppermute | solution.py:57
  65.2 5.0 %collective-permute-start.8 = (f32[128,128]{1,0:T(8,128)S(1)}, f32[128,128]{1,0:T(8,128)S(1)}, u32[]{:S(2)}, u32[]{:S(2)}) collective-permute-start(f32[128,128]{1,0:T(8,128)S(1)} %dynamic-slice_add_fusion), channel_id=1, source_target_pairs={{2,0},{10,8},{22,20},{30,28},{3,1},{11,9},{23,21},{31,29},{34,32},... | collective-permute-start | bytes 196616 | tf_op jit(solution)/shard_map/ppermute | solution.py:57
  70.3 13.4 %collective-permute-start.11 = (f32[128,128]{1,0:T(8,128)S(1)}, f32[128,128]{1,0:T(8,128)S(1)}, u32[]{:S(2)}, u32[]{:S(2)}) collective-permute-start(f32[128,128]{1,0:T(8,128)S(1)} %get-tuple-element.18), channel_id=1, source_target_pairs={{8,0},{9,1},{40,32},{41,33},{72,64},{73,65},{104,96},{105,97},{136... | collective-permute-start | bytes 196616 | tf_op jit(solution)/shard_map/ppermute | solution.py:59
  71.6 12.0 %collective-permute-start.13 = (bf16[128,128]{1,0:T(8,128)(2,1)S(1)}, bf16[128,128]{1,0:T(8,128)(2,1)S(1)}, u32[]{:S(2)}, u32[]{:S(2)}) collective-permute-start(bf16[128,128]{1,0:T(8,128)(2,1)S(1)} %get-tuple-element.17), channel_id=1, source_target_pairs={{28,0},{29,1},{60,32},{61,33},{92,64},{93,65},{124,96},{125,97},{1... | collective-permute-start | bytes 98312 | tf_op jit(solution)/shard_map/ppermute | solution.py:61
  72.9 10.8 %collective-permute-start.12 = (bf16[128,128]{1,0:T(8,128)(2,1)S(1)}, bf16[128,128]{1,0:T(8,128)(2,1)S(1)}, u32[]{:S(2)}, u32[]{:S(2)}) collective-permute-start(bf16[128,128]{1,0:T(8,128)(2,1)S(1)} %get-tuple-element.17), channel_id=1, source_target_pairs={{20,0},{21,1},{52,32},{53,33},{84,64},{85,65},{116,96},{117,97},{1... | collective-permute-start | bytes 98312 | tf_op jit(solution)/shard_map/ppermute | solution.py:61
  83.7 6.0 %collective-permute-start.14 = (f32[128,128]{1,0:T(8,128)S(1)}, f32[128,128]{1,0:T(8,128)S(1)}, u32[]{:S(2)}, u32[]{:S(2)}) collective-permute-start(f32[128,128]{1,0:T(8,128)S(1)} %add_add_fusion.1), channel_id=1, source_target_pairs={{1,0},{3,2},{5,4},{7,6},{9,8},{11,10},{13,12},{15,14},{17,16},{19,... | collective-permute-start | bytes 196616 | tf_op jit(solution)/shard_map/ppermute | solution.py:63
  104.3 18.4 %all-to-all-start.3 = ((f32[32,8,128]{2,1,0:T(8,128)}), f32[32,8,128]{2,1,0:T(8,128)S(1)}, u32[]{:S(2)}, u32[]{:S(2)}) async-start(f32[32,8,128]{2,1,0:T(8,128)} %broadcast_in_dim.57), calls=%async_computation.3 | async-start | bytes 262144 | tf_op jit(solution)/shard_map/all_to_all | solution.py:19
  111.6 7.8 %collective-permute-start.15 = (f32[16,128]{1,0:T(8,128)S(1)}, f32[16,128]{1,0:T(8,128)S(1)}, u32[]{:S(2)}, u32[]{:S(2)}) collective-permute-start(f32[16,128]{1,0:T(8,128)S(1)} %slice_bitcast_fusion), channel_id=1, source_target_pairs={{0,16},{1,17},{2,18},{3,19},{4,20},{5,21},{6,22},{7,23},{8,24},{9,... | collective-permute-start | bytes 24584 | tf_op jit(solution)/shard_map/ppermute | solution.py:242
  165.3 10.8 %all-to-all-start.6 = ((bf16[4,256,128]{2,1,0:T(8,128)(2,1)}), bf16[4,256,128]{2,1,0:T(8,128)(2,1)S(1)}, u32[]{:S(2)}, u32[]{:S(2)}) async-start(bf16[4,256,128]{2,1,0:T(8,128)(2,1)} %fusion), calls=%async_computation.6 | async-start | bytes 524288 | tf_op jit(solution)/shard_map/all_to_all | solution.py:19
  168.9 1.6 copy-start.2
  176.8 23.2 %all-to-all-start.7 = ((f32[32,8,128]{2,1,0:T(8,128)}), f32[32,8,128]{2,1,0:T(8,128)S(1)}, u32[]{:S(2)}, u32[]{:S(2)}) async-start(f32[32,8,128]{2,1,0:T(8,128)} %fusion.13), calls=%async_computation.7 | async-start | bytes 262144 | tf_op jit(solution)/shard_map/all_to_all | solution.py:19
  213.1 15.0 %all-to-all-start.9 = ((f32[32,8,128]{2,1,0:T(8,128)}), f32[32,8,128]{2,1,0:T(8,128)S(1)}, u32[]{:S(2)}, u32[]{:S(2)}) async-start(f32[32,8,128]{2,1,0:T(8,128)} %broadcast_in_dim.59), calls=%async_computation.9 | async-start | bytes 262144 | tf_op jit(solution)/shard_map/all_to_all | solution.py:19
  219.0 9.2 %collective-permute-start.16 = (f32[8,128]{1,0:T(8,128)S(1)}, f32[8,128]{1,0:T(8,128)S(1)}, u32[]{:S(2)}, u32[]{:S(2)}) collective-permute-start(f32[8,128]{1,0:T(8,128)S(1)} %reduce_sum.60), channel_id=1, source_target_pairs={{16,0},{17,1},{18,2},{19,3},{20,4},{21,5},{22,6},{23,7},{24,8},{25... | collective-permute-start | bytes 12296 | tf_op jit(solution)/shard_map/ppermute | solution.py:262
Sparse Core Ops, SparseCore 0:
  90.5 70.2 all-gather.1
